TPU v7x, 32 devices: a whole 2x2x4 slice. The times are simulated.
32 devices in a mesh: dp: 8 (over z, x), expert: 4 (over y, core).
Axes of the slice: x: 2, y: 2, z: 4, core: 2. Of those that a mesh axis runs over, the one named last changes fastest.
Arguments:
- out_grad: bfloat16 [512, 3072], P('expert'), may hold values from -1.1953125 to 1.1953125
- routes: int32 [512, 4], P('expert'), may hold values from 0 to 7, all different within a row; in each aligned block of 128 rows (0 to 127, 128 to 255, ...) at most 80 rows name the same one
- gate_values: float32 [512, 4], P('expert'), may hold values from 0.1 to 0.5
- layer_input: bfloat16 [512, 3072], P('expert'), may hold values from -6 to 6
- w_gate: bfloat16 [8, 3072, 8192], P('expert', None, 'dp'), may hold values from -0.109375 to 0.109375
- w_up: bfloat16 [8, 3072, 8192], P('expert', None, 'dp'), may hold values from -0.109375 to 0.109375
- w_down: bfloat16 [8, 3072, 8192], P('expert', None, 'dp'), may hold values from -0.109375 to 0.109375
Outputs:
- input_grad: bfloat16 [512, 3072], P('expert')
- grad_gate: float32 [8, 3072, 8192], P('expert', None, 'dp')
- grad_up: float32 [8, 3072, 8192], P('expert', None, 'dp')
Inputs may be any that keep to these rules, and one draw needn't show every extreme that they name: In every aligned block of 128 tokens (the tokens of one index of expert) no expert is named by more than 80 routes, a bound that some block reaches; the 4 experts of a token differ.
All inputs are finite; a program needn't handle non-finite values.
Results may differ from a plain program's by a relative error of at most 0.024.
Values may be sent and summed in bfloat16 or wider, within the bound.
No kernel may reach another device: no remote copies, remote signals or barrier semaphores. Data moves between devices by JAX's collectives and lax.ppermute only.
A program may use at most 192 MiB of HBM per device.

v0:
```python
import functools

import jax
import jax.numpy as jnp
from jax import lax
from jax.experimental import pallas as pl
from jax.experimental.pallas import tpu as pltpu
from jax.sharding import PartitionSpec as P

EXPERTS = 8
MOST = 80
UNIT_TILE = 512
FEATURE_TILE = 256
VMEM_BYTES = 52 * 1024 * 1024
BF16 = jnp.bfloat16
F32 = jnp.float32
NN = (((1,), (0,)), ((), ()))
NT = (((1,), (1,)), ((), ()))
TN = (((0,), (0,)), ((), ()))


def dot(a, b, dims=NN):
    return lax.dot_general(a, b, dims, preferred_element_type=F32)


def params(count):
    return pltpu.CompilerParams(
        dimension_semantics=("arbitrary",) * count, vmem_limit_bytes=VMEM_BYTES
    )


def whole(shape):
    return pl.BlockSpec(
        shape, lambda *_: (0,) * len(shape), pipeline_mode=pl.Buffered(buffer_count=1)
    )


def one_hot(slot_row):
    slots = lax.broadcasted_iota(jnp.int32, (MOST, slot_row.shape[1]), 0)
    return slots == slot_row.astype(jnp.int32)


def pick(chosen, pieces, block, tokens, columns):
    first, total, at = block * tokens, None, 0
    for piece in pieces:
        low, high = max(first, at), min(first + tokens, at + piece.shape[0])
        if low < high:
            term = dot(chosen[:, low - first : high - first], piece[low - at : high - at, columns])
            total = term if total is None else total + term
        at += piece.shape[0]
    return total


def column_chunks(features):
    step = 768 if features % 768 == 0 else features
    return [slice(c, c + step) for c in range(0, features, step)]


def forward_kernel(count, *refs):
    pieces, (slot, w_gate, w_up, rows, act, slope) = refs[:count], refs[count:]
    blocks, tokens = slot.shape[1:]

    @pl.when(pl.program_id(1) == 0)
    def _():
        for b in range(blocks):
            chosen = one_hot(slot[0, b : b + 1, :]).astype(BF16)
            for cols in column_chunks(rows.shape[2]):
                rows[0, b * MOST : (b + 1) * MOST, cols] = pick(
                    chosen, pieces, b, tokens, cols
                ).astype(BF16)

    x = rows[0]
    gate = dot(x, w_gate[0])
    up = dot(x, w_up[0])
    sig = jax.nn.sigmoid(gate)
    act[0] = gate * sig
    slope[0] = up * sig * (1.0 + gate * (1.0 - sig))


def forward(pieces, slot, w_gate, w_up):
    experts, blocks, tokens = slot.shape
    _, features, units = w_gate.shape
    tile = min(UNIT_TILE, units)
    slots = blocks * MOST
    weight = pl.BlockSpec((1, features, tile), lambda l, f: (l, 0, f))
    unit = pl.BlockSpec((1, slots, tile), lambda l, f: (l, 0, f))
    return pl.pallas_call(
        functools.partial(forward_kernel, len(pieces)),
        grid=(experts, units // tile),
        in_specs=[whole(p.shape) for p in pieces]
        + [pl.BlockSpec((1, blocks, tokens), lambda l, f: (l, 0, 0)), weight, weight],
        out_specs=[pl.BlockSpec((1, slots, features), lambda l, f: (l, 0, 0)), unit, unit],
        out_shape=[
            jax.ShapeDtypeStruct((experts, slots, features), BF16),
            jax.ShapeDtypeStruct((experts, slots, units), F32),
            jax.ShapeDtypeStruct((experts, slots, units), F32),
        ],
        compiler_params=params(2),
        cost_estimate=pl.CostEstimate(
            flops=4 * experts * slots * features * units,
            bytes_accessed=4 * experts * features * units,
            transcendentals=experts * slots * units,
        ),
    )(*pieces, slot, w_gate, w_up)


def hidden_kernel(count, *refs):
    pieces, (slot, weight, act, slope, w_down, gate_grad, up_grad, grads) = (
        refs[:count],
        refs[count:],
    )
    blocks, tokens = slot.shape[1:]

    @pl.when(pl.program_id(1) == 0)
    def _():
        for b in range(blocks):
            mask = one_hot(slot[0, b : b + 1, :])
            scale = jnp.sum(
                jnp.where(mask, weight[0, b : b + 1, :], 0.0), axis=1, keepdims=True
            )
            chosen = mask.astype(BF16)
            for cols in column_chunks(grads.shape[1]):
                taken = pick(chosen, pieces, b, tokens, cols)
                grads[b * MOST : (b + 1) * MOST, cols] = (taken * scale).astype(BF16)

    hidden = dot(grads[...], w_down[0])
    up_grad[0] = (hidden * act[0]).astype(BF16)
    gate_grad[0] = (hidden * slope[0]).astype(BF16)


def hidden_grads(pieces, slot, weight, act, slope, w_down):
    experts, blocks, tokens = slot.shape
    _, features, units = w_down.shape
    tile = min(UNIT_TILE, units)
    slots = blocks * MOST
    unit = pl.BlockSpec((1, slots, tile), lambda l, f: (l, 0, f))
    table = pl.BlockSpec((1, blocks, tokens), lambda l, f: (l, 0, 0))
    return pl.pallas_call(
        functools.partial(hidden_kernel, len(pieces)),
        grid=(experts, units // tile),
        in_specs=[whole(p.shape) for p in pieces]
        + [table, table, unit, unit]
        + [pl.BlockSpec((1, features, tile), lambda l, f: (l, 0, f))],
        out_specs=[unit, unit],
        out_shape=[jax.ShapeDtypeStruct((experts, slots, units), BF16)] * 2,
        scratch_shapes=[pltpu.VMEM((slots, features), BF16)],
        compiler_params=params(2),
        cost_estimate=pl.CostEstimate(
            flops=2 * experts * slots * features * units,
            bytes_accessed=2 * experts * features * units,
            transcendentals=0,
        ),
    )(*pieces, slot, weight, act, slope, w_down)


def inputs_kernel(groups, slot, gate_grad, up_grad, w_gate, w_up, *sums):
    experts, _, tokens = slot.shape
    partial = [
        (dot(gate_grad[l], w_gate[l], NT) + dot(up_grad[l], w_up[l], NT)).astype(BF16)
        for l in range(experts)
    ]
    for out, members in zip(sums, groups):
        for place, b in enumerate(members):
            total = None
            for l in range(experts):
                chosen = one_hot(slot[l, b : b + 1, :]).astype(BF16)
                term = dot(chosen, partial[l][b * MOST : (b + 1) * MOST], TN)
                total = term if total is None else total + term
            out[place * tokens : (place + 1) * tokens] = total.astype(BF16)


def input_sums(slot, gate_grad, up_grad, w_gate, w_up, groups, part, parts):
    experts, blocks, tokens = slot.shape
    _, features, units = w_gate.shape
    wide = FEATURE_TILE
    steps = features // parts // wide
    slots = blocks * MOST
    across = pl.BlockSpec((experts, wide, units), lambda i: (0, part * steps + i, 0))
    return pl.pallas_call(
        functools.partial(inputs_kernel, groups),
        grid=(steps,),
        in_specs=[whole(slot.shape), whole(gate_grad.shape), whole(up_grad.shape), across, across],
        out_specs=[pl.BlockSpec((len(g) * tokens, wide), lambda i: (0, i)) for g in groups],
        out_shape=[
            jax.ShapeDtypeStruct((len(g) * tokens, features // parts), BF16) for g in groups
        ],
        compiler_params=params(1),
        cost_estimate=pl.CostEstimate(
            flops=4 * experts * slots * features * units // parts,
            bytes_accessed=4 * experts * features * units // parts,
            transcendentals=0,
        ),
    )(slot, gate_grad, up_grad, w_gate, w_up)


def weights_kernel(rows, gate_grad, up_grad, *refs):
    grad_gate, grad_up = refs[-2:]
    grad_gate[0] = dot(rows[0], gate_grad[0], TN)
    grad_up[0] = dot(rows[0], up_grad[0], TN)


def weight_grads(rows, gate_grad, up_grad, before, expert, part=0, parts=1):
    experts, slots, features = rows.shape
    units = gate_grad.shape[2]
    wide = FEATURE_TILE
    steps = features // parts // wide
    unit = pl.BlockSpec((1, slots, units), lambda d: (expert, 0, 0))
    out = pl.BlockSpec((1, wide, units), lambda d: (expert, part * steps + d, 0))
    kept = [] if before is None else list(before)
    return pl.pallas_call(
        weights_kernel,
        grid=(steps,),
        in_specs=[
            pl.BlockSpec((1, slots, wide), lambda d: (expert, 0, part * steps + d)), unit, unit
        ]
        + [pl.BlockSpec(memory_space=pl.ANY)] * len(kept),
        out_specs=[out, out],
        out_shape=[jax.ShapeDtypeStruct((experts, features, units), F32)] * 2,
        input_output_aliases={3 + i: i for i in range(len(kept))},
        compiler_params=params(1),
        cost_estimate=pl.CostEstimate(
            flops=4 * slots * features * units // parts,
            bytes_accessed=8 * features * units // parts,
            transcendentals=0,
        ),
    )(rows, gate_grad, up_grad, *kept)


def route_table(routes, gate_values):
    tokens = routes.shape[0]
    experts = jnp.arange(EXPERTS, dtype=jnp.int32)[:, None, None]
    match = routes.T[None] == experts
    member = jnp.any(match, axis=1)
    gate = jnp.sum(jnp.where(match, gate_values.T[None], 0.0), axis=1)
    place = jnp.arange(tokens, dtype=jnp.int32)
    earlier = (place[:, None] < place[None, :]).astype(BF16)
    slot = jnp.where(member, dot(member.astype(BF16), earlier), -1.0)
    return jnp.stack([slot, gate], axis=1)


def flip(value, axis, bit):
    count = lax.axis_size(axis)
    return lax.ppermute(value, axis, [(i, i ^ bit) for i in range(count)])


def swap_order(value, side, pair, dim):
    shape = value.shape
    value = value.reshape(shape[:dim] + (2, 2, shape[dim] // 4) + shape[dim + 1 :])
    value = jnp.where(side == 1, jnp.flip(value, dim), value)
    return jnp.where(pair == 1, jnp.flip(value, dim + 1), value).reshape(shape)


def add(*terms):
    total = terms[0].astype(F32)
    for term in terms[1:]:
        total = total + term.astype(F32)
    return total.astype(BF16)


def fetch_near(block, mine):
    across = flip(mine, "expert", 2)
    sibling = flip(block, "expert", 1)
    beside = flip(across, "dp", 1)
    return [
        block, sibling, across, beside, flip(across, "expert", 1), flip(beside, "expert", 1)
    ]


def local_near(out_grad, routes, gate_values, layer_input, w_gate, w_up, w_down):
    experts, features, _ = w_gate.shape
    me = lax.axis_index("expert")
    position = lax.axis_index("dp")
    side, pair = position % 2, position // 2 % 2
    tokens = out_grad.shape[0]
    half, quarter = tokens // 2, tokens // 4
    x_mine = lax.dynamic_slice_in_dim(layer_input, side * half, half, 0)
    g_mine = lax.dynamic_slice_in_dim(out_grad, side * half, half, 0)
    x_mine, g_mine, layer_input, out_grad, routes = lax.optimization_barrier(
        (x_mine, g_mine, layer_input, out_grad, routes)
    )
    rows_in = fetch_near(layer_input, x_mine)
    grads_in = fetch_near(out_grad, g_mine)
    table = route_table(routes, gate_values)
    tables = []
    for r in range(4):
        part = lax.dynamic_slice_in_dim(table, (me ^ r) * experts, experts, 0)
        tables.append(flip(part, "expert", r) if r > 0 else part)
    table = jnp.stack(tables, axis=2)
    slot_out = swap_order(table[:, 0], side, pair, 2)
    far = jnp.where(side == 1, jnp.roll(table[:, :, 2:], half, axis=3), table[:, :, 2:])
    table = jnp.concatenate([table[:, :, :2], far], axis=2)
    slot, weight = table[:, 0], table[:, 1]
    rows, act, slope = forward(rows_in, slot, w_gate, w_up)
    gate_grad, up_grad = hidden_grads(grads_in, slot, weight, act, slope, w_down)

    groups = ((0, 2), (1, 3))
    kept_a, sent_a = input_sums(slot_out, gate_grad, up_grad, w_gate, w_up, groups, 0, 2)
    kept_b, sent_b = input_sums(slot_out, gate_grad, up_grad, w_gate, w_up, groups, 1, 2)

    def piece(after, before, expert, part):
        held, rows_now = lax.optimization_barrier((after, rows))
        return held, weight_grads(rows_now, gate_grad, up_grad, before, expert, part, 2)

    chip_a = add(kept_a, flip(sent_a, "expert", 1))
    sent_b, grads = piece(sent_b, None, 0, 0)
    far_a = flip(chip_a[tokens:], "expert", 2)
    got_b = flip(sent_b, "expert", 1)
    got_b, far_a, *grads = lax.optimization_barrier((got_b, far_a, *grads))
    own_a = add(chip_a[:tokens], far_a)
    mine_a, other_a = own_a[:half], own_a[half:]
    chip_b = [add(kept_b[i : i + half], got_b[i : i + half]) for i in range(0, 2 * tokens, half)]
    (mine_b, other_b, far_mine_b, far_other_b) = chip_b
    other_b = jnp.concatenate([other_b, far_other_b], axis=0)
    other_b, grads = piece(other_b, grads, 0, 1)
    got_a, got_b = flip(other_a, "dp", 1), flip(other_b, "dp", 1)
    got_a, got_b, *grads = lax.optimization_barrier((got_a, got_b, *grads))
    mine_a = add(mine_a, got_a)
    far_mine_b = add(far_mine_b, got_b[half:])
    far_mine_b, grads = piece(far_mine_b, grads, 1, 0)
    got_y = flip(far_mine_b, "expert", 2)
    got_z = flip(mine_a[quarter:], "dp", 2)
    got_y, got_z, *grads = lax.optimization_barrier((got_y, got_z, *grads))
    mine_b = add(mine_b, got_b[:half], got_y)
    mine_a = add(mine_a[:quarter], got_z)
    mine_a, grads = piece(mine_a, grads, 1, 1)
    got_b = flip(mine_b[quarter:], "dp", 2)
    got_a = flip(mine_a, "dp", 4)
    got_a, got_b, *grads = lax.optimization_barrier((got_a, got_b, *grads))
    mine_a = add(mine_a, got_a)
    mine_b = add(mine_b[:quarter], got_b)
    mine_b = add(mine_b, flip(mine_b, "dp", 4))
    halves = []
    for mine in (mine_a, mine_b):
        both = jnp.concatenate([mine, flip(mine, "dp", 2)], axis=0)
        halves.append(jnp.concatenate([both, flip(both, "dp", 1)], axis=0))
    total = swap_order(jnp.concatenate(halves, axis=1), side, pair, 0)
    return (total, *grads)


def local_any(out_grad, routes, gate_values, layer_input, w_gate, w_up, w_down):
    experts = w_gate.shape[0]
    me = lax.axis_index("expert")
    rows_in = lax.all_gather(layer_input, "expert", tiled=True)
    grads_in = lax.all_gather(out_grad, "expert", tiled=True)
    table = lax.all_gather(route_table(routes, gate_values), "expert")
    table = lax.dynamic_slice_in_dim(table, me * experts, experts, 1)
    slot, weight = table[:, :, 0].swapaxes(0, 1), table[:, :, 1].swapaxes(0, 1)
    rows, act, slope = forward([rows_in], slot, w_gate, w_up)
    groups = (tuple(range(slot.shape[1])),)
    gate_grad, up_grad = hidden_grads([grads_in], slot, weight, act, slope, w_down)
    (sums,) = input_sums(slot, gate_grad, up_grad, w_gate, w_up, groups, 0, 1)
    grads = None
    for l in range(experts):
        grads = weight_grads(rows, gate_grad, up_grad, grads, l)
    own = lax.psum_scatter(sums, "expert", scatter_dimension=0, tiled=True)
    return (lax.psum(own, "dp"), *grads)


def solution(mesh):
    near = mesh.shape["dp"] == 8 and mesh.shape["expert"] == 4
    placed = (
        P("expert", None),
        P("expert", None),
        P("expert", None),
        P("expert", None),
        P("expert", None, "dp"),
        P("expert", None, "dp"),
        P("expert", None, "dp"),
    )
    return jax.shard_map(
        local_near if near else local_any,
        mesh=mesh,
        in_specs=placed,
        out_specs=(P("expert", None), P("expert", None, "dp"), P("expert", None, "dp")),
        check_vma=False,
    )
```

profile of v0, /device:TPU:0, one launch (start us, length us, event | category | flops | bytes accessed | tf_op | source)
XLA Modules:
  0.0 151.4 jit_solution(3845719757338660512)
XLA Ops:
  0.7 1.2 constant_dynamic-slice_fusion
  1.9 3.0 %collective-permute-start.9 = (bf16[64,3072]{1,0:T(8,128)(2,1)S(1)}, bf16[64,3072]{1,0:T(8,128)(2,1)S(1)}, u32[]{:S(2)}, u32[]{:S(2)}) collective-permute-start(bf16[64,3072]{1,0:T(8,128)(2,1)S(1)} %get-tuple-element.53), channel_id=1, source_target_pairs={{0,2},{1,3},{2,0},{3,1},{4,6},{5,7},{6,4},{7,5},{8,10},{9,11},{10,... | collective-permute-start | bytes 1179656 | tf_op jit(solution)/shard_map/ppermute | solution.py:243
  5.0 0.1 fusion
  5.2 0.1 collective-permute-start.1
  5.3 2.0 %collective-permute-start.2 = (f32[2,2,128]{2,0,1:T(2,128)S(1)}, f32[2,2,128]{2,0,1:T(2,128)S(1)}, u32[]{:S(2)}, u32[]{:S(2)}) collective-permute-start(f32[2,2,128]{2,0,1:T(2,128)S(1)} %get-tuple-element.102), channel_id=1, source_target_pairs={{0,3},{1,2},{2,1},{3,0},{4,7},{5,6},{6,5},{7,4},{8,11},{9,10},{10,... | collective-permute-start | bytes 6152 | tf_op jit(solution)/shard_map/ppermute | solution.py:243
  7.4 0.1 collective-permute-start.4
  7.5 7.5 %collective-permute-done.1 = f32[2,2,128]{2,0,1:T(2,128)S(1)} collective-permute-done((f32[2,2,128]{2,0,1:T(2,128)S(1)}, f32[2,2,128]{2,0,1:T(2,128)S(1)}, u32[]{:S(2)}, u32[]{:S(2)}) %collective-permute-start.1) | collective-permute-done | bytes 2080 | tf_op jit(solution)/shard_map/ppermute | solution.py:243
  15.0 0.5 collective-permute-start.8
  15.6 2.1 %collective-permute-start.10 = (bf16[64,3072]{1,0:T(8,128)(2,1)S(1)}, bf16[64,3072]{1,0:T(8,128)(2,1)S(1)}, u32[]{:S(2)}, u32[]{:S(2)}) collective-permute-start(bf16[64,3072]{1,0:T(8,128)(2,1)S(1)} %collective-permute-done.9.refs_2_), channel_id=1, source_target_pairs={{0,4},{4,0},{8,12},{12,8},{16,20},{20,16},{24,28},{28,24},{1,5},{5... | collective-permute-start | bytes 1179656 | tf_op jit(solution)/shard_map/ppermute | solution.py:243
  17.9 4.7 %collective-permute-done.4.refs_2_ = bf16[64,3072]{1,0:T(8,128)(2,1)S(1)} collective-permute-done((bf16[64,3072]{1,0:T(8,128)(2,1)S(1)}, bf16[64,3072]{1,0:T(8,128)(2,1)S(1)}, u32[]{:S(2)}, u32[]{:S(2)}) %collective-permute-start.4) | collective-permute-done | bytes 393248 | tf_op jit(solution)/shard_map/ppermute | solution.py:243
  22.6 1.7 %collective-permute-start.5 = (bf16[64,3072]{1,0:T(8,128)(2,1)S(1)}, bf16[64,3072]{1,0:T(8,128)(2,1)S(1)}, u32[]{:S(2)}, u32[]{:S(2)}) collective-permute-start(bf16[64,3072]{1,0:T(8,128)(2,1)S(1)} %collective-permute-done.4.refs_2_), channel_id=1, source_target_pairs={{0,4},{4,0},{8,12},{12,8},{16,20},{20,16},{24,28},{28,24},{1,5},{5... | collective-permute-start | bytes 1179656 | tf_op jit(solution)/shard_map/ppermute | solution.py:243
  24.3 3.3 %collective-permute-done.10.refs_3_ = bf16[64,3072]{1,0:T(8,128)(2,1)S(1)} collective-permute-done((bf16[64,3072]{1,0:T(8,128)(2,1)S(1)}, bf16[64,3072]{1,0:T(8,128)(2,1)S(1)}, u32[]{:S(2)}, u32[]{:S(2)}) %collective-permute-start.10) | collective-permute-done | bytes 393248 | tf_op jit(solution)/shard_map/ppermute | solution.py:243
  27.8 7.7 %collective-permute-done.5.refs_3_ = bf16[64,3072]{1,0:T(8,128)(2,1)S(1)} collective-permute-done((bf16[64,3072]{1,0:T(8,128)(2,1)S(1)}, bf16[64,3072]{1,0:T(8,128)(2,1)S(1)}, u32[]{:S(2)}, u32[]{:S(2)}) %collective-permute-start.5) | collective-permute-done | bytes 393248 | tf_op jit(solution)/shard_map/ppermute | solution.py:243
  35.5 0.5 collective-permute-start.7
  36.0 16.6 %shard_map.94 = (bf16[2,320,3072]{2,1,0:T(8,128)(2,1)}, f32[2,320,1024]{2,1,0:T(8,128)}, f32[2,320,1024]{2,1,0:T(8,128)}) custom-call(bf16[128,3072]{1,0:T(8,128)(2,1)} %refs_0_, bf16[128,3072]{1,0:T(8,128)(2,1)} %collective-permute-done.8.refs_1_, bf16[64,3072]{1,0:T(8,128)(2,1)S(1)} %collective-permute-done.9.refs_2_, ...), custom_call_target="tpu_custom_call" | custom-call | flops 8053063680 | bytes 25165824 | tf_op jit(solution)/shard_map/pallas_call | solution.py:87
  52.6 12.0 %shard_map.95 = (bf16[2,320,1024]{2,1,0:T(8,128)(2,1)}, bf16[2,320,1024]{2,1,0:T(8,128)(2,1)}) custom-call(bf16[128,3072]{1,0:T(8,128)(2,1)} %refs_0_.1, bf16[128,3072]{1,0:T(8,128)(2,1)} %collective-permute-done.3.refs_1_, bf16[64,3072]{1,0:T(8,128)(2,1)S(1)} %collective-permute-done.4.refs_2_, bf16[64,3072]{1,0:T(8,128)(2,1)S(1)} %collective-permute-done.5.refs_3_, ...), custom_call_target="tpu_custom_call" | custom-call | flops 4026531840 | bytes 12582912 | tf_op jit(solution)/shard_map/pallas_call | solution.py:138
  64.6 10.2 %shard_map.96 = (bf16[256,1536]{1,0:T(8,128)(2,1)S(1)}, bf16[256,1536]{1,0:T(8,128)(2,1)S(1)}) custom-call(f32[2,4,128]{2,1,0:T(4,128)S(1)} %reshape.17.slot, bf16[2,320,1024]{2,1,0:T(8,128)(2,1)} %get-tuple-element.56.gate_grad, bf16[2,320,1024]{2,1,0:T(8,128)(2,1)} %get-tuple-element.57.up_grad, bf16[2,3072,1024]{2,1,0:T(8,128)(2,1)} %w_gate.3, ...), custom_call_target="tpu_custom_call" | custom-call | flops 4026531840 | bytes 12582912 | tf_op jit(solution)/shard_map/pallas_call | solution.py:179
  74.8 0.1 collective-permute-start.13
  74.9 10.2 %shard_map.97 = (bf16[256,1536]{1,0:T(8,128)(2,1)S(1)}, bf16[256,1536]{1,0:T(8,128)(2,1)S(1)}) custom-call(f32[2,4,128]{2,1,0:T(4,128)S(1)} %reshape.17.slot, bf16[2,320,1024]{2,1,0:T(8,128)(2,1)} %get-tuple-element.56.gate_grad, bf16[2,320,1024]{2,1,0:T(8,128)(2,1)} %get-tuple-element.57.up_grad, bf16[2,3072,1024]{2,1,0:T(8,128)(2,1)} %w_gate.3, ...), custom_call_target="tpu_custom_call" | custom-call | flops 4026531840 | bytes 12582912 | tf_op jit(solution)/shard_map/pallas_call | solution.py:179
  85.1 0.5 collective-permute-start.14
  85.7 0.2 add_convert_fusion
  85.9 1.8 %collective-permute-start.15 = (bf16[128,1536]{1,0:T(8,128)(2,1)S(1)}, bf16[128,1536]{1,0:T(8,128)(2,1)S(1)}, u32[]{:S(2)}, u32[]{:S(2)}) collective-permute-start(bf16[128,1536]{1,0:T(8,128)(2,1)S(1)} %slice.109), channel_id=1, source_target_pairs={{0,2},{1,3},{2,0},{3,1},{4,6},{5,7},{6,4},{7,5},{8,10},{9,11},{10,... | collective-permute-start | bytes 1179656 | tf_op jit(solution)/shard_map/ppermute | solution.py:243
  87.7 7.7 %shard_map.98 = (f32[2,3072,1024]{2,1,0:T(8,128)}, f32[2,3072,1024]{2,1,0:T(8,128)}) custom-call(bf16[2,320,3072]{2,1,0:T(8,128)(2,1)} %get-tuple-element.86.rows, bf16[2,320,1024]{2,1,0:T(8,128)(2,1)S(1)} %copy-done, bf16[2,320,1024]{2,1,0:T(8,128)(2,1)} %get-tuple-element.57.up_grad), custom_call_target="tpu_custom_call" | custom-call | flops 2013265920 | bytes 12582912 | tf_op jit(solution)/shard_map/pallas_call | solution.py:210
  95.4 1.6 %collective-permute-done.15 = bf16[128,1536]{1,0:T(8,128)(2,1)S(1)} collective-permute-done((bf16[128,1536]{1,0:T(8,128)(2,1)S(1)}, bf16[128,1536]{1,0:T(8,128)(2,1)S(1)}, u32[]{:S(2)}, u32[]{:S(2)}) %collective-permute-start.15) | collective-permute-done | bytes 393248 | tf_op jit(solution)/shard_map/ppermute | solution.py:243
  97.1 0.1 add_convert_fusion.8
  97.2 1.8 %collective-permute-start.17 = (bf16[128,1536]{1,0:T(8,128)(2,1)S(1)}, bf16[128,1536]{1,0:T(8,128)(2,1)S(1)}, u32[]{:S(2)}, u32[]{:S(2)}) collective-permute-start(bf16[128,1536]{1,0:T(8,128)(2,1)S(1)} %pad_maximum_fusion), channel_id=1, source_target_pairs={{0,4},{4,0},{8,12},{12,8},{16,20},{20,16},{24,28},{28,24},{1,5},{5... | collective-permute-start | bytes 1179656 | tf_op jit(solution)/shard_map/ppermute | solution.py:243
  99.0 0.1 add_convert_fusion.1
  99.1 0.4 collective-permute-start.16
  99.5 7.7 %shard_map.99 = (f32[2,3072,1024]{2,1,0:T(8,128)}, f32[2,3072,1024]{2,1,0:T(8,128)}) custom-call(bf16[2,320,3072]{2,1,0:T(8,128)(2,1)} %get-tuple-element.86.rows, bf16[2,320,1024]{2,1,0:T(8,128)(2,1)S(1)} %copy-done, bf16[2,320,1024]{2,1,0:T(8,128)(2,1)} %get-tuple-element.57.up_grad, ...), custom_call_target="tpu_custom_call", output_to_operand_aliasing={{0}: (3, {}), {1}: (4, {})} | custom-call | flops 2013265920 | bytes 12582912 | tf_op jit(solution)/shard_map/pallas_call | solution.py:210
  107.2 4.6 %collective-permute-done.16 = bf16[64,1536]{1,0:T(8,128)(2,1)S(1)} collective-permute-done((bf16[64,1536]{1,0:T(8,128)(2,1)S(1)}, bf16[64,1536]{1,0:T(8,128)(2,1)S(1)}, u32[]{:S(2)}, u32[]{:S(2)}) %collective-permute-start.16) | collective-permute-done | bytes 196640 | tf_op jit(solution)/shard_map/ppermute | solution.py:243
  111.8 1.8 %collective-permute-start.18 = (bf16[64,1536]{1,0:T(8,128)(2,1)S(1)}, bf16[64,1536]{1,0:T(8,128)(2,1)S(1)}, u32[]{:S(2)}, u32[]{:S(2)}) collective-permute-start(bf16[64,1536]{1,0:T(8,128)(2,1)S(1)} %add_convert_fusion.4), channel_id=1, source_target_pairs={{0,2},{1,3},{2,0},{3,1},{4,6},{5,7},{6,4},{7,5},{8,10},{9,11},{10,... | collective-permute-start | bytes 589832 | tf_op jit(solution)/shard_map/ppermute | solution.py:243
  113.6 1.6 %collective-permute-start.19 = (bf16[32,1536]{1,0:T(8,128)(2,1)S(1)}, bf16[32,1536]{1,0:T(8,128)(2,1)S(1)}, u32[]{:S(2)}, u32[]{:S(2)}) collective-permute-start(bf16[32,1536]{1,0:T(8,128)(2,1)S(1)} %slice.113), channel_id=1, source_target_pairs={{0,8},{4,12},{8,0},{12,4},{16,24},{20,28},{24,16},{28,20},{1,9},{5... | collective-permute-start | bytes 294920 | tf_op jit(solution)/shard_map/ppermute | solution.py:243
  115.3 7.7 %shard_map.100 = (f32[2,3072,1024]{2,1,0:T(8,128)}, f32[2,3072,1024]{2,1,0:T(8,128)}) custom-call(bf16[2,320,3072]{2,1,0:T(8,128)(2,1)} %get-tuple-element.86.rows, bf16[2,320,1024]{2,1,0:T(8,128)(2,1)S(1)} %copy-done, bf16[2,320,1024]{2,1,0:T(8,128)(2,1)} %get-tuple-element.57.up_grad, ...), custom_call_target="tpu_custom_call", output_to_operand_aliasing={{0}: (3, {}), {1}: (4, {})} | custom-call | flops 2013265920 | bytes 12582912 | tf_op jit(solution)/shard_map/pallas_call | solution.py:210
  123.0 0.1 add_convert_fusion.2
  123.1 0.5 collective-permute-start.21
  123.7 2.6 %collective-permute-start.20 = (bf16[32,1536]{1,0:T(8,128)(2,1)S(1)}, bf16[32,1536]{1,0:T(8,128)(2,1)S(1)}, u32[]{:S(2)}, u32[]{:S(2)}) collective-permute-start(bf16[32,1536]{1,0:T(8,128)(2,1)S(1)} %add_convert_fusion.12), channel_id=1, source_target_pairs={{0,16},{4,20},{8,24},{12,28},{16,0},{20,4},{24,8},{28,12},{1,17},{... | collective-permute-start | bytes 294920 | tf_op jit(solution)/shard_map/ppermute | solution.py:243
  126.3 7.7 %shard_map.101 = (f32[2,3072,1024]{2,1,0:T(8,128)}, f32[2,3072,1024]{2,1,0:T(8,128)}) custom-call(bf16[2,320,3072]{2,1,0:T(8,128)(2,1)} %get-tuple-element.86.rows, bf16[2,320,1024]{2,1,0:T(8,128)(2,1)S(1)} %copy-done, bf16[2,320,1024]{2,1,0:T(8,128)(2,1)} %get-tuple-element.57.up_grad, ...), custom_call_target="tpu_custom_call", output_to_operand_aliasing={{0}: (3, {}), {1}: (4, {})} | custom-call | flops 2013265920 | bytes 12582912 | tf_op jit(solution)/shard_map/pallas_call | solution.py:210
  134.0 0.4 collective-permute-start.24
  134.4 1.6 %collective-permute-start.22 = (bf16[32,1536]{1,0:T(8,128)(2,1)S(1)}, bf16[32,1536]{1,0:T(8,128)(2,1)S(1)}, u32[]{:S(2)}, u32[]{:S(2)}) collective-permute-start(bf16[32,1536]{1,0:T(8,128)(2,1)S(1)} %add_convert_fusion.11), channel_id=1, source_target_pairs={{0,8},{4,12},{8,0},{12,4},{16,24},{20,28},{24,16},{28,20},{1,9},{5... | collective-permute-start | bytes 294920 | tf_op jit(solution)/shard_map/ppermute | solution.py:243
  136.1 3.6 %collective-permute-done.24 = bf16[32,1536]{1,0:T(8,128)(2,1)S(1)} collective-permute-done((bf16[32,1536]{1,0:T(8,128)(2,1)S(1)}, bf16[32,1536]{1,0:T(8,128)(2,1)S(1)}, u32[]{:S(2)}, u32[]{:S(2)}) %collective-permute-start.24) | collective-permute-done | bytes 98336 | tf_op jit(solution)/shard_map/ppermute | solution.py:243
  139.7 1.9 %collective-permute-start.25 = (bf16[32,1536]{1,0:T(8,128)(2,1)S(1)}, bf16[32,1536]{1,0:T(8,128)(2,1)S(1)}, u32[]{:S(2)}, u32[]{:S(2)}) collective-permute-start(bf16[32,1536]{1,0:T(8,128)(2,1)S(1)} %add_convert_fusion.9), channel_id=1, source_target_pairs={{0,8},{4,12},{8,0},{12,4},{16,24},{20,28},{24,16},{28,20},{1,9},{5... | collective-permute-start | bytes 294920 | tf_op jit(solution)/shard_map/ppermute | solution.py:243
  141.7 1.5 %collective-permute-start.23 = (bf16[64,1536]{1,0:T(8,128)(2,1)S(1)}, bf16[64,1536]{1,0:T(8,128)(2,1)S(1)}, u32[]{:S(2)}, u32[]{:S(2)}) collective-permute-start(bf16[64,1536]{1,0:T(8,128)(2,1)S(1)} %pad_maximum_fusion.1), channel_id=1, source_target_pairs={{0,4},{4,0},{8,12},{12,8},{16,20},{20,16},{24,28},{28,24},{1,5},{5... | collective-permute-start | bytes 589832 | tf_op jit(solution)/shard_map/ppermute | solution.py:243
  143.2 1.2 collective-permute-done.25
  144.4 1.5 %collective-permute-start.26 = (bf16[64,1536]{1,0:T(8,128)(2,1)S(1)}, bf16[64,1536]{1,0:T(8,128)(2,1)S(1)}, u32[]{:S(2)}, u32[]{:S(2)}) collective-permute-start(bf16[64,1536]{1,0:T(8,128)(2,1)S(1)} %pad_maximum_fusion.2), channel_id=1, source_target_pairs={{0,4},{4,0},{8,12},{12,8},{16,20},{20,16},{24,28},{28,24},{1,5},{5... | collective-permute-start | bytes 589832 | tf_op jit(solution)/shard_map/ppermute | solution.py:243
  146.0 2.0 %collective-permute-done.23 = bf16[64,1536]{1,0:T(8,128)(2,1)S(1)} collective-permute-done((bf16[64,1536]{1,0:T(8,128)(2,1)S(1)}, bf16[64,1536]{1,0:T(8,128)(2,1)S(1)}, u32[]{:S(2)}, u32[]{:S(2)}) %collective-permute-start.23) | collective-permute-done | bytes 196640 | tf_op jit(solution)/shard_map/ppermute | solution.py:243
  147.9 2.2 %collective-permute-done.26 = bf16[64,1536]{1,0:T(8,128)(2,1)S(1)} collective-permute-done((bf16[64,1536]{1,0:T(8,128)(2,1)S(1)}, bf16[64,1536]{1,0:T(8,128)(2,1)S(1)}, u32[]{:S(2)}, u32[]{:S(2)}) %collective-permute-start.26) | collective-permute-done | bytes 196640 | tf_op jit(solution)/shard_map/ppermute | solution.py:243
  150.3 0.1 reverse_select_fusion.1
  150.4 1.0 reverse_select_fusion
  (57 shorter events, 1.1 us)
Async XLA Ops:
  0.6 14.3 %copy-start.1 = (bf16[128,3072]{1,0:T(8,128)(2,1)S(1)}, bf16[128,3072]{1,0:T(8,128)(2,1)}, u32[]{:S(2)}) copy-start(bf16[128,3072]{1,0:T(8,128)(2,1)} %refs_0_.1) | copy-start | bytes 2359300
  0.6 4.3 %copy-start.2 = (s32[128,4]{0,1:T(4,128)S(1)}, s32[128,4]{0,1:T(4,128)}, u32[]{:S(2)}) copy-start(s32[128,4]{0,1:T(4,128)} %param.8) | copy-start | bytes 6148
  0.7 4.3 %copy-start.3 = (f32[128,4]{0,1:T(4,128)S(1)}, f32[128,4]{0,1:T(4,128)}, u32[]{:S(2)}) copy-start(f32[128,4]{0,1:T(4,128)} %param.9) | copy-start | bytes 6148
  1.9 13.6 %collective-permute-start.9 = (bf16[64,3072]{1,0:T(8,128)(2,1)S(1)}, bf16[64,3072]{1,0:T(8,128)(2,1)S(1)}, u32[]{:S(2)}, u32[]{:S(2)}) collective-permute-start(bf16[64,3072]{1,0:T(8,128)(2,1)S(1)} %get-tuple-element.53), channel_id=1, source_target_pairs={{0,2},{1,3},{2,0},{3,1},{4,6},{5,7},{6,4},{7,5},{8,10},{9,11},{10,... | collective-permute-start | bytes 1179656 | tf_op jit(solution)/shard_map/ppermute | solution.py:243
  5.2 9.8 %collective-permute-start.1 = (f32[2,2,128]{2,0,1:T(2,128)S(1)}, f32[2,2,128]{2,0,1:T(2,128)S(1)}, u32[]{:S(2)}, u32[]{:S(2)}) collective-permute-start(f32[2,2,128]{2,0,1:T(2,128)S(1)} %get-tuple-element.99), channel_id=1, source_target_pairs={{0,2},{1,3},{2,0},{3,1},{4,6},{5,7},{6,4},{7,5},{8,10},{9,11},{10,... | collective-permute-start | bytes 6152 | tf_op jit(solution)/shard_map/ppermute | solution.py:243
  5.3 9.7 %collective-permute-start = (f32[2,2,128]{2,0,1:T(2,128)S(1)}, f32[2,2,128]{2,0,1:T(2,128)S(1)}, u32[]{:S(2)}, u32[]{:S(2)}) collective-permute-start(f32[2,2,128]{2,0,1:T(2,128)S(1)} %get-tuple-element.101), channel_id=1, source_target_pairs={{0,1},{1,0},{2,3},{3,2},{4,5},{5,4},{6,7},{7,6},{8,9},{9,8},{10,11... | collective-permute-start | bytes 6152 | tf_op jit(solution)/shard_map/ppermute | solution.py:243
  5.3 10.1 %collective-permute-start.2 = (f32[2,2,128]{2,0,1:T(2,128)S(1)}, f32[2,2,128]{2,0,1:T(2,128)S(1)}, u32[]{:S(2)}, u32[]{:S(2)}) collective-permute-start(f32[2,2,128]{2,0,1:T(2,128)S(1)} %get-tuple-element.102), channel_id=1, source_target_pairs={{0,3},{1,2},{2,1},{3,0},{4,7},{5,6},{6,5},{7,4},{8,11},{9,10},{10,... | collective-permute-start | bytes 6152 | tf_op jit(solution)/shard_map/ppermute | solution.py:243
  7.4 15.2 %collective-permute-start.4 = (bf16[64,3072]{1,0:T(8,128)(2,1)S(1)}, bf16[64,3072]{1,0:T(8,128)(2,1)S(1)}, u32[]{:S(2)}, u32[]{:S(2)}) collective-permute-start(bf16[64,3072]{1,0:T(8,128)(2,1)S(1)} %get-tuple-element.51), channel_id=1, source_target_pairs={{0,2},{1,3},{2,0},{3,1},{4,6},{5,7},{6,4},{7,5},{8,10},{9,11},{10,... | collective-permute-start | bytes 1179656 | tf_op jit(solution)/shard_map/ppermute | solution.py:243
  14.9 37.6 %collective-permute-start.3 = (bf16[128,3072]{1,0:T(8,128)(2,1)S(1)}, bf16[128,3072]{1,0:T(8,128)(2,1)}, u32[]{:S(2)}, u32[]{:S(2)}) collective-permute-start(bf16[128,3072]{1,0:T(8,128)(2,1)S(1)} %copy-done.1), channel_id=1, source_target_pairs={{0,1},{1,0},{2,3},{3,2},{4,5},{5,4},{6,7},{7,6},{8,9},{9,8},{10,11... | collective-permute-start | bytes 2359304 | tf_op jit(solution)/shard_map/ppermute | solution.py:243
  15.0 21.0 %collective-permute-start.8 = (bf16[128,3072]{1,0:T(8,128)(2,1)}, bf16[128,3072]{1,0:T(8,128)(2,1)}, u32[]{:S(2)}, u32[]{:S(2)}) collective-permute-start(bf16[128,3072]{1,0:T(8,128)(2,1)} %refs_0_), channel_id=1, source_target_pairs={{0,1},{1,0},{2,3},{3,2},{4,5},{5,4},{6,7},{7,6},{8,9},{9,8},{10,11... | collective-permute-start | bytes 2359304 | tf_op jit(solution)/shard_map/ppermute | solution.py:243
  15.6 12.0 %collective-permute-start.10 = (bf16[64,3072]{1,0:T(8,128)(2,1)S(1)}, bf16[64,3072]{1,0:T(8,128)(2,1)S(1)}, u32[]{:S(2)}, u32[]{:S(2)}) collective-permute-start(bf16[64,3072]{1,0:T(8,128)(2,1)S(1)} %collective-permute-done.9.refs_2_), channel_id=1, source_target_pairs={{0,4},{4,0},{8,12},{12,8},{16,20},{20,16},{24,28},{28,24},{1,5},{5... | collective-permute-start | bytes 1179656 | tf_op jit(solution)/shard_map/ppermute | solution.py:243
  17.8 17.6 %collective-permute-start.11 = (bf16[64,3072]{1,0:T(8,128)(2,1)S(1)}, bf16[64,3072]{1,0:T(8,128)(2,1)S(1)}, u32[]{:S(2)}, u32[]{:S(2)}) collective-permute-start(bf16[64,3072]{1,0:T(8,128)(2,1)S(1)} %collective-permute-done.9.refs_2_), channel_id=1, source_target_pairs={{0,1},{1,0},{2,3},{3,2},{4,5},{5,4},{6,7},{7,6},{8,9},{9,8},{10,11... | collective-permute-start | bytes 1179656 | tf_op jit(solution)/shard_map/ppermute | solution.py:243
  22.6 12.9 %collective-permute-start.5 = (bf16[64,3072]{1,0:T(8,128)(2,1)S(1)}, bf16[64,3072]{1,0:T(8,128)(2,1)S(1)}, u32[]{:S(2)}, u32[]{:S(2)}) collective-permute-start(bf16[64,3072]{1,0:T(8,128)(2,1)S(1)} %collective-permute-done.4.refs_2_), channel_id=1, source_target_pairs={{0,4},{4,0},{8,12},{12,8},{16,20},{20,16},{24,28},{28,24},{1,5},{5... | collective-permute-start | bytes 1179656 | tf_op jit(solution)/shard_map/ppermute | solution.py:243
  27.6 8.4 %collective-permute-start.12 = (bf16[64,3072]{1,0:T(8,128)(2,1)S(1)}, bf16[64,3072]{1,0:T(8,128)(2,1)S(1)}, u32[]{:S(2)}, u32[]{:S(2)}) collective-permute-start(bf16[64,3072]{1,0:T(8,128)(2,1)S(1)} %collective-permute-done.10.refs_3_), channel_id=1, source_target_pairs={{0,1},{1,0},{2,3},{3,2},{4,5},{5,4},{6,7},{7,6},{8,9},{9,8},{10,11... | collective-permute-start | bytes 1179656 | tf_op jit(solution)/shard_map/ppermute | solution.py:243
  35.4 17.1 %collective-permute-start.6 = (bf16[64,3072]{1,0:T(8,128)(2,1)S(1)}, bf16[64,3072]{1,0:T(8,128)(2,1)S(1)}, u32[]{:S(2)}, u32[]{:S(2)}) collective-permute-start(bf16[64,3072]{1,0:T(8,128)(2,1)S(1)} %collective-permute-done.4.refs_2_), channel_id=1, source_target_pairs={{0,1},{1,0},{2,3},{3,2},{4,5},{5,4},{6,7},{7,6},{8,9},{9,8},{10,11... | collective-permute-start | bytes 1179656 | tf_op jit(solution)/shard_map/ppermute | solution.py:243
  35.5 17.1 %collective-permute-start.7 = (bf16[64,3072]{1,0:T(8,128)(2,1)S(1)}, bf16[64,3072]{1,0:T(8,128)(2,1)S(1)}, u32[]{:S(2)}, u32[]{:S(2)}) collective-permute-start(bf16[64,3072]{1,0:T(8,128)(2,1)S(1)} %collective-permute-done.5.refs_3_), channel_id=1, source_target_pairs={{0,1},{1,0},{2,3},{3,2},{4,5},{5,4},{6,7},{7,6},{8,9},{9,8},{10,11... | collective-permute-start | bytes 1179656 | tf_op jit(solution)/shard_map/ppermute | solution.py:243
  74.8 10.8 %collective-permute-start.13 = (bf16[256,1536]{1,0:T(8,128)(2,1)S(1)}, bf16[256,1536]{1,0:T(8,128)(2,1)S(1)}, u32[]{:S(2)}, u32[]{:S(2)}) collective-permute-start(bf16[256,1536]{1,0:T(8,128)(2,1)S(1)} %get-tuple-element.59), channel_id=1, source_target_pairs={{0,1},{1,0},{2,3},{3,2},{4,5},{5,4},{6,7},{7,6},{8,9},{9,8},{10,11... | collective-permute-start | bytes 2359304 | tf_op jit(solution)/shard_map/ppermute | solution.py:243
  85.1 10.3 %collective-permute-start.14 = (bf16[256,1536]{1,0:T(8,128)(2,1)S(1)}, bf16[256,1536]{1,0:T(8,128)(2,1)S(1)}, u32[]{:S(2)}, u32[]{:S(2)}) collective-permute-start(bf16[256,1536]{1,0:T(8,128)(2,1)S(1)} %get-tuple-element.62), channel_id=1, source_target_pairs={{0,1},{1,0},{2,3},{3,2},{4,5},{5,4},{6,7},{7,6},{8,9},{9,8},{10,11... | collective-permute-start | bytes 2359304 | tf_op jit(solution)/shard_map/ppermute | solution.py:243
  85.7 2.1 %copy-start = (bf16[2,320,1024]{2,1,0:T(8,128)(2,1)S(1)}, bf16[2,320,1024]{2,1,0:T(8,128)(2,1)}, u32[]{:S(2)}) copy-start(bf16[2,320,1024]{2,1,0:T(8,128)(2,1)} %get-tuple-element.56.gate_grad) | copy-start | bytes 3932164
  85.9 11.2 %collective-permute-start.15 = (bf16[128,1536]{1,0:T(8,128)(2,1)S(1)}, bf16[128,1536]{1,0:T(8,128)(2,1)S(1)}, u32[]{:S(2)}, u32[]{:S(2)}) collective-permute-start(bf16[128,1536]{1,0:T(8,128)(2,1)S(1)} %slice.109), channel_id=1, source_target_pairs={{0,2},{1,3},{2,0},{3,1},{4,6},{5,7},{6,4},{7,5},{8,10},{9,11},{10,... | collective-permute-start | bytes 1179656 | tf_op jit(solution)/shard_map/ppermute | solution.py:243
  97.2 14.5 %collective-permute-start.17 = (bf16[128,1536]{1,0:T(8,128)(2,1)S(1)}, bf16[128,1536]{1,0:T(8,128)(2,1)S(1)}, u32[]{:S(2)}, u32[]{:S(2)}) collective-permute-start(bf16[128,1536]{1,0:T(8,128)(2,1)S(1)} %pad_maximum_fusion), channel_id=1, source_target_pairs={{0,4},{4,0},{8,12},{12,8},{16,20},{20,16},{24,28},{28,24},{1,5},{5... | collective-permute-start | bytes 1179656 | tf_op jit(solution)/shard_map/ppermute | solution.py:243
  99.1 12.6 %collective-permute-start.16 = (bf16[64,1536]{1,0:T(8,128)(2,1)S(1)}, bf16[64,1536]{1,0:T(8,128)(2,1)S(1)}, u32[]{:S(2)}, u32[]{:S(2)}) collective-permute-start(bf16[64,1536]{1,0:T(8,128)(2,1)S(1)} %slice.111), channel_id=1, source_target_pairs={{0,4},{4,0},{8,12},{12,8},{16,20},{20,16},{24,28},{28,24},{1,5},{5... | collective-permute-start | bytes 589832 | tf_op jit(solution)/shard_map/ppermute | solution.py:243
  111.8 11.2 %collective-permute-start.18 = (bf16[64,1536]{1,0:T(8,128)(2,1)S(1)}, bf16[64,1536]{1,0:T(8,128)(2,1)S(1)}, u32[]{:S(2)}, u32[]{:S(2)}) collective-permute-start(bf16[64,1536]{1,0:T(8,128)(2,1)S(1)} %add_convert_fusion.4), channel_id=1, source_target_pairs={{0,2},{1,3},{2,0},{3,1},{4,6},{5,7},{6,4},{7,5},{8,10},{9,11},{10,... | collective-permute-start | bytes 589832 | tf_op jit(solution)/shard_map/ppermute | solution.py:243
  113.6 9.3 %collective-permute-start.19 = (bf16[32,1536]{1,0:T(8,128)(2,1)S(1)}, bf16[32,1536]{1,0:T(8,128)(2,1)S(1)}, u32[]{:S(2)}, u32[]{:S(2)}) collective-permute-start(bf16[32,1536]{1,0:T(8,128)(2,1)S(1)} %slice.113), channel_id=1, source_target_pairs={{0,8},{4,12},{8,0},{12,4},{16,24},{20,28},{24,16},{28,20},{1,9},{5... | collective-permute-start | bytes 294920 | tf_op jit(solution)/shard_map/ppermute | solution.py:243
  123.1 10.8 %collective-permute-start.21 = (bf16[32,1536]{1,0:T(8,128)(2,1)S(1)}, bf16[32,1536]{1,0:T(8,128)(2,1)S(1)}, u32[]{:S(2)}, u32[]{:S(2)}) collective-permute-start(bf16[32,1536]{1,0:T(8,128)(2,1)S(1)} %slice.114), channel_id=1, source_target_pairs={{0,8},{4,12},{8,0},{12,4},{16,24},{20,28},{24,16},{28,20},{1,9},{5... | collective-permute-start | bytes 294920 | tf_op jit(solution)/shard_map/ppermute | solution.py:243
  123.7 10.3 %collective-permute-start.20 = (bf16[32,1536]{1,0:T(8,128)(2,1)S(1)}, bf16[32,1536]{1,0:T(8,128)(2,1)S(1)}, u32[]{:S(2)}, u32[]{:S(2)}) collective-permute-start(bf16[32,1536]{1,0:T(8,128)(2,1)S(1)} %add_convert_fusion.12), channel_id=1, source_target_pairs={{0,16},{4,20},{8,24},{12,28},{16,0},{20,4},{24,8},{28,12},{1,17},{... | collective-permute-start | bytes 294920 | tf_op jit(solution)/shard_map/ppermute | solution.py:243
  134.0 5.7 %collective-permute-start.24 = (bf16[32,1536]{1,0:T(8,128)(2,1)S(1)}, bf16[32,1536]{1,0:T(8,128)(2,1)S(1)}, u32[]{:S(2)}, u32[]{:S(2)}) collective-permute-start(bf16[32,1536]{1,0:T(8,128)(2,1)S(1)} %add_convert_fusion.10), channel_id=1, source_target_pairs={{0,16},{4,20},{8,24},{12,28},{16,0},{20,4},{24,8},{28,12},{1,17},{... | collective-permute-start | bytes 294920 | tf_op jit(solution)/shard_map/ppermute | solution.py:243
  134.4 7.2 %collective-permute-start.22 = (bf16[32,1536]{1,0:T(8,128)(2,1)S(1)}, bf16[32,1536]{1,0:T(8,128)(2,1)S(1)}, u32[]{:S(2)}, u32[]{:S(2)}) collective-permute-start(bf16[32,1536]{1,0:T(8,128)(2,1)S(1)} %add_convert_fusion.11), channel_id=1, source_target_pairs={{0,8},{4,12},{8,0},{12,4},{16,24},{20,28},{24,16},{28,20},{1,9},{5... | collective-permute-start | bytes 294920 | tf_op jit(solution)/shard_map/ppermute | solution.py:243
  139.7 4.7 %collective-permute-start.25 = (bf16[32,1536]{1,0:T(8,128)(2,1)S(1)}, bf16[32,1536]{1,0:T(8,128)(2,1)S(1)}, u32[]{:S(2)}, u32[]{:S(2)}) collective-permute-start(bf16[32,1536]{1,0:T(8,128)(2,1)S(1)} %add_convert_fusion.9), channel_id=1, source_target_pairs={{0,8},{4,12},{8,0},{12,4},{16,24},{20,28},{24,16},{28,20},{1,9},{5... | collective-permute-start | bytes 294920 | tf_op jit(solution)/shard_map/ppermute | solution.py:243
  141.7 6.3 %collective-permute-start.23 = (bf16[64,1536]{1,0:T(8,128)(2,1)S(1)}, bf16[64,1536]{1,0:T(8,128)(2,1)S(1)}, u32[]{:S(2)}, u32[]{:S(2)}) collective-permute-start(bf16[64,1536]{1,0:T(8,128)(2,1)S(1)} %pad_maximum_fusion.1), channel_id=1, source_target_pairs={{0,4},{4,0},{8,12},{12,8},{16,20},{20,16},{24,28},{28,24},{1,5},{5... | collective-permute-start | bytes 589832 | tf_op jit(solution)/shard_map/ppermute | solution.py:243
  144.4 5.7 %collective-permute-start.26 = (bf16[64,1536]{1,0:T(8,128)(2,1)S(1)}, bf16[64,1536]{1,0:T(8,128)(2,1)S(1)}, u32[]{:S(2)}, u32[]{:S(2)}) collective-permute-start(bf16[64,1536]{1,0:T(8,128)(2,1)S(1)} %pad_maximum_fusion.2), channel_id=1, source_target_pairs={{0,4},{4,0},{8,12},{12,8},{16,20},{20,16},{24,28},{28,24},{1,5},{5... | collective-permute-start | bytes 589832 | tf_op jit(solution)/shard_map/ppermute | solution.py:243
where the time goes:
time: 152 us; the launch traced here: 151 us
  Pallas kernels  79.9 us (53%)
  waiting for transfers between devices  38.4 us (25%)
  starting transfers between devices  28.4 us (19%)
  other arithmetic  2.22 us (1%)
  local copies, waits for them, and re-layouts  1.54 us (1%)
    ppermute x27, waiting for transfers between devices, flip(): return lax.ppermute(value, axis, [(i, i ^ bit) for i in range(count)])  38.4 us
    pallas_call x4, Pallas kernels, weight_grads(): pl.pallas_call(weights_kernel, grid=(steps,), in_specs=[pl.BlockSpec((1,...  30.8 us
    ppermute x27, starting transfers between devices, flip(): return lax.ppermute(value, axis, [(i, i ^ bit) for i in range(count)])  28.4 us
    pallas_call x2, Pallas kernels, input_sums(): pl.pallas_call(functools.partial(inputs_kernel, groups), grid=(steps,), i...  20.4 us
    pallas_call x1, Pallas kernels, forward(): pl.pallas_call(functools.partial(forward_kernel, len(pieces)), grid=(expe...  16.6 us
    pallas_call x1, Pallas kernels, hidden_grads(): pl.pallas_call(functools.partial(hidden_kernel, len(pieces)), grid=(exper...  12 us
  transfers between devices with their start and end apart: 27, of which 10 were waited for; matrix products, arithmetic and copies ran while one was open for 1% of the time, Pallas kernels for 38%

commit v1 on v0

v1 whole, which is shorter than its diff:
```python
import functools

import jax
import jax.numpy as jnp
from jax import lax
from jax.experimental import pallas as pl
from jax.experimental.pallas import tpu as pltpu
from jax.sharding import PartitionSpec as P

EXPERTS = 8
MOST = 80
UNIT_TILE = 256
FEATURE_TILE = 512
VMEM_BYTES = 52 * 1024 * 1024
BF16 = jnp.bfloat16
F32 = jnp.float32
NN = (((1,), (0,)), ((), ()))
NT = (((1,), (1,)), ((), ()))
TN = (((0,), (0,)), ((), ()))


def dot(a, b, dims=NN):
    return lax.dot_general(a, b, dims, preferred_element_type=F32)


def params(count):
    return pltpu.CompilerParams(
        dimension_semantics=("arbitrary",) * count, vmem_limit_bytes=VMEM_BYTES
    )


def whole(shape):
    return pl.BlockSpec(
        shape, lambda *_: (0,) * len(shape), pipeline_mode=pl.Buffered(buffer_count=1)
    )


def one_hot(slot_row):
    slots = lax.broadcasted_iota(jnp.int32, (MOST, slot_row.shape[1]), 0)
    return slots == slot_row.astype(jnp.int32)


def gather_block(held, pieces, block):
    tokens = held.shape[0]
    first, at = block * tokens, 0
    for piece in pieces:
        low, high = max(first, at), min(first + tokens, at + piece.shape[0])
        if low < high:
            held[low - first : high - first] = piece[low - at : high - at]
        at += piece.shape[0]


def column_chunks(features):
    step = 768 if features % 768 == 0 else features
    return [slice(c, c + step) for c in range(0, features, step)]


def slots_kernel(count, *refs):
    x_pieces, g_pieces = refs[:count], refs[count : 2 * count]
    slot, weight, w_gate, w_up, w_down = refs[2 * count : 2 * count + 5]
    rows, gate_grad, up_grad, held, grads = refs[-5:]
    blocks = slot.shape[1]

    @pl.when(pl.program_id(1) == 0)
    def _():
        for b in range(blocks):
            mask = one_hot(slot[0, b : b + 1, :])
            scale = jnp.sum(
                jnp.where(mask, weight[0, b : b + 1, :], 0.0), axis=1, keepdims=True
            )
            chosen = mask.astype(BF16)
            span = slice(b * MOST, (b + 1) * MOST)
            gather_block(held, x_pieces, b)
            for cols in column_chunks(held.shape[1]):
                rows[0, span, cols] = dot(chosen, held[:, cols]).astype(BF16)
            gather_block(held, g_pieces, b)
            for cols in column_chunks(held.shape[1]):
                grads[span, cols] = (dot(chosen, held[:, cols]) * scale).astype(BF16)

    gate = dot(rows[0], w_gate[0])
    up = dot(rows[0], w_up[0])
    hidden = dot(grads[...], w_down[0])
    sig = jax.nn.sigmoid(gate)
    up_grad[0] = (hidden * (gate * sig)).astype(BF16)
    gate_grad[0] = (hidden * up * sig * (1.0 + gate * (1.0 - sig))).astype(BF16)


def slot_grads(x_pieces, g_pieces, slot, weight, w_gate, w_up, w_down, before, first, last, part, parts):
    experts, blocks, tokens = slot.shape
    _, features, units = w_gate.shape
    tile = min(UNIT_TILE, units)
    slots = blocks * MOST
    count = last - first
    table = pl.BlockSpec((1, blocks, tokens), lambda l, f: (first + l, 0, 0))
    matrix = pl.BlockSpec((1, features, tile), lambda l, f: (first + l, 0, f))
    unit = pl.BlockSpec((1, slots, tile), lambda l, f: (first + l, part, f))
    pieces = [*x_pieces, *g_pieces]
    kept = [] if before is None else list(before)
    return pl.pallas_call(
        functools.partial(slots_kernel, len(x_pieces)),
        grid=(count, units // tile),
        in_specs=[whole(p.shape) for p in pieces]
        + [table, table, matrix, matrix, matrix]
        + [pl.BlockSpec(memory_space=pl.ANY)] * len(kept),
        out_specs=[
            pl.BlockSpec((1, slots, features), lambda l, f: (first + l, part, 0)), unit, unit
        ],
        out_shape=[
            jax.ShapeDtypeStruct((experts, parts * slots, features), BF16),
            jax.ShapeDtypeStruct((experts, parts * slots, units), BF16),
            jax.ShapeDtypeStruct((experts, parts * slots, units), BF16),
        ],
        scratch_shapes=[pltpu.VMEM((tokens, features), BF16), pltpu.VMEM((slots, features), BF16)],
        input_output_aliases={len(pieces) + 5 + i: i for i in range(len(kept))},
        compiler_params=params(2),
        cost_estimate=pl.CostEstimate(
            flops=6 * count * slots * features * units,
            bytes_accessed=6 * count * features * units,
            transcendentals=count * slots * units,
        ),
    )(*pieces, slot, weight, w_gate, w_up, w_down, *kept)


def inputs_kernel(groups, back, gate_grad, up_grad, w_gate, w_up, *refs):
    sums, held = refs[:-1], refs[-1]
    blocks, tokens, _ = back.shape
    for l in range(gate_grad.shape[0]):
        partial = dot(gate_grad[l], w_gate[l], NT) + dot(up_grad[l], w_up[l], NT)
        for b in range(blocks):
            held[b, l * MOST : (l + 1) * MOST] = partial[b * MOST : (b + 1) * MOST].astype(BF16)
    for out, members in zip(sums, groups):
        for place, b in enumerate(members):
            out[place * tokens : (place + 1) * tokens] = dot(back[b], held[b]).astype(BF16)


def input_sums(back, gate_grad, up_grad, w_gate, w_up, groups, part, parts):
    blocks, tokens, _ = back.shape
    experts, features, units = w_gate.shape
    wide = FEATURE_TILE
    steps = features // parts // wide
    slots = blocks * MOST
    across = pl.BlockSpec((experts, wide, units), lambda i: (0, part * steps + i, 0))
    return pl.pallas_call(
        functools.partial(inputs_kernel, groups),
        grid=(steps,),
        in_specs=[whole(back.shape), whole(gate_grad.shape), whole(up_grad.shape), across, across],
        out_specs=[pl.BlockSpec((len(g) * tokens, wide), lambda i: (0, i)) for g in groups],
        out_shape=[
            jax.ShapeDtypeStruct((len(g) * tokens, features // parts), BF16) for g in groups
        ],
        scratch_shapes=[pltpu.VMEM((blocks, experts * MOST, wide), BF16)],
        compiler_params=params(1),
        cost_estimate=pl.CostEstimate(
            flops=4 * experts * slots * features * units // parts,
            bytes_accessed=4 * experts * features * units // parts,
            transcendentals=0,
        ),
    )(back, gate_grad, up_grad, w_gate, w_up)


def back_matrix(slot):
    places = jnp.arange(MOST, dtype=F32)
    chosen = slot.transpose(1, 2, 0)[..., None] == places
    return chosen.reshape(slot.shape[1], slot.shape[2], -1).astype(BF16)


def weights_kernel(rows, gate_grad, up_grad, *refs):
    grad_gate, grad_up = refs[-2:]
    grad_gate[0] = dot(rows[0], gate_grad[0], TN)
    grad_up[0] = dot(rows[0], up_grad[0], TN)


def weight_grads(rows, gate_grad, up_grad, before, expert, part=0, parts=1):
    experts, slots, features = rows.shape
    units = gate_grad.shape[2]
    wide = FEATURE_TILE
    steps = features // parts // wide
    unit = pl.BlockSpec((1, slots, units), lambda d: (expert, 0, 0))
    out = pl.BlockSpec((1, wide, units), lambda d: (expert, part * steps + d, 0))
    kept = [] if before is None else list(before)
    return pl.pallas_call(
        weights_kernel,
        grid=(steps,),
        in_specs=[
            pl.BlockSpec((1, slots, wide), lambda d: (expert, 0, part * steps + d)), unit, unit
        ]
        + [pl.BlockSpec(memory_space=pl.ANY)] * len(kept),
        out_specs=[out, out],
        out_shape=[jax.ShapeDtypeStruct((experts, features, units), F32)] * 2,
        input_output_aliases={3 + i: i for i in range(len(kept))},
        compiler_params=params(1),
        cost_estimate=pl.CostEstimate(
            flops=4 * slots * features * units // parts,
            bytes_accessed=8 * features * units // parts,
            transcendentals=0,
        ),
    )(rows, gate_grad, up_grad, *kept)


def route_table(routes, gate_values):
    tokens = routes.shape[0]
    experts = jnp.arange(EXPERTS, dtype=jnp.int32)[:, None, None]
    match = routes.T[None] == experts
    member = jnp.any(match, axis=1)
    gate = jnp.sum(jnp.where(match, gate_values.T[None], 0.0), axis=1)
    place = jnp.arange(tokens, dtype=jnp.int32)
    earlier = (place[:, None] < place[None, :]).astype(BF16)
    slot = jnp.where(member, dot(member.astype(BF16), earlier), -1.0)
    return jnp.stack([slot, gate], axis=1)


def flip(value, axis, bit):
    count = lax.axis_size(axis)
    return lax.ppermute(value, axis, [(i, i ^ bit) for i in range(count)])


def swap_order(value, side, pair, dim):
    shape = value.shape
    value = value.reshape(shape[:dim] + (2, 2, shape[dim] // 4) + shape[dim + 1 :])
    value = jnp.where(side == 1, jnp.flip(value, dim), value)
    return jnp.where(pair == 1, jnp.flip(value, dim + 1), value).reshape(shape)


def add(*terms):
    total = terms[0].astype(F32)
    for term in terms[1:]:
        total = total + term.astype(F32)
    return total.astype(BF16)


def quarters(value, count, at):
    return lax.dynamic_slice_in_dim(value, at * (count // 4), count // 4, 0)


def local_near(out_grad, routes, gate_values, layer_input, w_gate, w_up, w_down):
    experts, features, _ = w_gate.shape
    me = lax.axis_index("expert")
    position = lax.axis_index("dp")
    side, pair = position % 2, position // 2 % 2
    tokens = out_grad.shape[0]
    half, quarter = tokens // 2, tokens // 4
    corner = side * 2 + pair

    def fetched(block):
        return jnp.concatenate(
            [quarters(block, tokens, corner), quarters(block, tokens, 3 - corner)], axis=0
        )

    x_mine, g_mine = fetched(layer_input), fetched(out_grad)
    x_mine, g_mine, layer_input, out_grad, routes = lax.optimization_barrier(
        (x_mine, g_mine, layer_input, out_grad, routes)
    )
    table = route_table(routes, gate_values)
    x_sibling, g_sibling = flip(layer_input, "expert", 1), flip(out_grad, "expert", 1)
    x_across, g_across = flip(x_mine, "expert", 2), flip(g_mine, "expert", 2)

    def for_expert(value, owner):
        return lax.dynamic_slice_in_dim(value, owner * experts, experts, 0)

    beside = flip(for_expert(table, me ^ 1), "expert", 1)
    near = jnp.stack([for_expert(table, me), beside], axis=2)
    every = lax.all_gather(table, "expert")
    weights = (w_gate, w_up, w_down)
    x_near, g_near = (layer_input, x_sibling), (out_grad, g_sibling)
    made = slot_grads(x_near, g_near, near[:, 0], near[:, 1], *weights, None, 0, 1, 0, 2)
    x_across, every, near, *made = lax.optimization_barrier((x_across, every, near, *made))
    x_side, x_pair = flip(x_across[:quarter], "dp", 1), flip(x_across[:quarter], "dp", 2)
    made = slot_grads(x_near, g_near, near[:, 0], near[:, 1], *weights, made, 1, experts, 0, 2)
    g_across, *made = lax.optimization_barrier((g_across, *made))
    g_side, g_pair = flip(g_across[:quarter], "dp", 1), flip(g_across[:quarter], "dp", 2)
    far = jnp.stack(
        [
            for_expert(lax.dynamic_index_in_dim(every, me ^ r, 0, keepdims=False), me)
            for r in (2, 3)
        ],
        axis=2,
    )
    slot_back = swap_order(jnp.concatenate([near[:, 0], far[:, 0]], axis=1), side, pair, 2)
    back = back_matrix(slot_back)
    far = swap_order(far, side, pair, 3).reshape(experts, 2, 2, 4, quarter)
    far = jnp.stack([far[:, :, :, q] for q in (0, 3, 2, 1)], axis=3)
    far = far.reshape(experts, 2, 2, tokens)

    x_far = (x_across, x_side, x_pair)
    g_far = (g_across, g_side, g_pair)
    x_far = (*x_far, *(flip(v, "expert", 1) for v in x_far))
    g_far = (*g_far, *(flip(v, "expert", 1) for v in g_far))
    rows, gate_grad, up_grad = slot_grads(
        x_far, g_far, far[:, 0], far[:, 1], *weights, made, 0, experts, 1, 2
    )

    groups = ((0, 2), (1, 3))
    kept_a, sent_a = input_sums(back, gate_grad, up_grad, w_gate, w_up, groups, 0, 2)
    kept_b, sent_b = input_sums(back, gate_grad, up_grad, w_gate, w_up, groups, 1, 2)

    def piece(after, before, expert, part):
        held, rows_now = lax.optimization_barrier((after, rows))
        return held, weight_grads(rows_now, gate_grad, up_grad, before, expert, part, 2)

    chip_a = add(kept_a, flip(sent_a, "expert", 1))
    got = flip(sent_b, "expert", 1)
    chip_b = [add(kept_b[i : i + half], got[i : i + half]) for i in range(0, 2 * tokens, half)]
    (mine_b, other_b, far_mine_b, far_other_b) = chip_b
    other_b = jnp.concatenate([other_b, far_other_b], axis=0)
    far_a = chip_a[tokens:]
    (far_a, other_b), grads = piece((far_a, other_b), None, 0, 0)
    got_a, got_b = flip(far_a, "expert", 2), flip(other_b, "dp", 1)
    got_a, got_b, *grads = lax.optimization_barrier((got_a, got_b, *grads))
    own_a = [add(chip_a[i : i + half], got_a[i : i + half]) for i in (0, half)]
    mine_a, other_a = own_a
    far_mine_b = add(far_mine_b, got_b[half:])
    (other_a, far_mine_b), grads = piece((other_a, far_mine_b), grads, 0, 1)
    got_a, got_y = flip(other_a, "dp", 1), flip(far_mine_b, "expert", 2)
    got_a, got_y, *grads = lax.optimization_barrier((got_a, got_y, *grads))
    mine = jnp.concatenate([add(mine_a, got_a), add(mine_b, got_b[:half], got_y)], axis=1)
    mine = add(mine[:quarter], flip(mine[quarter:], "dp", 2))
    mine, grads = piece(mine, grads, 1, 0)
    got = flip(mine, "dp", 4)
    got, *grads = lax.optimization_barrier((got, *grads))
    mine = add(mine, got)
    mine = jnp.concatenate([mine, flip(mine, "dp", 2)], axis=0)
    mine, grads = piece(mine, grads, 1, 1)
    got = flip(mine, "dp", 1)
    got, *grads = lax.optimization_barrier((got, *grads))
    total = swap_order(jnp.concatenate([mine, got], axis=0), side, pair, 0)
    return (total, *grads)


def local_any(out_grad, routes, gate_values, layer_input, w_gate, w_up, w_down):
    experts = w_gate.shape[0]
    me = lax.axis_index("expert")
    rows_in = lax.all_gather(layer_input, "expert", tiled=True)
    grads_in = lax.all_gather(out_grad, "expert", tiled=True)
    table = lax.all_gather(route_table(routes, gate_values), "expert")
    table = lax.dynamic_slice_in_dim(table, me * experts, experts, 1)
    slot, weight = table[:, :, 0].swapaxes(0, 1), table[:, :, 1].swapaxes(0, 1)
    rows, gate_grad, up_grad = slot_grads(
        [rows_in], [grads_in], slot, weight, w_gate, w_up, w_down, None, 0, experts, 0, 1
    )
    groups = (tuple(range(slot.shape[1])),)
    (sums,) = input_sums(back_matrix(slot), gate_grad, up_grad, w_gate, w_up, groups, 0, 1)
    grads = None
    for l in range(experts):
        grads = weight_grads(rows, gate_grad, up_grad, grads, l)
    own = lax.psum_scatter(sums, "expert", scatter_dimension=0, tiled=True)
    return (lax.psum(own, "dp"), *grads)


def solution(mesh):
    near = mesh.shape["dp"] == 8 and mesh.shape["expert"] == 4
    placed = (
        P("expert", None),
        P("expert", None),
        P("expert", None),
        P("expert", None),
        P("expert", None, "dp"),
        P("expert", None, "dp"),
        P("expert", None, "dp"),
    )
    return jax.shard_map(
        local_near if near else local_any,
        mesh=mesh,
        in_specs=placed,
        out_specs=(P("expert", None), P("expert", None, "dp"), P("expert", None, "dp")),
        check_vma=False,
    )
```

time: 152 us -> 157 us (1.033)
  blocking collectives: 0 us -> 19.7 us
  waiting for transfers between devices: 38.4 us -> 19.8 us
  starting transfers between devices: 28.4 us -> 19.9 us
  Pallas kernels: 79.9 us -> 85.2 us
  local copies, waits for them, and re-layouts: 1.54 us -> 6.73 us
  other arithmetic: 2.22 us -> 4.31 us
    all_gather x0 -> x1, blocking collectives: none -> 19.7 us  [local_near(): every = lax.all_gather(table, 'expert')]
    ppermute x27 -> x25, waiting for transfers between devices: 38.4 us -> 19.8 us  [flip(): return lax.ppermute(value, axis, [(i, i ^ bit) for i in range(count)])]
    pallas_call x2 -> x3, Pallas kernels: 28.6 us -> 40.9 us  [slot_grads(): pl.pallas_call(functools.partial(slots_kernel, len(x_pieces)), grid=(coun...]
    ppermute x27 -> x25, starting transfers between devices: 28.4 us -> 19.9 us  [flip(): return lax.ppermute(value, axis, [(i, i ^ bit) for i in range(count)])]
    pallas_call x4, Pallas kernels: 30.8 us -> 26.5 us  [weight_grads(): pl.pallas_call(weights_kernel, grid=(steps,), in_specs=[pl.BlockSpec((1,...]
    pallas_call x2, Pallas kernels: 20.4 us -> 17.7 us  [input_sums(): pl.pallas_call(functools.partial(inputs_kernel, groups), grid=(steps,), i...]
    unnamed x8 -> x14, local copies, waits for them, and re-layouts: 0.02 us -> 1.75 us
  transfers between devices with their start and end apart: 27 -> 25, of which waited for: 10 -> 12; matrix products, arithmetic and copies ran while one was open for 1% -> 4% of each run, Pallas kernels for 38% -> 36%
where the time goes in v1:
time: 157 us
  Pallas kernels  85.2 us (54%)
  starting transfers between devices  19.9 us (13%)
  waiting for transfers between devices  19.8 us (13%)
  blocking collectives  19.7 us (13%)
  local copies, waits for them, and re-layouts  6.73 us (4%)
  other arithmetic  4.31 us (3%)
    pallas_call x3, Pallas kernels, slot_grads(): pl.pallas_call(functools.partial(slots_kernel, len(x_pieces)), grid=(coun...  40.9 us
    pallas_call x4, Pallas kernels, weight_grads(): pl.pallas_call(weights_kernel, grid=(steps,), in_specs=[pl.BlockSpec((1,...  26.5 us
    ppermute x25, starting transfers between devices, flip(): return lax.ppermute(value, axis, [(i, i ^ bit) for i in range(count)])  19.9 us
    ppermute x25, waiting for transfers between devices, flip(): return lax.ppermute(value, axis, [(i, i ^ bit) for i in range(count)])  19.8 us
    all_gather x1, blocking collectives, local_near(): every = lax.all_gather(table, 'expert')  19.7 us
    pallas_call x2, Pallas kernels, input_sums(): pl.pallas_call(functools.partial(inputs_kernel, groups), grid=(steps,), i...  17.7 us
  transfers between devices with their start and end apart: 25, of which 12 were waited for; matrix products, arithmetic and copies ran while one was open for 4% of the time, Pallas kernels for 36%

profile of v1, /device:TPU:0, one launch (start us, length us, event | category | flops | bytes accessed | tf_op | source)
XLA Modules:
  0.0 156.8 jit_solution(14055703924504408185)
XLA Ops:
  0.7 1.3 constant_dynamic-slice_fusion.3
  2.0 0.8 pad_maximum_fusion.2
  2.8 0.5 collective-permute-start.2
  3.4 0.7 fusion.2
  4.1 0.7 select_reduce_fusion
  5.0 0.5 collective-permute-start.1
  5.4 2.6 %collective-permute-start = (bf16[64,3072]{1,0:T(8,128)(2,1)S(1)}, bf16[64,3072]{1,0:T(8,128)(2,1)S(1)}, u32[]{:S(2)}, u32[]{:S(2)}) collective-permute-start(bf16[64,3072]{1,0:T(8,128)(2,1)S(1)} %pad_maximum_fusion.1), channel_id=1, source_target_pairs={{0,2},{1,3},{2,0},{3,1},{4,6},{5,7},{6,4},{7,5},{8,10},{9,11},{10,... | collective-permute-start | bytes 1179656 | tf_op jit(solution)/shard_map/ppermute | solution.py:214
  8.1 19.7 %all-gather = f32[32,2,128]{2,0,1:T(8,128)} all-gather(f32[8,2,128]{2,0,1:T(8,128)S(1)} %pad_maximum_fusion.7), channel_id=2, replica_groups=mesh['dp'=8,'expert'=4] {'expert'}, dimensions={0}, use_global_device_ids=true | all-gather | bytes 40960 | tf_op jit(solution)/shard_map/all_gather | solution.py:262
  27.8 0.6 eq.53
  28.4 0.8 eq.54
  29.2 0.9 copy-done.2
  30.1 10.9 %shard_map.94 = (bf16[2,320,3072]{2,1,0:T(8,128)(2,1)}, bf16[2,320,1024]{2,1,0:T(8,128)(2,1)}, bf16[2,320,1024]{2,1,0:T(8,128)(2,1)}) custom-call(bf16[128,3072]{1,0:T(8,128)(2,1)S(1)} %copy-done.1, bf16[128,3072]{1,0:T(8,128)(2,1)S(1)} %collective-permute-done.2.refs_1_, bf16[128,3072]{1,0:T(8,128)(2,1)} %refs_2_.1, bf16[128,3072]{1,0:T(8,128)(2,1)} %copy-done.2, ...), custom_call_target="tpu_custom_call" | custom-call | flops 3019898880 | bytes 18874368 | tf_op jit(solution)/shard_map/pallas_call | solution.py:99
  40.9 0.7 slice.97
  41.6 1.8 %collective-permute-start.5 = (bf16[32,3072]{1,0:T(8,128)(2,1)}, bf16[32,3072]{1,0:T(8,128)(2,1)S(1)}, u32[]{:S(2)}, u32[]{:S(2)}) collective-permute-start(bf16[32,3072]{1,0:T(8,128)(2,1)} %slice.97), channel_id=1, source_target_pairs={{0,8},{4,12},{8,0},{12,4},{16,24},{20,28},{24,16},{28,20},{1,9},{5... | collective-permute-start | bytes 589832 | tf_op jit(solution)/shard_map/ppermute | solution.py:214
  43.4 1.5 collective-permute-start.4
  44.9 10.9 %shard_map.95 = (bf16[2,320,3072]{2,1,0:T(8,128)(2,1)}, bf16[2,320,1024]{2,1,0:T(8,128)(2,1)}, bf16[2,320,1024]{2,1,0:T(8,128)(2,1)}) custom-call(bf16[128,3072]{1,0:T(8,128)(2,1)S(1)} %copy-done.1, bf16[128,3072]{1,0:T(8,128)(2,1)S(1)} %collective-permute-done.2.refs_1_, ...), custom_call_target="tpu_custom_call", output_to_operand_aliasing={{0}: (9, {}), {1}: (10, {}), {2}: (11, {})} | custom-call | flops 3019898880 | bytes 18874368 | tf_op jit(solution)/shard_map/pallas_call | solution.py:99
  55.8 0.5 collective-permute-start.11
  56.4 0.3 collective-permute-start.10
  56.7 0.7 constant_dynamic-slice_fusion.1
  58.4 0.6 collective-permute-start.6
  59.1 3.4 %collective-permute-done.11.refs_8_ = bf16[32,3072]{1,0:T(8,128)(2,1)S(1)} collective-permute-done((bf16[32,3072]{1,0:T(8,128)(2,1)S(1)}, bf16[32,3072]{1,0:T(8,128)(2,1)S(1)}, u32[]{:S(2)}, u32[]{:S(2)}) %collective-permute-start.11) | collective-permute-done | bytes 196640 | tf_op jit(solution)/shard_map/ppermute | solution.py:214
  62.6 0.3 collective-permute-start.14
  63.2 0.8 collective-permute-done.7.refs_4_
  64.5 0.7 copy-done.4
  65.4 19.2 %shard_map.96 = (bf16[2,320,3072]{2,1,0:T(8,128)(2,1)}, bf16[2,320,1024]{2,1,0:T(8,128)(2,1)}, bf16[2,320,1024]{2,1,0:T(8,128)(2,1)}) custom-call(bf16[64,3072]{1,0:T(8,128)(2,1)S(1)} %collective-permute-done.refs_0_, bf16[32,3072]{1,0:T(8,128)(2,1)S(1)} %collective-permute-done.4.refs_1_, ...), custom_call_target="tpu_custom_call", output_to_operand_aliasing={{0}: (17, {}), {1}: (18, {}), {2}: (19, {})} | custom-call | flops 6039797760 | bytes 37748736 | tf_op jit(solution)/shard_map/pallas_call | solution.py:99
  84.6 8.8 %shard_map.97 = (bf16[256,1536]{1,0:T(8,128)(2,1)S(1)}, bf16[256,1536]{1,0:T(8,128)(2,1)S(1)}) custom-call(bf16[4,128,160]{2,1,0:T(8,128)(2,1)S(1)} %compare_convert_fusion.back, bf16[2,320,1024]{2,1,0:T(8,128)(2,1)} %get-tuple-element.84.gate_grad, bf16[2,320,1024]{2,1,0:T(8,128)(2,1)} %get-tuple-element.85.up_grad, bf16[2,3072,1024]{2,1,0:T(8,128)(2,1)} %w_gate.3, ...), custom_call_target="tpu_custom_call" | custom-call | flops 4026531840 | bytes 12582912 | tf_op jit(solution)/shard_map/pallas_call | solution.py:143
  93.4 0.3 collective-permute-start.15
  93.7 8.8 %shard_map.98 = (bf16[256,1536]{1,0:T(8,128)(2,1)S(1)}, bf16[256,1536]{1,0:T(8,128)(2,1)S(1)}) custom-call(bf16[4,128,160]{2,1,0:T(8,128)(2,1)S(1)} %compare_convert_fusion.back, bf16[2,320,1024]{2,1,0:T(8,128)(2,1)} %get-tuple-element.84.gate_grad, bf16[2,320,1024]{2,1,0:T(8,128)(2,1)} %get-tuple-element.85.up_grad, bf16[2,3072,1024]{2,1,0:T(8,128)(2,1)} %w_gate.3, ...), custom_call_target="tpu_custom_call" | custom-call | flops 4026531840 | bytes 12582912 | tf_op jit(solution)/shard_map/pallas_call | solution.py:143
  102.6 0.3 collective-permute-start.16
  103.2 1.8 %collective-permute-done.16 = bf16[256,1536]{1,0:T(8,128)(2,1)S(1)} collective-permute-done((bf16[256,1536]{1,0:T(8,128)(2,1)S(1)}, bf16[256,1536]{1,0:T(8,128)(2,1)S(1)}, u32[]{:S(2)}, u32[]{:S(2)}) %collective-permute-start.16) | collective-permute-done | bytes 786464 | tf_op jit(solution)/shard_map/ppermute | solution.py:214
  105.1 1.6 %collective-permute-start.17 = (bf16[128,1536]{1,0:T(8,128)(2,1)S(1)}, bf16[128,1536]{1,0:T(8,128)(2,1)S(1)}, u32[]{:S(2)}, u32[]{:S(2)}) collective-permute-start(bf16[128,1536]{1,0:T(8,128)(2,1)S(1)} %slice.134), channel_id=1, source_target_pairs={{0,2},{1,3},{2,0},{3,1},{4,6},{5,7},{6,4},{7,5},{8,10},{9,11},{10,... | collective-permute-start | bytes 1179656 | tf_op jit(solution)/shard_map/ppermute | solution.py:214
  106.7 0.5 collective-permute-start.18
  107.2 6.6 %shard_map.99 = (f32[2,3072,1024]{2,1,0:T(8,128)}, f32[2,3072,1024]{2,1,0:T(8,128)}) custom-call(bf16[2,320,3072]{2,1,0:T(8,128)(2,1)} %get-tuple-element.115.rows, bf16[2,320,1024]{2,1,0:T(8,128)(2,1)S(1)} %copy-done, bf16[2,320,1024]{2,1,0:T(8,128)(2,1)} %get-tuple-element.85.up_grad), custom_call_target="tpu_custom_call" | custom-call | flops 2013265920 | bytes 12582912 | tf_op jit(solution)/shard_map/pallas_call | solution.py:181
  113.8 2.6 %collective-permute-done.17 = bf16[128,1536]{1,0:T(8,128)(2,1)S(1)} collective-permute-done((bf16[128,1536]{1,0:T(8,128)(2,1)S(1)}, bf16[128,1536]{1,0:T(8,128)(2,1)S(1)}, u32[]{:S(2)}, u32[]{:S(2)}) %collective-permute-start.17) | collective-permute-done | bytes 393248 | tf_op jit(solution)/shard_map/ppermute | solution.py:214
  116.4 1.2 collective-permute-done.18
  117.8 0.6 collective-permute-start.19
  118.4 0.5 collective-permute-start.20
  118.9 6.6 %shard_map.100 = (f32[2,3072,1024]{2,1,0:T(8,128)}, f32[2,3072,1024]{2,1,0:T(8,128)}) custom-call(bf16[2,320,3072]{2,1,0:T(8,128)(2,1)} %get-tuple-element.115.rows, bf16[2,320,1024]{2,1,0:T(8,128)(2,1)S(1)} %copy-done, bf16[2,320,1024]{2,1,0:T(8,128)(2,1)} %get-tuple-element.85.up_grad, ...), custom_call_target="tpu_custom_call", output_to_operand_aliasing={{0}: (3, {}), {1}: (4, {})} | custom-call | flops 2013265920 | bytes 12582912 | tf_op jit(solution)/shard_map/pallas_call | solution.py:181
  125.8 1.5 collective-permute-start.21
  127.3 4.2 %collective-permute-done.21 = bf16[32,3072]{1,0:T(8,128)(2,1)S(1)} collective-permute-done((bf16[32,3072]{1,0:T(8,128)(2,1)S(1)}, bf16[32,3072]{1,0:T(8,128)(2,1)S(1)}, u32[]{:S(2)}, u32[]{:S(2)}) %collective-permute-start.21) | collective-permute-done | bytes 196640 | tf_op jit(solution)/shard_map/ppermute | solution.py:214
  131.6 2.6 %collective-permute-start.22 = (bf16[32,3072]{1,0:T(8,128)(2,1)S(1)}, bf16[32,3072]{1,0:T(8,128)(2,1)S(1)}, u32[]{:S(2)}, u32[]{:S(2)}) collective-permute-start(bf16[32,3072]{1,0:T(8,128)(2,1)S(1)} %add_convert_fusion.2), channel_id=1, source_target_pairs={{0,16},{4,20},{8,24},{12,28},{16,0},{20,4},{24,8},{28,12},{1,17},{... | collective-permute-start | bytes 589832 | tf_op jit(solution)/shard_map/ppermute | solution.py:214
  134.2 6.6 %shard_map.101 = (f32[2,3072,1024]{2,1,0:T(8,128)}, f32[2,3072,1024]{2,1,0:T(8,128)}) custom-call(bf16[2,320,3072]{2,1,0:T(8,128)(2,1)} %get-tuple-element.115.rows, bf16[2,320,1024]{2,1,0:T(8,128)(2,1)S(1)} %copy-done, bf16[2,320,1024]{2,1,0:T(8,128)(2,1)} %get-tuple-element.85.up_grad, ...), custom_call_target="tpu_custom_call", output_to_operand_aliasing={{0}: (3, {}), {1}: (4, {})} | custom-call | flops 2013265920 | bytes 12582912 | tf_op jit(solution)/shard_map/pallas_call | solution.py:181
  141.1 1.3 collective-permute-start.23
  142.4 4.4 %collective-permute-done.23 = bf16[32,3072]{1,0:T(8,128)(2,1)S(1)} collective-permute-done((bf16[32,3072]{1,0:T(8,128)(2,1)S(1)}, bf16[32,3072]{1,0:T(8,128)(2,1)S(1)}, u32[]{:S(2)}, u32[]{:S(2)}) %collective-permute-start.23) | collective-permute-done | bytes 196640 | tf_op jit(solution)/shard_map/ppermute | solution.py:214
  146.9 1.6 %collective-permute-start.24 = (bf16[64,3072]{1,0:T(8,128)(2,1)S(1)}, bf16[64,3072]{1,0:T(8,128)(2,1)S(1)}, u32[]{:S(2)}, u32[]{:S(2)}) collective-permute-start(bf16[64,3072]{1,0:T(8,128)(2,1)S(1)} %pad_maximum_fusion.4), channel_id=1, source_target_pairs={{0,4},{4,0},{8,12},{12,8},{16,20},{20,16},{24,28},{28,24},{1,5},{5... | collective-permute-start | bytes 1179656 | tf_op jit(solution)/shard_map/ppermute | solution.py:214
  148.5 6.6 %shard_map.102 = (f32[2,3072,1024]{2,1,0:T(8,128)}, f32[2,3072,1024]{2,1,0:T(8,128)}) custom-call(bf16[2,320,3072]{2,1,0:T(8,128)(2,1)} %get-tuple-element.115.rows, bf16[2,320,1024]{2,1,0:T(8,128)(2,1)S(1)} %copy-done, bf16[2,320,1024]{2,1,0:T(8,128)(2,1)} %get-tuple-element.85.up_grad, ...), custom_call_target="tpu_custom_call", output_to_operand_aliasing={{0}: (3, {}), {1}: (4, {})} | custom-call | flops 2013265920 | bytes 12582912 | tf_op jit(solution)/shard_map/pallas_call | solution.py:181
  155.1 0.4 collective-permute-done.24
  155.7 1.0 reverse_select_fusion
  (79 shorter events, 3.7 us)
Async XLA Ops:
  0.6 29.4 %copy-start.1 = (bf16[128,3072]{1,0:T(8,128)(2,1)S(1)}, bf16[128,3072]{1,0:T(8,128)(2,1)}, u32[]{:S(2)}) copy-start(bf16[128,3072]{1,0:T(8,128)(2,1)} %refs_0_.1) | copy-start | bytes 2359300
  2.8 26.3 %collective-permute-start.2 = (bf16[128,3072]{1,0:T(8,128)(2,1)}, bf16[128,3072]{1,0:T(8,128)(2,1)S(1)}, u32[]{:S(2)}, u32[]{:S(2)}) collective-permute-start(bf16[128,3072]{1,0:T(8,128)(2,1)} %refs_0_.1), channel_id=1, source_target_pairs={{0,1},{1,0},{2,3},{3,2},{4,5},{5,4},{6,7},{7,6},{8,9},{9,8},{10,11... | collective-permute-start | bytes 2359304 | tf_op jit(solution)/shard_map/ppermute | solution.py:214
  3.3 25.8 %collective-permute-start.3 = (bf16[128,3072]{1,0:T(8,128)(2,1)}, bf16[128,3072]{1,0:T(8,128)(2,1)S(1)}, u32[]{:S(2)}, u32[]{:S(2)}) collective-permute-start(bf16[128,3072]{1,0:T(8,128)(2,1)} %refs_2_.1), channel_id=1, source_target_pairs={{0,1},{1,0},{2,3},{3,2},{4,5},{5,4},{6,7},{7,6},{8,9},{9,8},{10,11... | collective-permute-start | bytes 2359304 | tf_op jit(solution)/shard_map/ppermute | solution.py:214
  5.0 24.2 %collective-permute-start.1 = (f32[2,2,128]{2,0,1:T(2,128)S(1)}, f32[2,2,128]{2,0,1:T(2,128)S(1)}, u32[]{:S(2)}, u32[]{:S(2)}) collective-permute-start(f32[2,2,128]{2,0,1:T(2,128)S(1)} %get-tuple-element.136), channel_id=1, source_target_pairs={{0,1},{1,0},{2,3},{3,2},{4,5},{5,4},{6,7},{7,6},{8,9},{9,8},{10,11... | collective-permute-start | bytes 6152 | tf_op jit(solution)/shard_map/ppermute | solution.py:214
  5.4 35.5 %collective-permute-start = (bf16[64,3072]{1,0:T(8,128)(2,1)S(1)}, bf16[64,3072]{1,0:T(8,128)(2,1)S(1)}, u32[]{:S(2)}, u32[]{:S(2)}) collective-permute-start(bf16[64,3072]{1,0:T(8,128)(2,1)S(1)} %pad_maximum_fusion.1), channel_id=1, source_target_pairs={{0,2},{1,3},{2,0},{3,1},{4,6},{5,7},{6,4},{7,5},{8,10},{9,11},{10,... | collective-permute-start | bytes 1179656 | tf_op jit(solution)/shard_map/ppermute | solution.py:214
  8.0 47.8 %collective-permute-start.9 = (bf16[64,3072]{1,0:T(8,128)(2,1)}, bf16[64,3072]{1,0:T(8,128)(2,1)S(1)}, u32[]{:S(2)}, u32[]{:S(2)}) collective-permute-start(bf16[64,3072]{1,0:T(8,128)(2,1)} %pad_maximum_fusion.2), channel_id=1, source_target_pairs={{0,2},{1,3},{2,0},{3,1},{4,6},{5,7},{6,4},{7,5},{8,10},{9,11},{10,... | collective-permute-start | bytes 1179656 | tf_op jit(solution)/shard_map/ppermute | solution.py:214
  29.2 0.9 copy-start.2
  41.6 16.8 %collective-permute-start.5 = (bf16[32,3072]{1,0:T(8,128)(2,1)}, bf16[32,3072]{1,0:T(8,128)(2,1)S(1)}, u32[]{:S(2)}, u32[]{:S(2)}) collective-permute-start(bf16[32,3072]{1,0:T(8,128)(2,1)} %slice.97), channel_id=1, source_target_pairs={{0,8},{4,12},{8,0},{12,4},{16,24},{20,28},{24,16},{28,20},{1,9},{5... | collective-permute-start | bytes 589832 | tf_op jit(solution)/shard_map/ppermute | solution.py:214
  43.4 15.5 %collective-permute-start.4 = (bf16[32,3072]{1,0:T(8,128)(2,1)}, bf16[32,3072]{1,0:T(8,128)(2,1)S(1)}, u32[]{:S(2)}, u32[]{:S(2)}) collective-permute-start(bf16[32,3072]{1,0:T(8,128)(2,1)} %slice.97), channel_id=1, source_target_pairs={{0,4},{4,0},{8,12},{12,8},{16,20},{20,16},{24,28},{28,24},{1,5},{5... | collective-permute-start | bytes 589832 | tf_op jit(solution)/shard_map/ppermute | solution.py:214
  55.8 8.7 %copy-start.3 = (bf16[64,3072]{1,0:T(8,128)(2,1)}, bf16[64,3072]{1,0:T(8,128)(2,1)S(1)}, u32[]{:S(2)}) copy-start(bf16[64,3072]{1,0:T(8,128)(2,1)S(1)} %collective-permute-done.9.refs_6_) | copy-start | bytes 1179652
  55.8 6.6 %collective-permute-start.11 = (bf16[32,3072]{1,0:T(8,128)(2,1)S(1)}, bf16[32,3072]{1,0:T(8,128)(2,1)S(1)}, u32[]{:S(2)}, u32[]{:S(2)}) collective-permute-start(bf16[32,3072]{1,0:T(8,128)(2,1)S(1)} %slice.99), channel_id=1, source_target_pairs={{0,8},{4,12},{8,0},{12,4},{16,24},{20,28},{24,16},{28,20},{1,9},{5... | collective-permute-start | bytes 589832 | tf_op jit(solution)/shard_map/ppermute | solution.py:214
  56.4 6.3 %collective-permute-start.10 = (bf16[32,3072]{1,0:T(8,128)(2,1)S(1)}, bf16[32,3072]{1,0:T(8,128)(2,1)S(1)}, u32[]{:S(2)}, u32[]{:S(2)}) collective-permute-start(bf16[32,3072]{1,0:T(8,128)(2,1)S(1)} %slice.99), channel_id=1, source_target_pairs={{0,4},{4,0},{8,12},{12,8},{16,20},{20,16},{24,28},{28,24},{1,5},{5... | collective-permute-start | bytes 589832 | tf_op jit(solution)/shard_map/ppermute | solution.py:214
  56.7 7.8 %collective-permute-start.12 = (bf16[64,3072]{1,0:T(8,128)(2,1)S(1)}, bf16[64,3072]{1,0:T(8,128)(2,1)S(1)}, u32[]{:S(2)}, u32[]{:S(2)}) collective-permute-start(bf16[64,3072]{1,0:T(8,128)(2,1)S(1)} %collective-permute-done.9.refs_6_), channel_id=1, source_target_pairs={{0,1},{1,0},{2,3},{3,2},{4,5},{5,4},{6,7},{7,6},{8,9},{9,8},{10,11... | collective-permute-start | bytes 1179656 | tf_op jit(solution)/shard_map/ppermute | solution.py:214
  58.4 6.1 %collective-permute-start.6 = (bf16[64,3072]{1,0:T(8,128)(2,1)S(1)}, bf16[64,3072]{1,0:T(8,128)(2,1)S(1)}, u32[]{:S(2)}, u32[]{:S(2)}) collective-permute-start(bf16[64,3072]{1,0:T(8,128)(2,1)S(1)} %collective-permute-done.refs_0_), channel_id=1, source_target_pairs={{0,1},{1,0},{2,3},{3,2},{4,5},{5,4},{6,7},{7,6},{8,9},{9,8},{10,11... | collective-permute-start | bytes 1179656 | tf_op jit(solution)/shard_map/ppermute | solution.py:214
  59.0 4.0 %collective-permute-start.8 = (bf16[32,3072]{1,0:T(8,128)(2,1)S(1)}, bf16[32,3072]{1,0:T(8,128)(2,1)S(1)}, u32[]{:S(2)}, u32[]{:S(2)}) collective-permute-start(bf16[32,3072]{1,0:T(8,128)(2,1)S(1)} %collective-permute-done.5.refs_2_), channel_id=1, source_target_pairs={{0,1},{1,0},{2,3},{3,2},{4,5},{5,4},{6,7},{7,6},{8,9},{9,8},{10,11... | collective-permute-start | bytes 589832 | tf_op jit(solution)/shard_map/ppermute | solution.py:214
  62.5 1.4 collective-permute-start.7
  62.6 1.6 collective-permute-start.14
  63.0 1.5 collective-permute-start.13
  64.5 0.8 copy-start.4
  64.5 0.9 copy-start.5
  93.4 9.5 %collective-permute-start.15 = (bf16[256,1536]{1,0:T(8,128)(2,1)S(1)}, bf16[256,1536]{1,0:T(8,128)(2,1)S(1)}, u32[]{:S(2)}, u32[]{:S(2)}) collective-permute-start(bf16[256,1536]{1,0:T(8,128)(2,1)S(1)} %get-tuple-element.87), channel_id=1, source_target_pairs={{0,1},{1,0},{2,3},{3,2},{4,5},{5,4},{6,7},{7,6},{8,9},{9,8},{10,11... | collective-permute-start | bytes 2359304 | tf_op jit(solution)/shard_map/ppermute | solution.py:214
  102.6 4.6 %copy-start = (bf16[2,320,1024]{2,1,0:T(8,128)(2,1)S(1)}, bf16[2,320,1024]{2,1,0:T(8,128)(2,1)}, u32[]{:S(2)}) copy-start(bf16[2,320,1024]{2,1,0:T(8,128)(2,1)} %get-tuple-element.84.gate_grad) | copy-start | bytes 3932164
  102.6 2.4 %collective-permute-start.16 = (bf16[256,1536]{1,0:T(8,128)(2,1)S(1)}, bf16[256,1536]{1,0:T(8,128)(2,1)S(1)}, u32[]{:S(2)}, u32[]{:S(2)}) collective-permute-start(bf16[256,1536]{1,0:T(8,128)(2,1)S(1)} %get-tuple-element.89), channel_id=1, source_target_pairs={{0,1},{1,0},{2,3},{3,2},{4,5},{5,4},{6,7},{7,6},{8,9},{9,8},{10,11... | collective-permute-start | bytes 2359304 | tf_op jit(solution)/shard_map/ppermute | solution.py:214
  105.1 11.4 %collective-permute-start.17 = (bf16[128,1536]{1,0:T(8,128)(2,1)S(1)}, bf16[128,1536]{1,0:T(8,128)(2,1)S(1)}, u32[]{:S(2)}, u32[]{:S(2)}) collective-permute-start(bf16[128,1536]{1,0:T(8,128)(2,1)S(1)} %slice.134), channel_id=1, source_target_pairs={{0,2},{1,3},{2,0},{3,1},{4,6},{5,7},{6,4},{7,5},{8,10},{9,11},{10,... | collective-permute-start | bytes 1179656 | tf_op jit(solution)/shard_map/ppermute | solution.py:214
  106.7 11.0 %collective-permute-start.18 = (bf16[128,1536]{1,0:T(8,128)(2,1)S(1)}, bf16[128,1536]{1,0:T(8,128)(2,1)S(1)}, u32[]{:S(2)}, u32[]{:S(2)}) collective-permute-start(bf16[128,1536]{1,0:T(8,128)(2,1)S(1)} %pad_maximum_fusion.3), channel_id=1, source_target_pairs={{0,4},{4,0},{8,12},{12,8},{16,20},{20,16},{24,28},{28,24},{1,5},{5... | collective-permute-start | bytes 1179656 | tf_op jit(solution)/shard_map/ppermute | solution.py:214
  117.8 7.7 %collective-permute-start.19 = (bf16[64,1536]{1,0:T(8,128)(2,1)S(1)}, bf16[64,1536]{1,0:T(8,128)(2,1)S(1)}, u32[]{:S(2)}, u32[]{:S(2)}) collective-permute-start(bf16[64,1536]{1,0:T(8,128)(2,1)S(1)} %add_convert_fusion.8), channel_id=1, source_target_pairs={{0,4},{4,0},{8,12},{12,8},{16,20},{20,16},{24,28},{28,24},{1,5},{5... | collective-permute-start | bytes 589832 | tf_op jit(solution)/shard_map/ppermute | solution.py:214
  118.4 7.1 %collective-permute-start.20 = (bf16[64,1536]{1,0:T(8,128)(2,1)S(1)}, bf16[64,1536]{1,0:T(8,128)(2,1)S(1)}, u32[]{:S(2)}, u32[]{:S(2)}) collective-permute-start(bf16[64,1536]{1,0:T(8,128)(2,1)S(1)} %add_convert_fusion.6), channel_id=1, source_target_pairs={{0,2},{1,3},{2,0},{3,1},{4,6},{5,7},{6,4},{7,5},{8,10},{9,11},{10,... | collective-permute-start | bytes 589832 | tf_op jit(solution)/shard_map/ppermute | solution.py:214
  125.8 5.7 %collective-permute-start.21 = (bf16[32,3072]{1,0:T(8,128)(2,1)S(1)}, bf16[32,3072]{1,0:T(8,128)(2,1)S(1)}, u32[]{:S(2)}, u32[]{:S(2)}) collective-permute-start(bf16[32,3072]{1,0:T(8,128)(2,1)S(1)} %pad_maximum_fusion.5), channel_id=1, source_target_pairs={{0,8},{4,12},{8,0},{12,4},{16,24},{20,28},{24,16},{28,20},{1,9},{5... | collective-permute-start | bytes 589832 | tf_op jit(solution)/shard_map/ppermute | solution.py:214
  131.6 9.5 %collective-permute-start.22 = (bf16[32,3072]{1,0:T(8,128)(2,1)S(1)}, bf16[32,3072]{1,0:T(8,128)(2,1)S(1)}, u32[]{:S(2)}, u32[]{:S(2)}) collective-permute-start(bf16[32,3072]{1,0:T(8,128)(2,1)S(1)} %add_convert_fusion.2), channel_id=1, source_target_pairs={{0,16},{4,20},{8,24},{12,28},{16,0},{20,4},{24,8},{28,12},{1,17},{... | collective-permute-start | bytes 589832 | tf_op jit(solution)/shard_map/ppermute | solution.py:214
  141.1 5.7 %collective-permute-start.23 = (bf16[32,3072]{1,0:T(8,128)(2,1)S(1)}, bf16[32,3072]{1,0:T(8,128)(2,1)S(1)}, u32[]{:S(2)}, u32[]{:S(2)}) collective-permute-start(bf16[32,3072]{1,0:T(8,128)(2,1)S(1)} %add_convert_fusion.1), channel_id=1, source_target_pairs={{0,8},{4,12},{8,0},{12,4},{16,24},{20,28},{24,16},{28,20},{1,9},{5... | collective-permute-start | bytes 589832 | tf_op jit(solution)/shard_map/ppermute | solution.py:214
  146.9 8.6 %collective-permute-start.24 = (bf16[64,3072]{1,0:T(8,128)(2,1)S(1)}, bf16[64,3072]{1,0:T(8,128)(2,1)S(1)}, u32[]{:S(2)}, u32[]{:S(2)}) collective-permute-start(bf16[64,3072]{1,0:T(8,128)(2,1)S(1)} %pad_maximum_fusion.4), channel_id=1, source_target_pairs={{0,4},{4,0},{8,12},{12,8},{16,20},{20,16},{24,28},{28,24},{1,5},{5... | collective-permute-start | bytes 1179656 | tf_op jit(solution)/shard_map/ppermute | solution.py:214

commit v2 on v1

--- a/solution.py
+++ b/solution.py
@@ -40,11 +40,10 @@
     return slots == slot_row.astype(jnp.int32)
 
 
-def gather_block(held, pieces, block):
-    tokens = held.shape[0]
-    first, at = block * tokens, 0
+def lay_out(held, pieces, first):
+    rows, at = held.shape[0], 0
     for piece in pieces:
-        low, high = max(first, at), min(first + tokens, at + piece.shape[0])
+        low, high = max(first, at), min(first + rows, at + piece.shape[0])
         if low < high:
             held[low - first : high - first] = piece[low - at : high - at]
         at += piece.shape[0]
@@ -58,67 +57,88 @@
 def slots_kernel(count, *refs):
     x_pieces, g_pieces = refs[:count], refs[count : 2 * count]
     slot, weight, w_gate, w_up, w_down = refs[2 * count : 2 * count + 5]
-    rows, gate_grad, up_grad, held, grads = refs[-5:]
-    blocks = slot.shape[1]
-
-    @pl.when(pl.program_id(1) == 0)
+    rows, gate_grad, up_grad, held, chosen, grads = refs[-6:]
+    experts, blocks, tokens = slot.shape
+    group = held.shape[0] // tokens
+    expert = pl.program_id(0)
+
+    @pl.when((expert == 0) & (pl.program_id(1) == 0))
     def _():
-        for b in range(blocks):
-            mask = one_hot(slot[0, b : b + 1, :])
-            scale = jnp.sum(
-                jnp.where(mask, weight[0, b : b + 1, :], 0.0), axis=1, keepdims=True
-            )
-            chosen = mask.astype(BF16)
-            span = slice(b * MOST, (b + 1) * MOST)
-            gather_block(held, x_pieces, b)
-            for cols in column_chunks(held.shape[1]):
-                rows[0, span, cols] = dot(chosen, held[:, cols]).astype(BF16)
-            gather_block(held, g_pieces, b)
-            for cols in column_chunks(held.shape[1]):
-                grads[span, cols] = (dot(chosen, held[:, cols]) * scale).astype(BF16)
-
-    gate = dot(rows[0], w_gate[0])
-    up = dot(rows[0], w_up[0])
-    hidden = dot(grads[...], w_down[0])
+        for start in range(0, blocks, group):
+            chosen[...] = jnp.zeros_like(chosen)
+            scales = []
+            places = [(l, b) for l in range(experts) for b in range(group)]
+            for i, (l, b) in enumerate(places):
+                at = slice(start + b, start + b + 1)
+                mask = one_hot(slot[l, at, :])
+                chosen[i * MOST : (i + 1) * MOST, b * tokens : (b + 1) * tokens] = mask.astype(BF16)
+                scales.append(
+                    jnp.sum(jnp.where(mask, weight[l, at, :], 0.0), axis=1, keepdims=True)
+                )
+            for pieces, out in ((x_pieces, rows), (g_pieces, grads)):
+                lay_out(held, pieces, start * tokens)
+                for cols in column_chunks(held.shape[1]):
+                    taken = dot(chosen[...], held[:, cols])
+                    for i, (l, b) in enumerate(places):
+                        part = taken[i * MOST : (i + 1) * MOST]
+                        if out is grads:
+                            part = part * scales[i]
+                        span = slice((start + b) * MOST, (start + b + 1) * MOST)
+                        out[l, span, cols] = part.astype(BF16)
+
+    x = rows[expert]
+    gate = dot(x, w_gate[0])
+    up = dot(x, w_up[0])
+    hidden = dot(grads[expert], w_down[0])
     sig = jax.nn.sigmoid(gate)
     up_grad[0] = (hidden * (gate * sig)).astype(BF16)
     gate_grad[0] = (hidden * up * sig * (1.0 + gate * (1.0 - sig))).astype(BF16)
 
 
-def slot_grads(x_pieces, g_pieces, slot, weight, w_gate, w_up, w_down, before, first, last, part, parts):
+def slot_grads(x_pieces, g_pieces, table, weights, before, first, last, part, parts, share=(0, 1)):
+    slot, weight = table[:, 0], table[:, 1]
     experts, blocks, tokens = slot.shape
-    _, features, units = w_gate.shape
+    _, features, units = weights[0].shape
     tile = min(UNIT_TILE, units)
+    tiles = units // tile // share[1]
+    skip = share[0] * tiles
     slots = blocks * MOST
     count = last - first
-    table = pl.BlockSpec((1, blocks, tokens), lambda l, f: (first + l, 0, 0))
-    matrix = pl.BlockSpec((1, features, tile), lambda l, f: (first + l, 0, f))
-    unit = pl.BlockSpec((1, slots, tile), lambda l, f: (first + l, part, f))
+    group = 2 if blocks % 2 == 0 else 1
+    routes = pl.BlockSpec((count, blocks, tokens), lambda l, f: (first // count, 0, 0))
+    matrix = pl.BlockSpec((1, features, tile), lambda l, f: (first + l, 0, skip + f))
+    unit = pl.BlockSpec((1, slots, tile), lambda l, f: (first + l, part, skip + f))
     pieces = [*x_pieces, *g_pieces]
     kept = [] if before is None else list(before)
     return pl.pallas_call(
         functools.partial(slots_kernel, len(x_pieces)),
-        grid=(count, units // tile),
+        grid=(count, tiles),
         in_specs=[whole(p.shape) for p in pieces]
-        + [table, table, matrix, matrix, matrix]
+        + [routes, routes, matrix, matrix, matrix]
         + [pl.BlockSpec(memory_space=pl.ANY)] * len(kept),
         out_specs=[
-            pl.BlockSpec((1, slots, features), lambda l, f: (first + l, part, 0)), unit, unit
+            pl.BlockSpec((count, slots, features), lambda l, f: (first // count, part, 0)),
+            unit,
+            unit,
         ],
         out_shape=[
             jax.ShapeDtypeStruct((experts, parts * slots, features), BF16),
             jax.ShapeDtypeStruct((experts, parts * slots, units), BF16),
             jax.ShapeDtypeStruct((experts, parts * slots, units), BF16),
         ],
-        scratch_shapes=[pltpu.VMEM((tokens, features), BF16), pltpu.VMEM((slots, features), BF16)],
+        scratch_shapes=[
+            pltpu.VMEM((group * tokens, features), BF16),
+            pltpu.VMEM((count * group * MOST, group * tokens), BF16),
+            pltpu.VMEM((count, slots, features), BF16),
+        ],
         input_output_aliases={len(pieces) + 5 + i: i for i in range(len(kept))},
         compiler_params=params(2),
         cost_estimate=pl.CostEstimate(
-            flops=6 * count * slots * features * units,
-            bytes_accessed=6 * count * features * units,
-            transcendentals=count * slots * units,
+            flops=6 * count * slots * features * tiles * tile,
+            bytes_accessed=6 * count * features * tiles * tile,
+            transcendentals=count * slots * tiles * tile,
         ),
-    )(*pieces, slot, weight, w_gate, w_up, w_down, *kept)
+    )(*pieces, slot, weight, *weights, *kept)
 
 
 def inputs_kernel(groups, back, gate_grad, up_grad, w_gate, w_up, *refs):
@@ -251,78 +271,72 @@
         (x_mine, g_mine, layer_input, out_grad, routes)
     )
     table = route_table(routes, gate_values)
+    tables = []
+    for r in range(4):
+        part = lax.dynamic_slice_in_dim(table, (me ^ r) * experts, experts, 0)
+        tables.append(flip(part, "expert", r) if r > 0 else part)
+    x_across, g_across = flip(x_mine, "expert", 2), flip(g_mine, "expert", 2)
     x_sibling, g_sibling = flip(layer_input, "expert", 1), flip(out_grad, "expert", 1)
-    x_across, g_across = flip(x_mine, "expert", 2), flip(g_mine, "expert", 2)
-
-    def for_expert(value, owner):
-        return lax.dynamic_slice_in_dim(value, owner * experts, experts, 0)
-
-    beside = flip(for_expert(table, me ^ 1), "expert", 1)
-    near = jnp.stack([for_expert(table, me), beside], axis=2)
-    every = lax.all_gather(table, "expert")
+
+    def onward(across):
+        here = (across, flip(across[:quarter], "dp", 1), flip(across[:quarter], "dp", 2))
+        return (*here, *(flip(v, "expert", 1) for v in here))
+
     weights = (w_gate, w_up, w_down)
-    x_near, g_near = (layer_input, x_sibling), (out_grad, g_sibling)
-    made = slot_grads(x_near, g_near, near[:, 0], near[:, 1], *weights, None, 0, 1, 0, 2)
-    x_across, every, near, *made = lax.optimization_barrier((x_across, every, near, *made))
-    x_side, x_pair = flip(x_across[:quarter], "dp", 1), flip(x_across[:quarter], "dp", 2)
-    made = slot_grads(x_near, g_near, near[:, 0], near[:, 1], *weights, made, 1, experts, 0, 2)
+    near = jnp.stack(tables[:2], axis=2)
+    near_rows = ((layer_input, x_sibling), (out_grad, g_sibling), near, weights)
+    made = slot_grads(*near_rows, None, 0, 1, 0, 2)
+    x_across, tables[2], tables[3], *made = lax.optimization_barrier(
+        (x_across, tables[2], tables[3], *made)
+    )
+    x_far = onward(x_across)
+    made = slot_grads(*near_rows, made, 1, 2, 0, 2, (0, 2))
     g_across, *made = lax.optimization_barrier((g_across, *made))
-    g_side, g_pair = flip(g_across[:quarter], "dp", 1), flip(g_across[:quarter], "dp", 2)
-    far = jnp.stack(
-        [
-            for_expert(lax.dynamic_index_in_dim(every, me ^ r, 0, keepdims=False), me)
-            for r in (2, 3)
-        ],
-        axis=2,
-    )
-    slot_back = swap_order(jnp.concatenate([near[:, 0], far[:, 0]], axis=1), side, pair, 2)
-    back = back_matrix(slot_back)
+    g_far = onward(g_across)
+    made = slot_grads(*near_rows, made, 1, 2, 0, 2, (1, 2))
+    far = jnp.stack(tables[2:], axis=2)
+    slot_back = jnp.concatenate([near[:, 0], far[:, 0]], axis=1)
+    back = back_matrix(swap_order(slot_back, side, pair, 2))
     far = swap_order(far, side, pair, 3).reshape(experts, 2, 2, 4, quarter)
     far = jnp.stack([far[:, :, :, q] for q in (0, 3, 2, 1)], axis=3)
     far = far.reshape(experts, 2, 2, tokens)
-
-    x_far = (x_across, x_side, x_pair)
-    g_far = (g_across, g_side, g_pair)
-    x_far = (*x_far, *(flip(v, "expert", 1) for v in x_far))
-    g_far = (*g_far, *(flip(v, "expert", 1) for v in g_far))
-    rows, gate_grad, up_grad = slot_grads(
-        x_far, g_far, far[:, 0], far[:, 1], *weights, made, 0, experts, 1, 2
-    )
+    rows, gate_grad, up_grad = slot_grads(x_far, g_far, far, weights, made, 0, experts, 1, 2)
 
     groups = ((0, 2), (1, 3))
     kept_a, sent_a = input_sums(back, gate_grad, up_grad, w_gate, w_up, groups, 0, 2)
     kept_b, sent_b = input_sums(back, gate_grad, up_grad, w_gate, w_up, groups, 1, 2)
 
-    def piece(after, before, expert, part):
+    def piece(after, before, *which):
         held, rows_now = lax.optimization_barrier((after, rows))
-        return held, weight_grads(rows_now, gate_grad, up_grad, before, expert, part, 2)
+        return held, weight_grads(rows_now, gate_grad, up_grad, before, *which)
+
+    def corners(value):
+        return [flip(v, "dp", step) for v, step in zip(value, (2, 1, 3))]
+
+    def cut(value, count):
+        return [value[i : i + quarter] for i in range(0, count * quarter, quarter)]
 
     chip_a = add(kept_a, flip(sent_a, "expert", 1))
     got = flip(sent_b, "expert", 1)
-    chip_b = [add(kept_b[i : i + half], got[i : i + half]) for i in range(0, 2 * tokens, half)]
-    (mine_b, other_b, far_mine_b, far_other_b) = chip_b
-    other_b = jnp.concatenate([other_b, far_other_b], axis=0)
+    chip_b = [add(a, b) for a, b in zip(cut(kept_b, 8), cut(got, 8))]
     far_a = chip_a[tokens:]
-    (far_a, other_b), grads = piece((far_a, other_b), None, 0, 0)
-    got_a, got_b = flip(far_a, "expert", 2), flip(other_b, "dp", 1)
+    away = [jnp.concatenate([chip_b[q], chip_b[4 + q]], axis=0) for q in (1, 2, 3)]
+    (far_a, *away), grads = piece((far_a, *away), None, 0)
+    got_a, got_b = flip(far_a, "expert", 2), corners(away)
     got_a, got_b, *grads = lax.optimization_barrier((got_a, got_b, *grads))
-    own_a = [add(chip_a[i : i + half], got_a[i : i + half]) for i in (0, half)]
-    mine_a, other_a = own_a
-    far_mine_b = add(far_mine_b, got_b[half:])
-    (other_a, far_mine_b), grads = piece((other_a, far_mine_b), grads, 0, 1)
-    got_a, got_y = flip(other_a, "dp", 1), flip(far_mine_b, "expert", 2)
-    got_a, got_y, *grads = lax.optimization_barrier((got_a, got_y, *grads))
-    mine = jnp.concatenate([add(mine_a, got_a), add(mine_b, got_b[:half], got_y)], axis=1)
-    mine = add(mine[:quarter], flip(mine[quarter:], "dp", 2))
-    mine, grads = piece(mine, grads, 1, 0)
+    own_a = [add(a, b) for a, b in zip(cut(chip_a, 4), cut(got_a, 4))]
+    mine_b = add(chip_b[0], *(v[:quarter] for v in got_b))
+    far_b = add(chip_b[4], *(v[quarter:] for v in got_b))
+    got_a, got_b = corners(own_a[1:]), flip(far_b, "expert", 2)
+    mine = jnp.concatenate([add(own_a[0], *got_a), add(mine_b, got_b)], axis=1)
+    mine, grads = piece(mine, grads, 1, 0, 2)
     got = flip(mine, "dp", 4)
     got, *grads = lax.optimization_barrier((got, *grads))
     mine = add(mine, got)
-    mine = jnp.concatenate([mine, flip(mine, "dp", 2)], axis=0)
-    mine, grads = piece(mine, grads, 1, 1)
-    got = flip(mine, "dp", 1)
+    mine, grads = piece(mine, grads, 1, 1, 2)
+    got = corners([mine] * 3)
     got, *grads = lax.optimization_barrier((got, *grads))
-    total = swap_order(jnp.concatenate([mine, got], axis=0), side, pair, 0)
+    total = swap_order(jnp.concatenate([mine, *got], axis=0), side, pair, 0)
     return (total, *grads)
 
 
@@ -332,11 +346,11 @@
     rows_in = lax.all_gather(layer_input, "expert", tiled=True)
     grads_in = lax.all_gather(out_grad, "expert", tiled=True)
     table = lax.all_gather(route_table(routes, gate_values), "expert")
-    table = lax.dynamic_slice_in_dim(table, me * experts, experts, 1)
-    slot, weight = table[:, :, 0].swapaxes(0, 1), table[:, :, 1].swapaxes(0, 1)
+    table = lax.dynamic_slice_in_dim(table, me * experts, experts, 1).transpose(1, 2, 0, 3)
     rows, gate_grad, up_grad = slot_grads(
-        [rows_in], [grads_in], slot, weight, w_gate, w_up, w_down, None, 0, experts, 0, 1
-    )
+        [rows_in], [grads_in], table, (w_gate, w_up, w_down), None, 0, experts, 0, 1
+    )
+    slot = table[:, 0]
     groups = (tuple(range(slot.shape[1])),)
     (sums,) = input_sums(back_matrix(slot), gate_grad, up_grad, w_gate, w_up, groups, 0, 1)
     grads = None

time: 157 us -> 137 us (0.87)
  blocking collectives: 19.7 us -> 0 us
  waiting for transfers between devices: 19.8 us -> 8.82 us
  starting transfers between devices: 19.9 us -> 27.7 us
  local copies, waits for them, and re-layouts: 6.73 us -> 10.3 us
    all_gather x1 -> x0, blocking collectives: 19.7 us -> none  [local_near(): every = lax.all_gather(table, 'expert')]
    ppermute x25 -> x31, waiting for transfers between devices: 19.8 us -> 8.82 us  [flip(): return lax.ppermute(value, axis, [(i, i ^ bit) for i in range(count)])]
    ppermute x25 -> x31, starting transfers between devices: 19.9 us -> 27.7 us  [flip(): return lax.ppermute(value, axis, [(i, i ^ bit) for i in range(count)])]
    pallas_call x4 -> x3, Pallas kernels: 26.5 us -> 23.9 us  [weight_grads(): pl.pallas_call(weights_kernel, grid=(steps,), in_specs=[pl.BlockSpec((1,...]
    pallas_call x3 -> x4, Pallas kernels: 40.9 us -> 43.4 us  [slot_grads(): pl.pallas_call(functools.partial(slots_kernel, len(x_pieces)), grid=(coun...]
    slice x2, local copies, waits for them, and re-layouts: 0.71 us -> 2.31 us  [onward(): across[:quarter]]
  transfers between devices with their start and end apart: 25 -> 31, of which waited for: 12 -> 11; matrix products, arithmetic and copies ran while one was open for 4% -> 8% of each run, Pallas kernels for 36% -> 42%
where the time goes in v2:
time: 137 us; the launch traced here: 136 us
  Pallas kernels  85 us (62%)
  starting transfers between devices  27.7 us (20%)
  local copies, waits for them, and re-layouts  10.3 us (8%)
  waiting for transfers between devices  8.82 us (6%)
  other arithmetic  3.41 us (2%)
    pallas_call x4, Pallas kernels, slot_grads(): pl.pallas_call(functools.partial(slots_kernel, len(x_pieces)), grid=(coun...  43.4 us
    ppermute x31, starting transfers between devices, flip(): return lax.ppermute(value, axis, [(i, i ^ bit) for i in range(count)])  27.7 us
    pallas_call x3, Pallas kernels, weight_grads(): pl.pallas_call(weights_kernel, grid=(steps,), in_specs=[pl.BlockSpec((1,...  23.9 us
    pallas_call x2, Pallas kernels, input_sums(): pl.pallas_call(functools.partial(inputs_kernel, groups), grid=(steps,), i...  17.7 us
    ppermute x31, waiting for transfers between devices, flip(): return lax.ppermute(value, axis, [(i, i ^ bit) for i in range(count)])  8.82 us
  transfers between devices with their start and end apart: 31, of which 11 were waited for; matrix products, arithmetic and copies ran while one was open for 8% of the time, Pallas kernels for 42%

profile of v2, /device:TPU:0, one launch (start us, length us, event | category | flops | bytes accessed | tf_op | source)
XLA Modules:
  0.0 136.4 jit_solution(5497683811052038620)
XLA Ops:
  0.7 1.4 %constant_dynamic-slice_fusion.1 = (bf16[32,3072]{1,0:T(8,128)(2,1)S(1)}, bf16[32,3072]{1,0:T(8,128)(2,1)S(1)}, bf16[32,3072]{1,0:T(8,128)(2,1)S(1)}, bf16[32,3072]{1,0:T(8,128)(2,1)S(1)}) fusion(bf16[128,3072]{1,0:T(8,128)(2,1)} %refs_2_.2, s32[]{:T(128)S(6)} %select_n.92, s32[]{:T(128)S(6)} %select_n.93, bf16[128,3072]{1,0:T(8,128)(2,1)} %refs_0_.2), kind=kLoop, calls=%fused_computation.55 | loop fusion | bytes 1572872 | tf_op jit(solution)/shard_map/dynamic_slice | solution.py:252
  2.2 0.5 collective-permute-start.4
  3.0 0.6 fusion.3
  4.0 2.6 %collective-permute-start.3 = (f32[2,2,128]{2,0,1:T(2,128)}, f32[2,2,128]{2,0,1:T(2,128)}, u32[]{:S(2)}, u32[]{:S(2)}) collective-permute-start(f32[2,2,128]{2,0,1:T(2,128)} %get-tuple-element.140), channel_id=1, source_target_pairs={{0,3},{1,2},{2,1},{3,0},{4,7},{5,6},{6,5},{7,4},{8,11},{9,10},{10,... | collective-permute-start | bytes 6152 | tf_op jit(solution)/shard_map/ppermute | solution.py:234
  6.7 0.6 eq.54
  7.3 2.0 %collective-permute-start.1 = (bf16[64,3072]{1,0:T(8,128)(2,1)S(1)}, bf16[64,3072]{1,0:T(8,128)(2,1)S(1)}, u32[]{:S(2)}, u32[]{:S(2)}) collective-permute-start(bf16[64,3072]{1,0:T(8,128)(2,1)S(1)} %pad_maximum_fusion.1), channel_id=1, source_target_pairs={{0,2},{1,3},{2,0},{3,1},{4,6},{5,7},{6,4},{7,5},{8,10},{9,11},{10,... | collective-permute-start | bytes 1179656 | tf_op jit(solution)/shard_map/ppermute | solution.py:234
  9.4 0.6 constant_dynamic-update-slice_fusion.1
  10.1 10.9 %shard_map.94 = (bf16[2,320,3072]{2,1,0:T(8,128)(2,1)}, bf16[2,320,1024]{2,1,0:T(8,128)(2,1)}, bf16[2,320,1024]{2,1,0:T(8,128)(2,1)}) custom-call(bf16[128,3072]{1,0:T(8,128)(2,1)S(1)} %copy-done.1, bf16[128,3072]{1,0:T(8,128)(2,1)S(1)} %collective-permute-done.4.refs_1_, bf16[128,3072]{1,0:T(8,128)(2,1)} %refs_2_.2, ...), custom_call_target="tpu_custom_call" | custom-call | flops 3019898880 | bytes 18874368 | tf_op jit(solution)/shard_map/pallas_call | solution.py:113
  21.0 0.7 slice.136
  21.7 2.0 %collective-permute-start.7 = (bf16[32,3072]{1,0:T(8,128)(2,1)}, bf16[32,3072]{1,0:T(8,128)(2,1)S(1)}, u32[]{:S(2)}, u32[]{:S(2)}) collective-permute-start(bf16[32,3072]{1,0:T(8,128)(2,1)} %slice.136), channel_id=1, source_target_pairs={{0,8},{4,12},{8,0},{12,4},{16,24},{20,28},{24,16},{28,20},{1,9},{5... | collective-permute-start | bytes 589832 | tf_op jit(solution)/shard_map/ppermute | solution.py:234
  23.7 1.5 %collective-permute-start.6 = (bf16[32,3072]{1,0:T(8,128)(2,1)}, bf16[32,3072]{1,0:T(8,128)(2,1)S(1)}, u32[]{:S(2)}, u32[]{:S(2)}) collective-permute-start(bf16[32,3072]{1,0:T(8,128)(2,1)} %slice.136), channel_id=1, source_target_pairs={{0,4},{4,0},{8,12},{12,8},{16,20},{20,16},{24,28},{28,24},{1,5},{5... | collective-permute-start | bytes 589832 | tf_op jit(solution)/shard_map/ppermute | solution.py:234
  25.2 6.7 %shard_map.95 = (bf16[2,320,3072]{2,1,0:T(8,128)(2,1)}, bf16[2,320,1024]{2,1,0:T(8,128)(2,1)}, bf16[2,320,1024]{2,1,0:T(8,128)(2,1)}) custom-call(bf16[128,3072]{1,0:T(8,128)(2,1)S(1)} %copy-done.1, bf16[128,3072]{1,0:T(8,128)(2,1)S(1)} %collective-permute-done.4.refs_1_, ...), custom_call_target="tpu_custom_call", output_to_operand_aliasing={{0}: (9, {}), {1}: (10, {}), {2}: (11, {})} | custom-call | flops 1509949440 | bytes 9437184 | tf_op jit(solution)/shard_map/pallas_call | solution.py:113
  31.9 1.6 %slice.137 = bf16[32,3072]{1,0:T(8,128)(2,1)} slice(bf16[64,3072]{1,0:T(8,128)(2,1)} %collective-permute-done.11.refs_6_), slice={[0:32], [0:3072]} | slice | bytes 393216 | tf_op jit(solution)/shard_map/slice | solution.py:282
  33.5 0.4 collective-permute-start.13
  34.1 0.7 stack.45
  34.8 0.7 stack.46
  35.6 0.7 pad_maximum_fusion.8
  36.4 0.6 copy.33
  37.2 0.7 eq.51
  38.0 1.2 copy.32
  39.2 0.9 fusion.8
  40.1 0.6 collective-permute-start.8
  40.9 6.8 %shard_map.96 = (bf16[2,320,3072]{2,1,0:T(8,128)(2,1)}, bf16[2,320,1024]{2,1,0:T(8,128)(2,1)}, bf16[2,320,1024]{2,1,0:T(8,128)(2,1)}) custom-call(bf16[128,3072]{1,0:T(8,128)(2,1)S(1)} %copy-done.1, bf16[128,3072]{1,0:T(8,128)(2,1)S(1)} %collective-permute-done.4.refs_1_, ...), custom_call_target="tpu_custom_call", output_to_operand_aliasing={{0}: (9, {}), {1}: (10, {}), {2}: (11, {})} | custom-call | flops 1509949440 | bytes 9437184 | tf_op jit(solution)/shard_map/pallas_call | solution.py:113
  47.7 0.5 collective-permute-start.9
  48.3 0.4 collective-permute-start.15
  48.7 0.6 collective-permute-done.9.refs_4_
  49.9 19.0 %shard_map.97 = (bf16[2,320,3072]{2,1,0:T(8,128)(2,1)}, bf16[2,320,1024]{2,1,0:T(8,128)(2,1)}, bf16[2,320,1024]{2,1,0:T(8,128)(2,1)}) custom-call(bf16[64,3072]{1,0:T(8,128)(2,1)S(1)} %collective-permute-done.1.refs_0_, bf16[32,3072]{1,0:T(8,128)(2,1)S(1)} %collective-permute-done.6.refs_1_, ...), custom_call_target="tpu_custom_call", output_to_operand_aliasing={{0}: (17, {}), {1}: (18, {}), {2}: (19, {})} | custom-call | flops 6039797760 | bytes 37748736 | tf_op jit(solution)/shard_map/pallas_call | solution.py:113
  68.9 8.9 %shard_map.98 = (bf16[256,1536]{1,0:T(8,128)(2,1)S(1)}, bf16[256,1536]{1,0:T(8,128)(2,1)S(1)}) custom-call(bf16[4,128,160]{2,1,0:T(8,128)(2,1)S(1)} %compare_convert_fusion.back, bf16[2,320,1024]{2,1,0:T(8,128)(2,1)} %get-tuple-element.87.gate_grad, bf16[2,320,1024]{2,1,0:T(8,128)(2,1)} %get-tuple-element.88.up_grad, bf16[2,3072,1024]{2,1,0:T(8,128)(2,1)} %w_gate.3, ...), custom_call_target="tpu_custom_call" | custom-call | flops 4026531840 | bytes 12582912 | tf_op jit(solution)/shard_map/pallas_call | solution.py:163
  78.1 8.9 %shard_map.99 = (bf16[256,1536]{1,0:T(8,128)(2,1)S(1)}, bf16[256,1536]{1,0:T(8,128)(2,1)S(1)}) custom-call(bf16[4,128,160]{2,1,0:T(8,128)(2,1)S(1)} %compare_convert_fusion.back, bf16[2,320,1024]{2,1,0:T(8,128)(2,1)} %get-tuple-element.87.gate_grad, bf16[2,320,1024]{2,1,0:T(8,128)(2,1)} %get-tuple-element.88.up_grad, bf16[2,3072,1024]{2,1,0:T(8,128)(2,1)} %w_gate.3, ...), custom_call_target="tpu_custom_call" | custom-call | flops 4026531840 | bytes 12582912 | tf_op jit(solution)/shard_map/pallas_call | solution.py:163
  87.5 1.8 %collective-permute-done.18 = bf16[256,1536]{1,0:T(8,128)(2,1)S(1)} collective-permute-done((bf16[256,1536]{1,0:T(8,128)(2,1)S(1)}, bf16[256,1536]{1,0:T(8,128)(2,1)S(1)}, u32[]{:S(2)}, u32[]{:S(2)}) %collective-permute-start.18) | collective-permute-done | bytes 786464 | tf_op jit(solution)/shard_map/ppermute | solution.py:234
  89.5 2.0 %collective-permute-start.19 = (bf16[128,1536]{1,0:T(8,128)(2,1)S(1)}, bf16[128,1536]{1,0:T(8,128)(2,1)S(1)}, u32[]{:S(2)}, u32[]{:S(2)}) collective-permute-start(bf16[128,1536]{1,0:T(8,128)(2,1)S(1)} %slice.184), channel_id=1, source_target_pairs={{0,2},{1,3},{2,0},{3,1},{4,6},{5,7},{6,4},{7,5},{8,10},{9,11},{10,... | collective-permute-start | bytes 1179656 | tf_op jit(solution)/shard_map/ppermute | solution.py:234
  91.6 1.6 %collective-permute-start.20 = (bf16[64,1536]{1,0:T(8,128)(2,1)S(1)}, bf16[64,1536]{1,0:T(8,128)(2,1)S(1)}, u32[]{:S(2)}, u32[]{:S(2)}) collective-permute-start(bf16[64,1536]{1,0:T(8,128)(2,1)S(1)} %pad_maximum_fusion.3), channel_id=1, source_target_pairs={{0,8},{4,12},{8,0},{12,4},{16,24},{20,28},{24,16},{28,20},{1,9},{5... | collective-permute-start | bytes 589832 | tf_op jit(solution)/shard_map/ppermute | solution.py:234
  93.1 1.5 %collective-permute-start.21 = (bf16[64,1536]{1,0:T(8,128)(2,1)S(1)}, bf16[64,1536]{1,0:T(8,128)(2,1)S(1)}, u32[]{:S(2)}, u32[]{:S(2)}) collective-permute-start(bf16[64,1536]{1,0:T(8,128)(2,1)S(1)} %pad_maximum_fusion.4), channel_id=1, source_target_pairs={{0,4},{4,0},{8,12},{12,8},{16,20},{20,16},{24,28},{28,24},{1,5},{5... | collective-permute-start | bytes 589832 | tf_op jit(solution)/shard_map/ppermute | solution.py:234
  95.0 10.6 %shard_map.100 = (f32[2,3072,1024]{2,1,0:T(8,128)}, f32[2,3072,1024]{2,1,0:T(8,128)}) custom-call(bf16[2,320,3072]{2,1,0:T(8,128)(2,1)} %get-tuple-element.113.rows, bf16[2,320,1024]{2,1,0:T(8,128)(2,1)S(1)} %copy-done, bf16[2,320,1024]{2,1,0:T(8,128)(2,1)} %get-tuple-element.88.up_grad), custom_call_target="tpu_custom_call" | custom-call | flops 4026531840 | bytes 25165824 | tf_op jit(solution)/shard_map/pallas_call | solution.py:201
  106.2 1.9 %collective-permute-start.23 = (bf16[32,1536]{1,0:T(8,128)(2,1)S(1)}, bf16[32,1536]{1,0:T(8,128)(2,1)S(1)}, u32[]{:S(2)}, u32[]{:S(2)}) collective-permute-start(bf16[32,1536]{1,0:T(8,128)(2,1)S(1)} %get-tuple-element.129), channel_id=1, source_target_pairs={{0,8},{4,12},{8,0},{12,4},{16,24},{20,28},{24,16},{28,20},{1,9},{5... | collective-permute-start | bytes 294920 | tf_op jit(solution)/shard_map/ppermute | solution.py:234
  108.1 1.4 %collective-permute-start.25 = (bf16[32,1536]{1,0:T(8,128)(2,1)S(1)}, bf16[32,1536]{1,0:T(8,128)(2,1)S(1)}, u32[]{:S(2)}, u32[]{:S(2)}) collective-permute-start(bf16[32,1536]{1,0:T(8,128)(2,1)S(1)} %get-tuple-element.130), channel_id=1, source_target_pairs={{0,12},{4,8},{8,4},{12,0},{16,28},{20,24},{24,20},{28,16},{1,13},{... | collective-permute-start | bytes 294920 | tf_op jit(solution)/shard_map/ppermute | solution.py:234
  109.8 0.7 collective-permute-done.26
  110.6 1.1 collective-permute-done.23
  111.6 2.0 %collective-permute-done.25 = bf16[32,1536]{1,0:T(8,128)(2,1)S(1)} collective-permute-done((bf16[32,1536]{1,0:T(8,128)(2,1)S(1)}, bf16[32,1536]{1,0:T(8,128)(2,1)S(1)}, u32[]{:S(2)}, u32[]{:S(2)}) %collective-permute-start.25) | collective-permute-done | bytes 98336 | tf_op jit(solution)/shard_map/ppermute | solution.py:234
  113.7 1.0 collective-permute-done.24
  114.7 2.6 %collective-permute-start.27 = (bf16[32,3072]{1,0:T(8,128)(2,1)S(1)}, bf16[32,3072]{1,0:T(8,128)(2,1)S(1)}, u32[]{:S(2)}, u32[]{:S(2)}) collective-permute-start(bf16[32,3072]{1,0:T(8,128)(2,1)S(1)} %pad_maximum_fusion.6), channel_id=1, source_target_pairs={{0,16},{4,20},{8,24},{12,28},{16,0},{20,4},{24,8},{28,12},{1,17},{... | collective-permute-start | bytes 589832 | tf_op jit(solution)/shard_map/ppermute | solution.py:234
  117.4 6.6 %shard_map.101 = (f32[2,3072,1024]{2,1,0:T(8,128)}, f32[2,3072,1024]{2,1,0:T(8,128)}) custom-call(bf16[2,320,3072]{2,1,0:T(8,128)(2,1)} %get-tuple-element.113.rows, bf16[2,320,1024]{2,1,0:T(8,128)(2,1)S(1)} %copy-done, bf16[2,320,1024]{2,1,0:T(8,128)(2,1)} %get-tuple-element.88.up_grad, ...), custom_call_target="tpu_custom_call", output_to_operand_aliasing={{0}: (3, {}), {1}: (4, {})} | custom-call | flops 2013265920 | bytes 12582912 | tf_op jit(solution)/shard_map/pallas_call | solution.py:201
  124.3 1.2 collective-permute-start.30
  125.5 1.2 collective-permute-start.29
  126.7 1.1 collective-permute-start.28
  127.8 6.6 %shard_map.102 = (f32[2,3072,1024]{2,1,0:T(8,128)}, f32[2,3072,1024]{2,1,0:T(8,128)}) custom-call(bf16[2,320,3072]{2,1,0:T(8,128)(2,1)} %get-tuple-element.113.rows, bf16[2,320,1024]{2,1,0:T(8,128)(2,1)S(1)} %copy-done, bf16[2,320,1024]{2,1,0:T(8,128)(2,1)} %get-tuple-element.88.up_grad, ...), custom_call_target="tpu_custom_call", output_to_operand_aliasing={{0}: (3, {}), {1}: (4, {})} | custom-call | flops 2013265920 | bytes 12582912 | tf_op jit(solution)/shard_map/pallas_call | solution.py:201
  134.8 0.4 collective-permute-done.28
  135.4 1.0 reverse_select_fusion
  (89 shorter events, 5.6 us)
Async XLA Ops:
  0.7 1.5 %copy-start.1 = (bf16[128,3072]{1,0:T(8,128)(2,1)S(1)}, bf16[128,3072]{1,0:T(8,128)(2,1)}, u32[]{:S(2)}) copy-start(bf16[128,3072]{1,0:T(8,128)(2,1)} %refs_0_.2) | copy-start | bytes 2359300
  0.7 2.0 %copy-start.2 = (bf16[128,3072]{1,0:T(8,128)(2,1)S(1)}, bf16[128,3072]{1,0:T(8,128)(2,1)}, u32[]{:S(2)}) copy-start(bf16[128,3072]{1,0:T(8,128)(2,1)} %refs_2_.2) | copy-start | bytes 2359300
  0.7 2.1 %copy-start.4 = (s32[128,4]{0,1:T(4,128)S(1)}, s32[128,4]{0,1:T(4,128)}, u32[]{:S(2)}) copy-start(s32[128,4]{0,1:T(4,128)} %param.8) | copy-start | bytes 6148
  0.7 2.1 %copy-start.6 = (f32[128,4]{0,1:T(4,128)S(1)}, f32[128,4]{0,1:T(4,128)}, u32[]{:S(2)}) copy-start(f32[128,4]{0,1:T(4,128)} %param.9) | copy-start | bytes 6148
  2.2 7.8 %collective-permute-start.4 = (bf16[128,3072]{1,0:T(8,128)(2,1)S(1)}, bf16[128,3072]{1,0:T(8,128)(2,1)S(1)}, u32[]{:S(2)}, u32[]{:S(2)}) collective-permute-start(bf16[128,3072]{1,0:T(8,128)(2,1)S(1)} %copy-done.1), channel_id=1, source_target_pairs={{0,1},{1,0},{2,3},{3,2},{4,5},{5,4},{6,7},{7,6},{8,9},{9,8},{10,11... | collective-permute-start | bytes 2359304 | tf_op jit(solution)/shard_map/ppermute | solution.py:234
  2.7 7.4 %collective-permute-start.5 = (bf16[128,3072]{1,0:T(8,128)(2,1)S(1)}, bf16[128,3072]{1,0:T(8,128)(2,1)}, u32[]{:S(2)}, u32[]{:S(2)}) collective-permute-start(bf16[128,3072]{1,0:T(8,128)(2,1)S(1)} %copy-done.2), channel_id=1, source_target_pairs={{0,1},{1,0},{2,3},{3,2},{4,5},{5,4},{6,7},{7,6},{8,9},{9,8},{10,11... | collective-permute-start | bytes 2359304 | tf_op jit(solution)/shard_map/ppermute | solution.py:234
  3.6 3.7 %collective-permute-start = (f32[2,2,128]{2,0,1:T(2,128)S(1)}, f32[2,2,128]{2,0,1:T(2,128)S(1)}, u32[]{:S(2)}, u32[]{:S(2)}) collective-permute-start(f32[2,2,128]{2,0,1:T(2,128)S(1)} %get-tuple-element.142), channel_id=1, source_target_pairs={{0,1},{1,0},{2,3},{3,2},{4,5},{5,4},{6,7},{7,6},{8,9},{9,8},{10,11... | collective-permute-start | bytes 6152 | tf_op jit(solution)/shard_map/ppermute | solution.py:234
  4.0 17.0 %collective-permute-start.3 = (f32[2,2,128]{2,0,1:T(2,128)}, f32[2,2,128]{2,0,1:T(2,128)}, u32[]{:S(2)}, u32[]{:S(2)}) collective-permute-start(f32[2,2,128]{2,0,1:T(2,128)} %get-tuple-element.140), channel_id=1, source_target_pairs={{0,3},{1,2},{2,1},{3,0},{4,7},{5,6},{6,5},{7,4},{8,11},{9,10},{10,... | collective-permute-start | bytes 6152 | tf_op jit(solution)/shard_map/ppermute | solution.py:234
  6.6 14.3 %collective-permute-start.2 = (f32[2,2,128]{2,0,1:T(2,128)}, f32[2,2,128]{2,0,1:T(2,128)}, u32[]{:S(2)}, u32[]{:S(2)}) collective-permute-start(f32[2,2,128]{2,0,1:T(2,128)} %get-tuple-element.143), channel_id=1, source_target_pairs={{0,2},{1,3},{2,0},{3,1},{4,6},{5,7},{6,4},{7,5},{8,10},{9,11},{10,... | collective-permute-start | bytes 6152 | tf_op jit(solution)/shard_map/ppermute | solution.py:234
  7.3 13.6 %collective-permute-start.1 = (bf16[64,3072]{1,0:T(8,128)(2,1)S(1)}, bf16[64,3072]{1,0:T(8,128)(2,1)S(1)}, u32[]{:S(2)}, u32[]{:S(2)}) collective-permute-start(bf16[64,3072]{1,0:T(8,128)(2,1)S(1)} %pad_maximum_fusion.1), channel_id=1, source_target_pairs={{0,2},{1,3},{2,0},{3,1},{4,6},{5,7},{6,4},{7,5},{8,10},{9,11},{10,... | collective-permute-start | bytes 1179656 | tf_op jit(solution)/shard_map/ppermute | solution.py:234
  10.0 21.9 %collective-permute-start.11 = (bf16[64,3072]{1,0:T(8,128)(2,1)S(1)}, bf16[64,3072]{1,0:T(8,128)(2,1)}, u32[]{:S(2)}, u32[]{:S(2)}) collective-permute-start(bf16[64,3072]{1,0:T(8,128)(2,1)S(1)} %pad_maximum_fusion.2), channel_id=1, source_target_pairs={{0,2},{1,3},{2,0},{3,1},{4,6},{5,7},{6,4},{7,5},{8,10},{9,11},{10,... | collective-permute-start | bytes 1179656 | tf_op jit(solution)/shard_map/ppermute | solution.py:234
  21.7 15.4 %copy-start.3 = (f32[2,4,2,2,32]{4,3,2,1,0:T(2,128)S(1)}, f32[2,4,2,2,32]{4,3,2,1,0:T(2,128)}, u32[]{:S(2)}) copy-start(f32[2,4,2,2,32]{4,3,2,1,0:T(2,128)} %constant_dynamic-update-slice_fusion.1) | copy-start | bytes 12292
  21.7 18.4 %collective-permute-start.7 = (bf16[32,3072]{1,0:T(8,128)(2,1)}, bf16[32,3072]{1,0:T(8,128)(2,1)S(1)}, u32[]{:S(2)}, u32[]{:S(2)}) collective-permute-start(bf16[32,3072]{1,0:T(8,128)(2,1)} %slice.136), channel_id=1, source_target_pairs={{0,8},{4,12},{8,0},{12,4},{16,24},{20,28},{24,16},{28,20},{1,9},{5... | collective-permute-start | bytes 589832 | tf_op jit(solution)/shard_map/ppermute | solution.py:234
  23.7 17.0 %collective-permute-start.6 = (bf16[32,3072]{1,0:T(8,128)(2,1)}, bf16[32,3072]{1,0:T(8,128)(2,1)S(1)}, u32[]{:S(2)}, u32[]{:S(2)}) collective-permute-start(bf16[32,3072]{1,0:T(8,128)(2,1)} %slice.136), channel_id=1, source_target_pairs={{0,4},{4,0},{8,12},{12,8},{16,20},{20,16},{24,28},{28,24},{1,5},{5... | collective-permute-start | bytes 589832 | tf_op jit(solution)/shard_map/ppermute | solution.py:234
  31.9 7.2 %copy-start.5 = (f32[160]{0:T(256)S(1)}, f32[160]{0:T(256)}, u32[]{:S(2)}) copy-start(f32[160]{0:T(256)} %eq.54) | copy-start | bytes 1924
  33.5 14.1 %collective-permute-start.13 = (bf16[32,3072]{1,0:T(8,128)(2,1)}, bf16[32,3072]{1,0:T(8,128)(2,1)S(1)}, u32[]{:S(2)}, u32[]{:S(2)}) collective-permute-start(bf16[32,3072]{1,0:T(8,128)(2,1)} %slice.137), channel_id=1, source_target_pairs={{0,8},{4,12},{8,0},{12,4},{16,24},{20,28},{24,16},{28,20},{1,9},{5... | collective-permute-start | bytes 589832 | tf_op jit(solution)/shard_map/ppermute | solution.py:234
  34.0 14.2 %collective-permute-start.12 = (bf16[32,3072]{1,0:T(8,128)(2,1)}, bf16[32,3072]{1,0:T(8,128)(2,1)S(1)}, u32[]{:S(2)}, u32[]{:S(2)}) collective-permute-start(bf16[32,3072]{1,0:T(8,128)(2,1)} %slice.137), channel_id=1, source_target_pairs={{0,4},{4,0},{8,12},{12,8},{16,20},{20,16},{24,28},{28,24},{1,5},{5... | collective-permute-start | bytes 589832 | tf_op jit(solution)/shard_map/ppermute | solution.py:234
  34.1 15.8 %collective-permute-start.14 = (bf16[64,3072]{1,0:T(8,128)(2,1)}, bf16[64,3072]{1,0:T(8,128)(2,1)}, u32[]{:S(2)}, u32[]{:S(2)}) collective-permute-start(bf16[64,3072]{1,0:T(8,128)(2,1)} %collective-permute-done.11.refs_6_), channel_id=1, source_target_pairs={{0,1},{1,0},{2,3},{3,2},{4,5},{5,4},{6,7},{7,6},{8,9},{9,8},{10,11... | collective-permute-start | bytes 1179656 | tf_op jit(solution)/shard_map/ppermute | solution.py:234
  40.1 9.8 %collective-permute-start.8 = (bf16[64,3072]{1,0:T(8,128)(2,1)S(1)}, bf16[64,3072]{1,0:T(8,128)(2,1)}, u32[]{:S(2)}, u32[]{:S(2)}) collective-permute-start(bf16[64,3072]{1,0:T(8,128)(2,1)S(1)} %collective-permute-done.1.refs_0_), channel_id=1, source_target_pairs={{0,1},{1,0},{2,3},{3,2},{4,5},{5,4},{6,7},{7,6},{8,9},{9,8},{10,11... | collective-permute-start | bytes 1179656 | tf_op jit(solution)/shard_map/ppermute | solution.py:234
  40.7 7.6 %collective-permute-start.10 = (bf16[32,3072]{1,0:T(8,128)(2,1)S(1)}, bf16[32,3072]{1,0:T(8,128)(2,1)S(1)}, u32[]{:S(2)}, u32[]{:S(2)}) collective-permute-start(bf16[32,3072]{1,0:T(8,128)(2,1)S(1)} %collective-permute-done.7.refs_2_), channel_id=1, source_target_pairs={{0,1},{1,0},{2,3},{3,2},{4,5},{5,4},{6,7},{7,6},{8,9},{9,8},{10,11... | collective-permute-start | bytes 589832 | tf_op jit(solution)/shard_map/ppermute | solution.py:234
  47.7 1.6 %collective-permute-start.9 = (bf16[32,3072]{1,0:T(8,128)(2,1)S(1)}, bf16[32,3072]{1,0:T(8,128)(2,1)S(1)}, u32[]{:S(2)}, u32[]{:S(2)}) collective-permute-start(bf16[32,3072]{1,0:T(8,128)(2,1)S(1)} %collective-permute-done.6.refs_1_), channel_id=1, source_target_pairs={{0,1},{1,0},{2,3},{3,2},{4,5},{5,4},{6,7},{7,6},{8,9},{9,8},{10,11... | collective-permute-start | bytes 589832 | tf_op jit(solution)/shard_map/ppermute | solution.py:234
  48.2 1.4 %collective-permute-start.16 = (bf16[32,3072]{1,0:T(8,128)(2,1)S(1)}, bf16[32,3072]{1,0:T(8,128)(2,1)S(1)}, u32[]{:S(2)}, u32[]{:S(2)}) collective-permute-start(bf16[32,3072]{1,0:T(8,128)(2,1)S(1)} %collective-permute-done.13.refs_8_), channel_id=1, source_target_pairs={{0,1},{1,0},{2,3},{3,2},{4,5},{5,4},{6,7},{7,6},{8,9},{9,8},{10,11... | collective-permute-start | bytes 589832 | tf_op jit(solution)/shard_map/ppermute | solution.py:234
  48.3 1.6 %collective-permute-start.15 = (bf16[32,3072]{1,0:T(8,128)(2,1)S(1)}, bf16[32,3072]{1,0:T(8,128)(2,1)S(1)}, u32[]{:S(2)}, u32[]{:S(2)}) collective-permute-start(bf16[32,3072]{1,0:T(8,128)(2,1)S(1)} %collective-permute-done.12.refs_7_), channel_id=1, source_target_pairs={{0,1},{1,0},{2,3},{3,2},{4,5},{5,4},{6,7},{7,6},{8,9},{9,8},{10,11... | collective-permute-start | bytes 589832 | tf_op jit(solution)/shard_map/ppermute | solution.py:234
  77.8 9.5 %collective-permute-start.17 = (bf16[256,1536]{1,0:T(8,128)(2,1)S(1)}, bf16[256,1536]{1,0:T(8,128)(2,1)S(1)}, u32[]{:S(2)}, u32[]{:S(2)}) collective-permute-start(bf16[256,1536]{1,0:T(8,128)(2,1)S(1)} %get-tuple-element.90), channel_id=1, source_target_pairs={{0,1},{1,0},{2,3},{3,2},{4,5},{5,4},{6,7},{7,6},{8,9},{9,8},{10,11... | collective-permute-start | bytes 2359304 | tf_op jit(solution)/shard_map/ppermute | solution.py:234
  87.0 2.4 %collective-permute-start.18 = (bf16[256,1536]{1,0:T(8,128)(2,1)S(1)}, bf16[256,1536]{1,0:T(8,128)(2,1)S(1)}, u32[]{:S(2)}, u32[]{:S(2)}) collective-permute-start(bf16[256,1536]{1,0:T(8,128)(2,1)S(1)} %get-tuple-element.92), channel_id=1, source_target_pairs={{0,1},{1,0},{2,3},{3,2},{4,5},{5,4},{6,7},{7,6},{8,9},{9,8},{10,11... | collective-permute-start | bytes 2359304 | tf_op jit(solution)/shard_map/ppermute | solution.py:234
  87.5 7.5 %copy-start = (bf16[2,320,1024]{2,1,0:T(8,128)(2,1)S(1)}, bf16[2,320,1024]{2,1,0:T(8,128)(2,1)}, u32[]{:S(2)}) copy-start(bf16[2,320,1024]{2,1,0:T(8,128)(2,1)} %get-tuple-element.87.gate_grad) | copy-start | bytes 3932164
  89.5 16.2 %collective-permute-start.19 = (bf16[128,1536]{1,0:T(8,128)(2,1)S(1)}, bf16[128,1536]{1,0:T(8,128)(2,1)S(1)}, u32[]{:S(2)}, u32[]{:S(2)}) collective-permute-start(bf16[128,1536]{1,0:T(8,128)(2,1)S(1)} %slice.184), channel_id=1, source_target_pairs={{0,2},{1,3},{2,0},{3,1},{4,6},{5,7},{6,4},{7,5},{8,10},{9,11},{10,... | collective-permute-start | bytes 1179656 | tf_op jit(solution)/shard_map/ppermute | solution.py:234
  91.6 14.1 %collective-permute-start.20 = (bf16[64,1536]{1,0:T(8,128)(2,1)S(1)}, bf16[64,1536]{1,0:T(8,128)(2,1)S(1)}, u32[]{:S(2)}, u32[]{:S(2)}) collective-permute-start(bf16[64,1536]{1,0:T(8,128)(2,1)S(1)} %pad_maximum_fusion.3), channel_id=1, source_target_pairs={{0,8},{4,12},{8,0},{12,4},{16,24},{20,28},{24,16},{28,20},{1,9},{5... | collective-permute-start | bytes 589832 | tf_op jit(solution)/shard_map/ppermute | solution.py:234
  93.1 12.6 %collective-permute-start.21 = (bf16[64,1536]{1,0:T(8,128)(2,1)S(1)}, bf16[64,1536]{1,0:T(8,128)(2,1)S(1)}, u32[]{:S(2)}, u32[]{:S(2)}) collective-permute-start(bf16[64,1536]{1,0:T(8,128)(2,1)S(1)} %pad_maximum_fusion.4), channel_id=1, source_target_pairs={{0,4},{4,0},{8,12},{12,8},{16,20},{20,16},{24,28},{28,24},{1,5},{5... | collective-permute-start | bytes 589832 | tf_op jit(solution)/shard_map/ppermute | solution.py:234
  94.6 11.1 %collective-permute-start.22 = (bf16[64,1536]{1,0:T(8,128)(2,1)S(1)}, bf16[64,1536]{1,0:T(8,128)(2,1)S(1)}, u32[]{:S(2)}, u32[]{:S(2)}) collective-permute-start(bf16[64,1536]{1,0:T(8,128)(2,1)S(1)} %pad_maximum_fusion.5), channel_id=1, source_target_pairs={{0,12},{4,8},{8,4},{12,0},{16,28},{20,24},{24,20},{28,16},{1,13},{... | collective-permute-start | bytes 589832 | tf_op jit(solution)/shard_map/ppermute | solution.py:234
  105.8 4.7 %collective-permute-start.26 = (bf16[32,1536]{1,0:T(8,128)(2,1)S(1)}, bf16[32,1536]{1,0:T(8,128)(2,1)S(1)}, u32[]{:S(2)}, u32[]{:S(2)}) collective-permute-start(bf16[32,1536]{1,0:T(8,128)(2,1)S(1)} %add_convert_fusion.3), channel_id=1, source_target_pairs={{0,2},{1,3},{2,0},{3,1},{4,6},{5,7},{6,4},{7,5},{8,10},{9,11},{10,... | collective-permute-start | bytes 294920 | tf_op jit(solution)/shard_map/ppermute | solution.py:234
  106.2 5.4 %collective-permute-start.23 = (bf16[32,1536]{1,0:T(8,128)(2,1)S(1)}, bf16[32,1536]{1,0:T(8,128)(2,1)S(1)}, u32[]{:S(2)}, u32[]{:S(2)}) collective-permute-start(bf16[32,1536]{1,0:T(8,128)(2,1)S(1)} %get-tuple-element.129), channel_id=1, source_target_pairs={{0,8},{4,12},{8,0},{12,4},{16,24},{20,28},{24,16},{28,20},{1,9},{5... | collective-permute-start | bytes 294920 | tf_op jit(solution)/shard_map/ppermute | solution.py:234
  108.1 5.6 %collective-permute-start.25 = (bf16[32,1536]{1,0:T(8,128)(2,1)S(1)}, bf16[32,1536]{1,0:T(8,128)(2,1)S(1)}, u32[]{:S(2)}, u32[]{:S(2)}) collective-permute-start(bf16[32,1536]{1,0:T(8,128)(2,1)S(1)} %get-tuple-element.130), channel_id=1, source_target_pairs={{0,12},{4,8},{8,4},{12,0},{16,28},{20,24},{24,20},{28,16},{1,13},{... | collective-permute-start | bytes 294920 | tf_op jit(solution)/shard_map/ppermute | solution.py:234
  109.5 5.2 %collective-permute-start.24 = (bf16[32,1536]{1,0:T(8,128)(2,1)S(1)}, bf16[32,1536]{1,0:T(8,128)(2,1)S(1)}, u32[]{:S(2)}, u32[]{:S(2)}) collective-permute-start(bf16[32,1536]{1,0:T(8,128)(2,1)S(1)} %get-tuple-element.131), channel_id=1, source_target_pairs={{0,4},{4,0},{8,12},{12,8},{16,20},{20,16},{24,28},{28,24},{1,5},{5... | collective-permute-start | bytes 294920 | tf_op jit(solution)/shard_map/ppermute | solution.py:234
  114.7 9.5 %collective-permute-start.27 = (bf16[32,3072]{1,0:T(8,128)(2,1)S(1)}, bf16[32,3072]{1,0:T(8,128)(2,1)S(1)}, u32[]{:S(2)}, u32[]{:S(2)}) collective-permute-start(bf16[32,3072]{1,0:T(8,128)(2,1)S(1)} %pad_maximum_fusion.6), channel_id=1, source_target_pairs={{0,16},{4,20},{8,24},{12,28},{16,0},{20,4},{24,8},{28,12},{1,17},{... | collective-permute-start | bytes 589832 | tf_op jit(solution)/shard_map/ppermute | solution.py:234
  124.3 10.2 %collective-permute-start.30 = (bf16[32,3072]{1,0:T(8,128)(2,1)S(1)}, bf16[32,3072]{1,0:T(8,128)(2,1)S(1)}, u32[]{:S(2)}, u32[]{:S(2)}) collective-permute-start(bf16[32,3072]{1,0:T(8,128)(2,1)S(1)} %add_convert_fusion.1), channel_id=1, source_target_pairs={{0,12},{4,8},{8,4},{12,0},{16,28},{20,24},{24,20},{28,16},{1,13},{... | collective-permute-start | bytes 589832 | tf_op jit(solution)/shard_map/ppermute | solution.py:234
  125.5 9.2 %collective-permute-start.29 = (bf16[32,3072]{1,0:T(8,128)(2,1)S(1)}, bf16[32,3072]{1,0:T(8,128)(2,1)S(1)}, u32[]{:S(2)}, u32[]{:S(2)}) collective-permute-start(bf16[32,3072]{1,0:T(8,128)(2,1)S(1)} %add_convert_fusion.1), channel_id=1, source_target_pairs={{0,4},{4,0},{8,12},{12,8},{16,20},{20,16},{24,28},{28,24},{1,5},{5... | collective-permute-start | bytes 589832 | tf_op jit(solution)/shard_map/ppermute | solution.py:234
  126.7 8.5 %collective-permute-start.28 = (bf16[32,3072]{1,0:T(8,128)(2,1)S(1)}, bf16[32,3072]{1,0:T(8,128)(2,1)S(1)}, u32[]{:S(2)}, u32[]{:S(2)}) collective-permute-start(bf16[32,3072]{1,0:T(8,128)(2,1)S(1)} %add_convert_fusion.1), channel_id=1, source_target_pairs={{0,8},{4,12},{8,0},{12,4},{16,24},{20,28},{24,16},{28,20},{1,9},{5... | collective-permute-start | bytes 589832 | tf_op jit(solution)/shard_map/ppermute | solution.py:234

commit v3 on v2

--- a/solution.py
+++ b/solution.py
@@ -9,7 +9,7 @@
 
 EXPERTS = 8
 MOST = 80
-UNIT_TILE = 256
+UNIT_TILE = 512
 FEATURE_TILE = 512
 VMEM_BYTES = 52 * 1024 * 1024
 BF16 = jnp.bfloat16
@@ -54,91 +54,128 @@
     return [slice(c, c + step) for c in range(0, features, step)]
 
 
-def slots_kernel(count, *refs):
-    x_pieces, g_pieces = refs[:count], refs[count : 2 * count]
-    slot, weight, w_gate, w_up, w_down = refs[2 * count : 2 * count + 5]
-    rows, gate_grad, up_grad, held, chosen, grads = refs[-6:]
+def dispatch(pieces, slot, held, chosen, out, weight=None):
     experts, blocks, tokens = slot.shape
     group = held.shape[0] // tokens
-    expert = pl.program_id(0)
-
-    @pl.when((expert == 0) & (pl.program_id(1) == 0))
-    def _():
-        for start in range(0, blocks, group):
-            chosen[...] = jnp.zeros_like(chosen)
-            scales = []
-            places = [(l, b) for l in range(experts) for b in range(group)]
-            for i, (l, b) in enumerate(places):
-                at = slice(start + b, start + b + 1)
-                mask = one_hot(slot[l, at, :])
-                chosen[i * MOST : (i + 1) * MOST, b * tokens : (b + 1) * tokens] = mask.astype(BF16)
+    places = [(l, b) for l in range(experts) for b in range(group)]
+    for start in range(0, blocks, group):
+        chosen[...] = jnp.zeros_like(chosen)
+        scales = []
+        for i, (l, b) in enumerate(places):
+            at = slice(start + b, start + b + 1)
+            mask = one_hot(slot[l, at, :])
+            chosen[i * MOST : (i + 1) * MOST, b * tokens : (b + 1) * tokens] = mask.astype(BF16)
+            if weight is not None:
                 scales.append(
                     jnp.sum(jnp.where(mask, weight[l, at, :], 0.0), axis=1, keepdims=True)
                 )
-            for pieces, out in ((x_pieces, rows), (g_pieces, grads)):
-                lay_out(held, pieces, start * tokens)
-                for cols in column_chunks(held.shape[1]):
-                    taken = dot(chosen[...], held[:, cols])
-                    for i, (l, b) in enumerate(places):
-                        part = taken[i * MOST : (i + 1) * MOST]
-                        if out is grads:
-                            part = part * scales[i]
-                        span = slice((start + b) * MOST, (start + b + 1) * MOST)
-                        out[l, span, cols] = part.astype(BF16)
+        lay_out(held, pieces, start * tokens)
+        for cols in column_chunks(held.shape[1]):
+            taken = dot(chosen[...], held[:, cols])
+            for i, (l, b) in enumerate(places):
+                part = taken[i * MOST : (i + 1) * MOST]
+                if scales:
+                    part = part * scales[i]
+                span = slice((start + b) * MOST, (start + b + 1) * MOST)
+                out[l, span, cols] = part.astype(BF16)
+
+
+def dispatch_scratch(experts, blocks, tokens, features):
+    group = 2 if blocks % 2 == 0 else 1
+    return [
+        pltpu.VMEM((group * tokens, features), BF16),
+        pltpu.VMEM((experts * group * MOST, group * tokens), BF16),
+        pltpu.VMEM((experts, blocks * MOST, features), BF16),
+    ]
+
+
+def forward_kernel(count, *refs):
+    pieces, (slot, w_gate, w_up, rows_out, act, slope) = refs[:count], refs[count : count + 6]
+    held, chosen, rows, sent = refs[count + 6 :]
+    expert, tile = pl.program_id(0), pl.program_id(1)
+    copy = pltpu.make_async_copy(rows, rows_out, sent)
+
+    @pl.when((expert == 0) & (tile == 0))
+    def _():
+        dispatch(pieces, slot, held, chosen, rows)
+        copy.start()
 
     x = rows[expert]
     gate = dot(x, w_gate[0])
     up = dot(x, w_up[0])
-    hidden = dot(grads[expert], w_down[0])
     sig = jax.nn.sigmoid(gate)
-    up_grad[0] = (hidden * (gate * sig)).astype(BF16)
-    gate_grad[0] = (hidden * up * sig * (1.0 + gate * (1.0 - sig))).astype(BF16)
-
-
-def slot_grads(x_pieces, g_pieces, table, weights, before, first, last, part, parts, share=(0, 1)):
-    slot, weight = table[:, 0], table[:, 1]
+    act[0] = gate * sig
+    slope[0] = up * sig * (1.0 + gate * (1.0 - sig))
+
+    @pl.when((expert == pl.num_programs(0) - 1) & (tile == pl.num_programs(1) - 1))
+    def _():
+        copy.wait()
+
+
+def forward(pieces, slot, w_gate, w_up):
     experts, blocks, tokens = slot.shape
-    _, features, units = weights[0].shape
+    _, features, units = w_gate.shape
     tile = min(UNIT_TILE, units)
-    tiles = units // tile // share[1]
-    skip = share[0] * tiles
     slots = blocks * MOST
-    count = last - first
-    group = 2 if blocks % 2 == 0 else 1
-    routes = pl.BlockSpec((count, blocks, tokens), lambda l, f: (first // count, 0, 0))
-    matrix = pl.BlockSpec((1, features, tile), lambda l, f: (first + l, 0, skip + f))
-    unit = pl.BlockSpec((1, slots, tile), lambda l, f: (first + l, part, skip + f))
-    pieces = [*x_pieces, *g_pieces]
-    kept = [] if before is None else list(before)
+    matrix = pl.BlockSpec((1, features, tile), lambda l, f: (l, 0, f))
+    unit = pl.BlockSpec((1, slots, tile), lambda l, f: (l, 0, f))
     return pl.pallas_call(
-        functools.partial(slots_kernel, len(x_pieces)),
-        grid=(count, tiles),
-        in_specs=[whole(p.shape) for p in pieces]
-        + [routes, routes, matrix, matrix, matrix]
-        + [pl.BlockSpec(memory_space=pl.ANY)] * len(kept),
-        out_specs=[
-            pl.BlockSpec((count, slots, features), lambda l, f: (first // count, part, 0)),
-            unit,
-            unit,
+        functools.partial(forward_kernel, len(pieces)),
+        grid=(experts, units // tile),
+        in_specs=[whole(p.shape) for p in pieces] + [whole(slot.shape), matrix, matrix],
+        out_specs=[pl.BlockSpec(memory_space=pl.ANY), unit, unit],
+        out_shape=[
+            jax.ShapeDtypeStruct((experts, slots, features), BF16),
+            jax.ShapeDtypeStruct((experts, slots, units), F32),
+            jax.ShapeDtypeStruct((experts, slots, units), F32),
         ],
-        out_shape=[
-            jax.ShapeDtypeStruct((experts, parts * slots, features), BF16),
-            jax.ShapeDtypeStruct((experts, parts * slots, units), BF16),
-            jax.ShapeDtypeStruct((experts, parts * slots, units), BF16),
-        ],
-        scratch_shapes=[
-            pltpu.VMEM((group * tokens, features), BF16),
-            pltpu.VMEM((count * group * MOST, group * tokens), BF16),
-            pltpu.VMEM((count, slots, features), BF16),
-        ],
-        input_output_aliases={len(pieces) + 5 + i: i for i in range(len(kept))},
+        scratch_shapes=dispatch_scratch(experts, blocks, tokens, features)
+        + [pltpu.SemaphoreType.DMA],
         compiler_params=params(2),
         cost_estimate=pl.CostEstimate(
-            flops=6 * count * slots * features * tiles * tile,
-            bytes_accessed=6 * count * features * tiles * tile,
-            transcendentals=count * slots * tiles * tile,
+            flops=4 * experts * slots * features * units,
+            bytes_accessed=4 * experts * features * units,
+            transcendentals=experts * slots * units,
         ),
-    )(*pieces, slot, weight, *weights, *kept)
+    )(*pieces, slot, w_gate, w_up)
+
+
+def hidden_kernel(count, *refs):
+    pieces, (slot, weight, act, slope, w_down) = refs[:count], refs[count : count + 5]
+    gate_grad, up_grad, held, chosen, grads = refs[count + 5 :]
+    expert = pl.program_id(0)
+
+    @pl.when((expert == 0) & (pl.program_id(1) == 0))
+    def _():
+        dispatch(pieces, slot, held, chosen, grads, weight)
+
+    hidden = dot(grads[expert], w_down[0])
+    up_grad[0] = (hidden * act[0]).astype(BF16)
+    gate_grad[0] = (hidden * slope[0]).astype(BF16)
+
+
+def hidden_grads(pieces, slot, weight, act, slope, w_down):
+    experts, blocks, tokens = slot.shape
+    _, features, units = w_down.shape
+    tile = min(UNIT_TILE, units)
+    slots = blocks * MOST
+    unit = pl.BlockSpec((1, slots, tile), lambda l, f: (l, 0, f))
+    return pl.pallas_call(
+        functools.partial(hidden_kernel, len(pieces)),
+        grid=(experts, units // tile),
+        in_specs=[whole(p.shape) for p in pieces]
+        + [whole(slot.shape), whole(slot.shape), unit, unit]
+        + [pl.BlockSpec((1, features, tile), lambda l, f: (l, 0, f))],
+        out_specs=[unit, unit],
+        out_shape=[jax.ShapeDtypeStruct((experts, slots, units), BF16)] * 2,
+        scratch_shapes=dispatch_scratch(experts, blocks, tokens, features),
+        compiler_params=params(2),
+        cost_estimate=pl.CostEstimate(
+            flops=2 * experts * slots * features * units,
+            bytes_accessed=2 * experts * features * units,
+            transcendentals=0,
+        ),
+    )(*pieces, slot, weight, act, slope, w_down)
 
 
 def inputs_kernel(groups, back, gate_grad, up_grad, w_gate, w_up, *refs):
@@ -190,19 +227,19 @@
     grad_up[0] = dot(rows[0], up_grad[0], TN)
 
 
-def weight_grads(rows, gate_grad, up_grad, before, expert, part=0, parts=1):
+def weight_grads(rows, gate_grad, up_grad, before, expert, first=0, steps=None):
     experts, slots, features = rows.shape
     units = gate_grad.shape[2]
     wide = FEATURE_TILE
-    steps = features // parts // wide
+    steps = features // wide if steps is None else steps
     unit = pl.BlockSpec((1, slots, units), lambda d: (expert, 0, 0))
-    out = pl.BlockSpec((1, wide, units), lambda d: (expert, part * steps + d, 0))
+    out = pl.BlockSpec((1, wide, units), lambda d: (expert, first + d, 0))
     kept = [] if before is None else list(before)
     return pl.pallas_call(
         weights_kernel,
         grid=(steps,),
         in_specs=[
-            pl.BlockSpec((1, slots, wide), lambda d: (expert, 0, part * steps + d)), unit, unit
+            pl.BlockSpec((1, slots, wide), lambda d: (expert, 0, first + d)), unit, unit
         ]
         + [pl.BlockSpec(memory_space=pl.ANY)] * len(kept),
         out_specs=[out, out],
@@ -210,8 +247,8 @@
         input_output_aliases={3 + i: i for i in range(len(kept))},
         compiler_params=params(1),
         cost_estimate=pl.CostEstimate(
-            flops=4 * slots * features * units // parts,
-            bytes_accessed=8 * features * units // parts,
+            flops=4 * slots * steps * wide * units,
+            bytes_accessed=8 * steps * wide * units,
             transcendentals=0,
         ),
     )(rows, gate_grad, up_grad, *kept)
@@ -266,41 +303,42 @@
             [quarters(block, tokens, corner), quarters(block, tokens, 3 - corner)], axis=0
         )
 
-    x_mine, g_mine = fetched(layer_input), fetched(out_grad)
-    x_mine, g_mine, layer_input, out_grad, routes = lax.optimization_barrier(
-        (x_mine, g_mine, layer_input, out_grad, routes)
-    )
+    def onward(across):
+        return (flip(across[:quarter], "dp", 1), flip(across[:quarter], "dp", 2))
+
+    def to_core(values):
+        return tuple(flip(v, "expert", 1) for v in values)
+
+    x_mine = fetched(layer_input)
+    x_mine, layer_input, out_grad, routes = lax.optimization_barrier(
+        (x_mine, layer_input, out_grad, routes)
+    )
+    x_across = flip(x_mine, "expert", 2)
+    x_sibling, g_sibling = flip(layer_input, "expert", 1), flip(out_grad, "expert", 1)
     table = route_table(routes, gate_values)
     tables = []
     for r in range(4):
         part = lax.dynamic_slice_in_dim(table, (me ^ r) * experts, experts, 0)
         tables.append(flip(part, "expert", r) if r > 0 else part)
-    x_across, g_across = flip(x_mine, "expert", 2), flip(g_mine, "expert", 2)
-    x_sibling, g_sibling = flip(layer_input, "expert", 1), flip(out_grad, "expert", 1)
-
-    def onward(across):
-        here = (across, flip(across[:quarter], "dp", 1), flip(across[:quarter], "dp", 2))
-        return (*here, *(flip(v, "expert", 1) for v in here))
-
-    weights = (w_gate, w_up, w_down)
-    near = jnp.stack(tables[:2], axis=2)
-    near_rows = ((layer_input, x_sibling), (out_grad, g_sibling), near, weights)
-    made = slot_grads(*near_rows, None, 0, 1, 0, 2)
-    x_across, tables[2], tables[3], *made = lax.optimization_barrier(
-        (x_across, tables[2], tables[3], *made)
-    )
-    x_far = onward(x_across)
-    made = slot_grads(*near_rows, made, 1, 2, 0, 2, (0, 2))
-    g_across, *made = lax.optimization_barrier((g_across, *made))
-    g_far = onward(g_across)
-    made = slot_grads(*near_rows, made, 1, 2, 0, 2, (1, 2))
-    far = jnp.stack(tables[2:], axis=2)
-    slot_back = jnp.concatenate([near[:, 0], far[:, 0]], axis=1)
-    back = back_matrix(swap_order(slot_back, side, pair, 2))
-    far = swap_order(far, side, pair, 3).reshape(experts, 2, 2, 4, quarter)
+    tables[1], g_mine = lax.optimization_barrier((tables[1], fetched(out_grad)))
+    g_across = flip(g_mine, "expert", 2)
+    x_far = (x_across, *onward(x_across))
+    x_far = (*x_far, *to_core(x_far))
+    *x_far, g_across = lax.optimization_barrier((*x_far, g_across))
+    g_beside = onward(g_across)
+    g_passed = to_core((g_across,))
+    table = jnp.stack(tables, axis=2)
+    back = back_matrix(swap_order(table[:, 0], side, pair, 2))
+    far = swap_order(table[:, :, 2:], side, pair, 3).reshape(experts, 2, 2, 4, quarter)
     far = jnp.stack([far[:, :, :, q] for q in (0, 3, 2, 1)], axis=3)
-    far = far.reshape(experts, 2, 2, tokens)
-    rows, gate_grad, up_grad = slot_grads(x_far, g_far, far, weights, made, 0, experts, 1, 2)
+    table = jnp.concatenate([table[:, :, :2], far.reshape(experts, 2, 2, tokens)], axis=2)
+    slot, weight = table[:, 0], table[:, 1]
+    rows, act, slope = forward((layer_input, x_sibling, *x_far), slot, w_gate, w_up)
+    act, *g_beside = lax.optimization_barrier((act, *g_beside))
+    g_far = (g_across, *g_beside, *g_passed, *to_core(g_beside))
+    gate_grad, up_grad = hidden_grads(
+        (out_grad, g_sibling, *g_far), slot, weight, act, slope, w_down
+    )
 
     groups = ((0, 2), (1, 3))
     kept_a, sent_a = input_sums(back, gate_grad, up_grad, w_gate, w_up, groups, 0, 2)
@@ -321,19 +359,21 @@
     chip_b = [add(a, b) for a, b in zip(cut(kept_b, 8), cut(got, 8))]
     far_a = chip_a[tokens:]
     away = [jnp.concatenate([chip_b[q], chip_b[4 + q]], axis=0) for q in (1, 2, 3)]
-    (far_a, *away), grads = piece((far_a, *away), None, 0)
+    (far_a, *away), grads = piece((far_a, *away), None, 0, 0, 4)
     got_a, got_b = flip(far_a, "expert", 2), corners(away)
     got_a, got_b, *grads = lax.optimization_barrier((got_a, got_b, *grads))
     own_a = [add(a, b) for a, b in zip(cut(chip_a, 4), cut(got_a, 4))]
     mine_b = add(chip_b[0], *(v[:quarter] for v in got_b))
     far_b = add(chip_b[4], *(v[quarter:] for v in got_b))
+    (far_b, *own_a), grads = piece((far_b, *own_a), grads, 0, 4, 2)
     got_a, got_b = corners(own_a[1:]), flip(far_b, "expert", 2)
+    got_a, got_b, *grads = lax.optimization_barrier((got_a, got_b, *grads))
     mine = jnp.concatenate([add(own_a[0], *got_a), add(mine_b, got_b)], axis=1)
-    mine, grads = piece(mine, grads, 1, 0, 2)
+    mine, grads = piece(mine, grads, 1, 0, 3)
     got = flip(mine, "dp", 4)
     got, *grads = lax.optimization_barrier((got, *grads))
     mine = add(mine, got)
-    mine, grads = piece(mine, grads, 1, 1, 2)
+    mine, grads = piece(mine, grads, 1, 3, 3)
     got = corners([mine] * 3)
     got, *grads = lax.optimization_barrier((got, *grads))
     total = swap_order(jnp.concatenate([mine, *got], axis=0), side, pair, 0)
@@ -347,10 +387,9 @@
     grads_in = lax.all_gather(out_grad, "expert", tiled=True)
     table = lax.all_gather(route_table(routes, gate_values), "expert")
     table = lax.dynamic_slice_in_dim(table, me * experts, experts, 1).transpose(1, 2, 0, 3)
-    rows, gate_grad, up_grad = slot_grads(
-        [rows_in], [grads_in], table, (w_gate, w_up, w_down), None, 0, experts, 0, 1
-    )
-    slot = table[:, 0]
+    slot, weight = table[:, 0], table[:, 1]
+    rows, act, slope = forward([rows_in], slot, w_gate, w_up)
+    gate_grad, up_grad = hidden_grads([grads_in], slot, weight, act, slope, w_down)
     groups = (tuple(range(slot.shape[1])),)
     (sums,) = input_sums(back_matrix(slot), gate_grad, up_grad, w_gate, w_up, groups, 0, 1)
     grads = None

time: 137 us -> 126 us (0.920)
  Pallas kernels: 85 us -> 71.9 us
  waiting for transfers between devices: 8.82 us -> 16.7 us
  local copies, waits for them, and re-layouts: 10.3 us -> 3.12 us
    pallas_call x4 -> x2, Pallas kernels: 43.4 us -> 27.7 us  [the longest x1 15.8 us: forward(): pl.pallas_call(functools.partial(forward_kernel, len(pieces)), grid=(expe...]
    ppermute x31, waiting for transfers between devices: 8.82 us -> 16.7 us  [flip(): return lax.ppermute(value, axis, [(i, i ^ bit) for i in range(count)])]
    pallas_call x3 -> x4, Pallas kernels: 23.9 us -> 26.5 us  [weight_grads(): pl.pallas_call(weights_kernel, grid=(steps,), in_specs=[pl.BlockSpec((1,...]
    slice x2, local copies, waits for them, and re-layouts: 2.31 us -> 0.03 us  [onward(): return (flip(across[:quarter], 'dp', 1), flip(across[:quarter], 'dp', 2))]
    eq x4, local copies, waits for them, and re-layouts: 2.55 us -> 0.31 us  [back_matrix(): chosen = slot.transpose(1, 2, 0)[..., None] == places]
  transfers between devices with their start and end apart: 31 -> 31, of which waited for: 11 -> 11; matrix products, arithmetic and copies ran while one was open for 8% -> 2% of each run, Pallas kernels for 42% -> 41%
where the time goes in v3:
time: 126 us; the launch traced here: 125 us
  Pallas kernels  71.9 us (57%)
  starting transfers between devices  28.1 us (22%)
  waiting for transfers between devices  16.7 us (13%)
  other arithmetic  4.3 us (3%)
  local copies, waits for them, and re-layouts  3.12 us (2%)
    ppermute x31, starting transfers between devices, flip(): return lax.ppermute(value, axis, [(i, i ^ bit) for i in range(count)])  28.1 us
    pallas_call x4, Pallas kernels, weight_grads(): pl.pallas_call(weights_kernel, grid=(steps,), in_specs=[pl.BlockSpec((1,...  26.5 us
    pallas_call x2, Pallas kernels, input_sums(): pl.pallas_call(functools.partial(inputs_kernel, groups), grid=(steps,), i...  17.7 us
    ppermute x31, waiting for transfers between devices, flip(): return lax.ppermute(value, axis, [(i, i ^ bit) for i in range(count)])  16.7 us
    pallas_call x1, Pallas kernels, forward(): pl.pallas_call(functools.partial(forward_kernel, len(pieces)), grid=(expe...  15.8 us
    pallas_call x1, Pallas kernels, hidden_grads(): pl.pallas_call(functools.partial(hidden_kernel, len(pieces)), grid=(exper...  11.9 us
  transfers between devices with their start and end apart: 31, of which 11 were waited for; matrix products, arithmetic and copies ran while one was open for 2% of the time, Pallas kernels for 41%

profile of v3, /device:TPU:0, one launch (start us, length us, event | category | flops | bytes accessed | tf_op | source)
XLA Modules:
  0.0 125.3 jit_solution(13555333583759648010)
XLA Ops:
  0.7 1.1 constant_dynamic-slice_fusion.3
  1.9 0.7 fusion.1
  2.7 0.7 select_reduce_fusion
  3.4 3.0 %collective-permute-start.1 = (f32[2,2,128]{2,0,1:T(2,128)S(1)}, f32[2,2,128]{2,0,1:T(2,128)S(1)}, u32[]{:S(2)}, u32[]{:S(2)}) collective-permute-start(f32[2,2,128]{2,0,1:T(2,128)S(1)} %get-tuple-element.159), channel_id=1, source_target_pairs={{0,2},{1,3},{2,0},{3,1},{4,6},{5,7},{6,4},{7,5},{8,10},{9,11},{10,... | collective-permute-start | bytes 6152 | tf_op jit(solution)/shard_map/ppermute | solution.py:271
  6.5 0.2 collective-permute-start.2
  6.7 1.9 %collective-permute-start.4 = (bf16[64,3072]{1,0:T(8,128)(2,1)S(1)}, bf16[64,3072]{1,0:T(8,128)(2,1)S(1)}, u32[]{:S(2)}, u32[]{:S(2)}) collective-permute-start(bf16[64,3072]{1,0:T(8,128)(2,1)S(1)} %pad_maximum_fusion.1), channel_id=1, source_target_pairs={{0,2},{1,3},{2,0},{3,1},{4,6},{5,7},{6,4},{7,5},{8,10},{9,11},{10,... | collective-permute-start | bytes 1179656 | tf_op jit(solution)/shard_map/ppermute | solution.py:271
  8.6 1.0 constant_dynamic-slice_fusion.1
  9.6 0.8 pad_maximum_fusion.2
  11.0 0.2 collective-permute-start.10
  11.2 7.4 %collective-permute-done.4.refs_2_ = bf16[64,3072]{1,0:T(8,128)(2,1)S(1)} collective-permute-done((bf16[64,3072]{1,0:T(8,128)(2,1)S(1)}, bf16[64,3072]{1,0:T(8,128)(2,1)S(1)}, u32[]{:S(2)}, u32[]{:S(2)}) %collective-permute-start.4) | collective-permute-done | bytes 393248 | tf_op jit(solution)/shard_map/ppermute | solution.py:271
  18.6 2.1 %collective-permute-start.6 = (bf16[32,3072]{1,0:T(8,128)(2,1)S(1)}, bf16[32,3072]{1,0:T(8,128)(2,1)S(1)}, u32[]{:S(2)}, u32[]{:S(2)}) collective-permute-start(bf16[32,3072]{1,0:T(8,128)(2,1)S(1)} %slice.168), channel_id=1, source_target_pairs={{0,8},{4,12},{8,0},{12,4},{16,24},{20,28},{24,16},{28,20},{1,9},{5... | collective-permute-start | bytes 589832 | tf_op jit(solution)/shard_map/ppermute | solution.py:271
  20.7 1.5 %collective-permute-start.5 = (bf16[32,3072]{1,0:T(8,128)(2,1)S(1)}, bf16[32,3072]{1,0:T(8,128)(2,1)S(1)}, u32[]{:S(2)}, u32[]{:S(2)}) collective-permute-start(bf16[32,3072]{1,0:T(8,128)(2,1)S(1)} %slice.168), channel_id=1, source_target_pairs={{0,4},{4,0},{8,12},{12,8},{16,20},{20,16},{24,28},{28,24},{1,5},{5... | collective-permute-start | bytes 589832 | tf_op jit(solution)/shard_map/ppermute | solution.py:271
  22.7 1.8 %collective-permute-done.6.refs_4_ = bf16[32,3072]{1,0:T(8,128)(2,1)S(1)} collective-permute-done((bf16[32,3072]{1,0:T(8,128)(2,1)S(1)}, bf16[32,3072]{1,0:T(8,128)(2,1)S(1)}, u32[]{:S(2)}, u32[]{:S(2)}) %collective-permute-start.6) | collective-permute-done | bytes 196640 | tf_op jit(solution)/shard_map/ppermute | solution.py:271
  24.5 1.9 %collective-permute-done.5.refs_3_ = bf16[32,3072]{1,0:T(8,128)(2,1)S(1)} collective-permute-done((bf16[32,3072]{1,0:T(8,128)(2,1)S(1)}, bf16[32,3072]{1,0:T(8,128)(2,1)S(1)}, u32[]{:S(2)}, u32[]{:S(2)}) %collective-permute-start.5) | collective-permute-done | bytes 196640 | tf_op jit(solution)/shard_map/ppermute | solution.py:271
  26.5 0.5 collective-permute-start.3
  27.0 0.9 collective-permute-done.8.refs_6_
  27.9 0.4 collective-permute-start.13
  28.2 1.6 %collective-permute-start.12 = (bf16[32,3072]{1,0:T(8,128)(2,1)S(1)}, bf16[32,3072]{1,0:T(8,128)(2,1)S(1)}, u32[]{:S(2)}, u32[]{:S(2)}) collective-permute-start(bf16[32,3072]{1,0:T(8,128)(2,1)S(1)} %slice.133), channel_id=1, source_target_pairs={{0,4},{4,0},{8,12},{12,8},{16,20},{20,16},{24,28},{28,24},{1,5},{5... | collective-permute-start | bytes 589832 | tf_op jit(solution)/shard_map/ppermute | solution.py:271
  29.9 15.8 %shard_map.94 = (bf16[2,320,3072]{2,1,0:T(8,128)(2,1)}, f32[2,320,1024]{2,1,0:T(8,128)}, f32[2,320,1024]{2,1,0:T(8,128)}) custom-call(bf16[128,3072]{1,0:T(8,128)(2,1)} %refs_0_, bf16[128,3072]{1,0:T(8,128)(2,1)} %collective-permute-done.11.refs_1_, bf16[64,3072]{1,0:T(8,128)(2,1)S(1)} %collective-permute-done.4.refs_2_, ...), custom_call_target="tpu_custom_call" | custom-call | flops 8053063680 | bytes 25165824 | tf_op jit(solution)/shard_map/pallas_call | solution.py:122
  45.7 0.6 collective-permute-start.15
  46.4 0.9 collective-permute-done.15.refs_6_
  47.3 0.4 collective-permute-done.16.refs_7_
  47.7 11.9 %shard_map.95 = (bf16[2,320,1024]{2,1,0:T(8,128)(2,1)}, bf16[2,320,1024]{2,1,0:T(8,128)(2,1)}) custom-call(bf16[128,3072]{1,0:T(8,128)(2,1)} %refs_0_.1, bf16[128,3072]{1,0:T(8,128)(2,1)} %copy-done.2, bf16[64,3072]{1,0:T(8,128)(2,1)S(1)} %collective-permute-done.10.refs_2_, bf16[32,3072]{1,0:T(8,128)(2,1)S(1)} %collective-permute-done.12.refs_3_, ...), custom_call_target="tpu_custom_call" | custom-call | flops 4026531840 | bytes 12582912 | tf_op jit(solution)/shard_map/pallas_call | solution.py:163
  59.6 8.9 %shard_map.97 = (bf16[256,1536]{1,0:T(8,128)(2,1)S(1)}, bf16[256,1536]{1,0:T(8,128)(2,1)S(1)}) custom-call(bf16[4,128,160]{2,1,0:T(8,128)(2,1)S(1)} %compare_convert_fusion.back, bf16[2,320,1024]{2,1,0:T(8,128)(2,1)} %get-tuple-element.89.gate_grad, bf16[2,320,1024]{2,1,0:T(8,128)(2,1)} %get-tuple-element.90.up_grad, bf16[2,3072,1024]{2,1,0:T(8,128)(2,1)} %w_gate.3, ...), custom_call_target="tpu_custom_call" | custom-call | flops 4026531840 | bytes 12582912 | tf_op jit(solution)/shard_map/pallas_call | solution.py:200
  68.5 0.3 collective-permute-start.18
  68.8 8.8 %shard_map.96 = (bf16[256,1536]{1,0:T(8,128)(2,1)S(1)}, bf16[256,1536]{1,0:T(8,128)(2,1)S(1)}) custom-call(bf16[4,128,160]{2,1,0:T(8,128)(2,1)S(1)} %compare_convert_fusion.back, bf16[2,320,1024]{2,1,0:T(8,128)(2,1)} %get-tuple-element.89.gate_grad, bf16[2,320,1024]{2,1,0:T(8,128)(2,1)} %get-tuple-element.90.up_grad, bf16[2,3072,1024]{2,1,0:T(8,128)(2,1)} %w_gate.3, ...), custom_call_target="tpu_custom_call" | custom-call | flops 4026531840 | bytes 12582912 | tf_op jit(solution)/shard_map/pallas_call | solution.py:200
  77.7 0.3 collective-permute-start.17
  78.2 1.8 %collective-permute-done.17 = bf16[256,1536]{1,0:T(8,128)(2,1)S(1)} collective-permute-done((bf16[256,1536]{1,0:T(8,128)(2,1)S(1)}, bf16[256,1536]{1,0:T(8,128)(2,1)S(1)}, u32[]{:S(2)}, u32[]{:S(2)}) %collective-permute-start.17) | collective-permute-done | bytes 786464 | tf_op jit(solution)/shard_map/ppermute | solution.py:271
  80.3 1.6 %collective-permute-start.19 = (bf16[128,1536]{1,0:T(8,128)(2,1)S(1)}, bf16[128,1536]{1,0:T(8,128)(2,1)S(1)}, u32[]{:S(2)}, u32[]{:S(2)}) collective-permute-start(bf16[128,1536]{1,0:T(8,128)(2,1)S(1)} %slice.176), channel_id=1, source_target_pairs={{0,2},{1,3},{2,0},{3,1},{4,6},{5,7},{6,4},{7,5},{8,10},{9,11},{10,... | collective-permute-start | bytes 1179656 | tf_op jit(solution)/shard_map/ppermute | solution.py:271
  81.8 1.6 %collective-permute-start.20 = (bf16[64,1536]{1,0:T(8,128)(2,1)S(1)}, bf16[64,1536]{1,0:T(8,128)(2,1)S(1)}, u32[]{:S(2)}, u32[]{:S(2)}) collective-permute-start(bf16[64,1536]{1,0:T(8,128)(2,1)S(1)} %get-tuple-element.97), channel_id=1, source_target_pairs={{0,8},{4,12},{8,0},{12,4},{16,24},{20,28},{24,16},{28,20},{1,9},{5... | collective-permute-start | bytes 589832 | tf_op jit(solution)/shard_map/ppermute | solution.py:271
  83.4 0.5 collective-permute-start.21
  83.9 1.4 %collective-permute-start.22 = (bf16[64,1536]{1,0:T(8,128)(2,1)S(1)}, bf16[64,1536]{1,0:T(8,128)(2,1)S(1)}, u32[]{:S(2)}, u32[]{:S(2)}) collective-permute-start(bf16[64,1536]{1,0:T(8,128)(2,1)S(1)} %pad_maximum_fusion.5), channel_id=1, source_target_pairs={{0,12},{4,8},{8,4},{12,0},{16,28},{20,24},{24,20},{28,16},{1,13},{... | collective-permute-start | bytes 589832 | tf_op jit(solution)/shard_map/ppermute | solution.py:271
  85.3 8.0 %shard_map.98 = (f32[2,3072,1024]{2,1,0:T(8,128)}, f32[2,3072,1024]{2,1,0:T(8,128)}) custom-call(bf16[2,320,3072]{2,1,0:T(8,128)(2,1)} %get-tuple-element.129.rows, bf16[2,320,1024]{2,1,0:T(8,128)(2,1)S(1)} %copy-done, bf16[2,320,1024]{2,1,0:T(8,128)(2,1)} %get-tuple-element.90.up_grad), custom_call_target="tpu_custom_call" | custom-call | flops 2684354560 | bytes 16777216 | tf_op jit(solution)/shard_map/pallas_call | solution.py:238
  93.3 0.8 collective-permute-done.21
  94.3 0.9 collective-permute-start.23
  95.1 0.9 collective-permute-start.24
  96.1 1.8 %collective-permute-start.25 = (bf16[32,1536]{1,0:T(8,128)(2,1)S(1)}, bf16[32,1536]{1,0:T(8,128)(2,1)S(1)}, u32[]{:S(2)}, u32[]{:S(2)}) collective-permute-start(bf16[32,1536]{1,0:T(8,128)(2,1)S(1)} %get-tuple-element.110), channel_id=1, source_target_pairs={{0,12},{4,8},{8,4},{12,0},{16,28},{20,24},{24,20},{28,16},{1,13},{... | collective-permute-start | bytes 294920 | tf_op jit(solution)/shard_map/ppermute | solution.py:271
  97.8 0.5 collective-permute-start.26
  98.3 5.3 %shard_map.99 = (f32[2,3072,1024]{2,1,0:T(8,128)}, f32[2,3072,1024]{2,1,0:T(8,128)}) custom-call(bf16[2,320,3072]{2,1,0:T(8,128)(2,1)} %get-tuple-element.129.rows, bf16[2,320,1024]{2,1,0:T(8,128)(2,1)S(1)} %copy-done, bf16[2,320,1024]{2,1,0:T(8,128)(2,1)} %get-tuple-element.90.up_grad, ...), custom_call_target="tpu_custom_call", output_to_operand_aliasing={{0}: (3, {}), {1}: (4, {})} | custom-call | flops 1342177280 | bytes 8388608 | tf_op jit(solution)/shard_map/pallas_call | solution.py:238
  103.8 2.7 %collective-permute-start.27 = (bf16[32,3072]{1,0:T(8,128)(2,1)S(1)}, bf16[32,3072]{1,0:T(8,128)(2,1)S(1)}, u32[]{:S(2)}, u32[]{:S(2)}) collective-permute-start(bf16[32,3072]{1,0:T(8,128)(2,1)S(1)} %pad_maximum_fusion.6), channel_id=1, source_target_pairs={{0,16},{4,20},{8,24},{12,28},{16,0},{20,4},{24,8},{28,12},{1,17},{... | collective-permute-start | bytes 589832 | tf_op jit(solution)/shard_map/ppermute | solution.py:271
  106.5 6.6 %shard_map.100 = (f32[2,3072,1024]{2,1,0:T(8,128)}, f32[2,3072,1024]{2,1,0:T(8,128)}) custom-call(bf16[2,320,3072]{2,1,0:T(8,128)(2,1)} %get-tuple-element.129.rows, bf16[2,320,1024]{2,1,0:T(8,128)(2,1)S(1)} %copy-done, bf16[2,320,1024]{2,1,0:T(8,128)(2,1)} %get-tuple-element.90.up_grad, ...), custom_call_target="tpu_custom_call", output_to_operand_aliasing={{0}: (3, {}), {1}: (4, {})} | custom-call | flops 2013265920 | bytes 12582912 | tf_op jit(solution)/shard_map/pallas_call | solution.py:238
  113.1 0.3 collective-permute-done.27
  113.5 0.9 collective-permute-start.30
  114.4 1.1 collective-permute-start.29
  115.4 1.6 %collective-permute-start.28 = (bf16[32,3072]{1,0:T(8,128)(2,1)S(1)}, bf16[32,3072]{1,0:T(8,128)(2,1)S(1)}, u32[]{:S(2)}, u32[]{:S(2)}) collective-permute-start(bf16[32,3072]{1,0:T(8,128)(2,1)S(1)} %add_convert_fusion.1), channel_id=1, source_target_pairs={{0,8},{4,12},{8,0},{12,4},{16,24},{20,28},{24,16},{28,20},{1,9},{5... | collective-permute-start | bytes 589832 | tf_op jit(solution)/shard_map/ppermute | solution.py:271
  117.0 6.6 %shard_map.101 = (f32[2,3072,1024]{2,1,0:T(8,128)}, f32[2,3072,1024]{2,1,0:T(8,128)}) custom-call(bf16[2,320,3072]{2,1,0:T(8,128)(2,1)} %get-tuple-element.129.rows, bf16[2,320,1024]{2,1,0:T(8,128)(2,1)S(1)} %copy-done, bf16[2,320,1024]{2,1,0:T(8,128)(2,1)} %get-tuple-element.90.up_grad, ...), custom_call_target="tpu_custom_call", output_to_operand_aliasing={{0}: (3, {}), {1}: (4, {})} | custom-call | flops 2013265920 | bytes 12582912 | tf_op jit(solution)/shard_map/pallas_call | solution.py:238
  123.7 0.4 collective-permute-done.29
  124.3 1.0 reverse_select_fusion
  (77 shorter events, 2.4 us)
Async XLA Ops:
  0.7 25.8 %copy-start.1 = (bf16[128,3072]{1,0:T(8,128)(2,1)S(1)}, bf16[128,3072]{1,0:T(8,128)(2,1)}, u32[]{:S(2)}) copy-start(bf16[128,3072]{1,0:T(8,128)(2,1)} %refs_0_.1) | copy-start | bytes 2359300
  3.4 7.1 %collective-permute-start.1 = (f32[2,2,128]{2,0,1:T(2,128)S(1)}, f32[2,2,128]{2,0,1:T(2,128)S(1)}, u32[]{:S(2)}, u32[]{:S(2)}) collective-permute-start(f32[2,2,128]{2,0,1:T(2,128)S(1)} %get-tuple-element.159), channel_id=1, source_target_pairs={{0,2},{1,3},{2,0},{3,1},{4,6},{5,7},{6,4},{7,5},{8,10},{9,11},{10,... | collective-permute-start | bytes 6152 | tf_op jit(solution)/shard_map/ppermute | solution.py:271
  6.5 4.4 %collective-permute-start = (f32[2,2,128]{2,0,1:T(2,128)S(1)}, f32[2,2,128]{2,0,1:T(2,128)S(1)}, u32[]{:S(2)}, u32[]{:S(2)}) collective-permute-start(f32[2,2,128]{2,0,1:T(2,128)S(1)} %get-tuple-element.161), channel_id=1, source_target_pairs={{0,1},{1,0},{2,3},{3,2},{4,5},{5,4},{6,7},{7,6},{8,9},{9,8},{10,11... | collective-permute-start | bytes 6152 | tf_op jit(solution)/shard_map/ppermute | solution.py:271
  6.5 4.2 %collective-permute-start.2 = (f32[2,2,128]{2,0,1:T(2,128)S(1)}, f32[2,2,128]{2,0,1:T(2,128)S(1)}, u32[]{:S(2)}, u32[]{:S(2)}) collective-permute-start(f32[2,2,128]{2,0,1:T(2,128)S(1)} %get-tuple-element.162), channel_id=1, source_target_pairs={{0,3},{1,2},{2,1},{3,0},{4,7},{5,6},{6,5},{7,4},{8,11},{9,10},{10,... | collective-permute-start | bytes 6152 | tf_op jit(solution)/shard_map/ppermute | solution.py:271
  6.7 11.9 %collective-permute-start.4 = (bf16[64,3072]{1,0:T(8,128)(2,1)S(1)}, bf16[64,3072]{1,0:T(8,128)(2,1)S(1)}, u32[]{:S(2)}, u32[]{:S(2)}) collective-permute-start(bf16[64,3072]{1,0:T(8,128)(2,1)S(1)} %pad_maximum_fusion.1), channel_id=1, source_target_pairs={{0,2},{1,3},{2,0},{3,1},{4,6},{5,7},{6,4},{7,5},{8,10},{9,11},{10,... | collective-permute-start | bytes 1179656 | tf_op jit(solution)/shard_map/ppermute | solution.py:271
  8.6 21.3 %collective-permute-start.11 = (bf16[128,3072]{1,0:T(8,128)(2,1)}, bf16[128,3072]{1,0:T(8,128)(2,1)}, u32[]{:S(2)}, u32[]{:S(2)}) collective-permute-start(bf16[128,3072]{1,0:T(8,128)(2,1)} %refs_0_), channel_id=1, source_target_pairs={{0,1},{1,0},{2,3},{3,2},{4,5},{5,4},{6,7},{7,6},{8,9},{9,8},{10,11... | collective-permute-start | bytes 2359304 | tf_op jit(solution)/shard_map/ppermute | solution.py:271
  11.0 15.5 %collective-permute-start.10 = (bf16[64,3072]{1,0:T(8,128)(2,1)}, bf16[64,3072]{1,0:T(8,128)(2,1)S(1)}, u32[]{:S(2)}, u32[]{:S(2)}) collective-permute-start(bf16[64,3072]{1,0:T(8,128)(2,1)} %pad_maximum_fusion.2), channel_id=1, source_target_pairs={{0,2},{1,3},{2,0},{3,1},{4,6},{5,7},{6,4},{7,5},{8,10},{9,11},{10,... | collective-permute-start | bytes 1179656 | tf_op jit(solution)/shard_map/ppermute | solution.py:271
  18.6 5.9 %collective-permute-start.6 = (bf16[32,3072]{1,0:T(8,128)(2,1)S(1)}, bf16[32,3072]{1,0:T(8,128)(2,1)S(1)}, u32[]{:S(2)}, u32[]{:S(2)}) collective-permute-start(bf16[32,3072]{1,0:T(8,128)(2,1)S(1)} %slice.168), channel_id=1, source_target_pairs={{0,8},{4,12},{8,0},{12,4},{16,24},{20,28},{24,16},{28,20},{1,9},{5... | collective-permute-start | bytes 589832 | tf_op jit(solution)/shard_map/ppermute | solution.py:271
  20.7 5.7 %collective-permute-start.5 = (bf16[32,3072]{1,0:T(8,128)(2,1)S(1)}, bf16[32,3072]{1,0:T(8,128)(2,1)S(1)}, u32[]{:S(2)}, u32[]{:S(2)}) collective-permute-start(bf16[32,3072]{1,0:T(8,128)(2,1)S(1)} %slice.168), channel_id=1, source_target_pairs={{0,4},{4,0},{8,12},{12,8},{16,20},{20,16},{24,28},{28,24},{1,5},{5... | collective-permute-start | bytes 589832 | tf_op jit(solution)/shard_map/ppermute | solution.py:271
  22.2 5.6 %collective-permute-start.7 = (bf16[64,3072]{1,0:T(8,128)(2,1)S(1)}, bf16[64,3072]{1,0:T(8,128)(2,1)S(1)}, u32[]{:S(2)}, u32[]{:S(2)}) collective-permute-start(bf16[64,3072]{1,0:T(8,128)(2,1)S(1)} %collective-permute-done.4.refs_2_), channel_id=1, source_target_pairs={{0,1},{1,0},{2,3},{3,2},{4,5},{5,4},{6,7},{7,6},{8,9},{9,8},{10,11... | collective-permute-start | bytes 1179656 | tf_op jit(solution)/shard_map/ppermute | solution.py:271
  24.5 2.5 %collective-permute-start.9 = (bf16[32,3072]{1,0:T(8,128)(2,1)S(1)}, bf16[32,3072]{1,0:T(8,128)(2,1)S(1)}, u32[]{:S(2)}, u32[]{:S(2)}) collective-permute-start(bf16[32,3072]{1,0:T(8,128)(2,1)S(1)} %collective-permute-done.6.refs_4_), channel_id=1, source_target_pairs={{0,1},{1,0},{2,3},{3,2},{4,5},{5,4},{6,7},{7,6},{8,9},{9,8},{10,11... | collective-permute-start | bytes 589832 | tf_op jit(solution)/shard_map/ppermute | solution.py:271
  26.4 1.4 %collective-permute-start.8 = (bf16[32,3072]{1,0:T(8,128)(2,1)S(1)}, bf16[32,3072]{1,0:T(8,128)(2,1)S(1)}, u32[]{:S(2)}, u32[]{:S(2)}) collective-permute-start(bf16[32,3072]{1,0:T(8,128)(2,1)S(1)} %collective-permute-done.5.refs_3_), channel_id=1, source_target_pairs={{0,1},{1,0},{2,3},{3,2},{4,5},{5,4},{6,7},{7,6},{8,9},{9,8},{10,11... | collective-permute-start | bytes 589832 | tf_op jit(solution)/shard_map/ppermute | solution.py:271
  26.5 19.9 %collective-permute-start.3 = (bf16[128,3072]{1,0:T(8,128)(2,1)S(1)}, bf16[128,3072]{1,0:T(8,128)(2,1)S(1)}, u32[]{:S(2)}, u32[]{:S(2)}) collective-permute-start(bf16[128,3072]{1,0:T(8,128)(2,1)S(1)} %copy-done.1), channel_id=1, source_target_pairs={{0,1},{1,0},{2,3},{3,2},{4,5},{5,4},{6,7},{7,6},{8,9},{9,8},{10,11... | collective-permute-start | bytes 2359304 | tf_op jit(solution)/shard_map/ppermute | solution.py:271
  27.9 17.8 %collective-permute-start.13 = (bf16[32,3072]{1,0:T(8,128)(2,1)S(1)}, bf16[32,3072]{1,0:T(8,128)(2,1)S(1)}, u32[]{:S(2)}, u32[]{:S(2)}) collective-permute-start(bf16[32,3072]{1,0:T(8,128)(2,1)S(1)} %slice.133), channel_id=1, source_target_pairs={{0,8},{4,12},{8,0},{12,4},{16,24},{20,28},{24,16},{28,20},{1,9},{5... | collective-permute-start | bytes 589832 | tf_op jit(solution)/shard_map/ppermute | solution.py:271
  28.2 17.4 %collective-permute-start.12 = (bf16[32,3072]{1,0:T(8,128)(2,1)S(1)}, bf16[32,3072]{1,0:T(8,128)(2,1)S(1)}, u32[]{:S(2)}, u32[]{:S(2)}) collective-permute-start(bf16[32,3072]{1,0:T(8,128)(2,1)S(1)} %slice.133), channel_id=1, source_target_pairs={{0,4},{4,0},{8,12},{12,8},{16,20},{20,16},{24,28},{28,24},{1,5},{5... | collective-permute-start | bytes 589832 | tf_op jit(solution)/shard_map/ppermute | solution.py:271
  29.9 16.6 %collective-permute-start.14 = (bf16[64,3072]{1,0:T(8,128)(2,1)S(1)}, bf16[64,3072]{1,0:T(8,128)(2,1)S(1)}, u32[]{:S(2)}, u32[]{:S(2)}) collective-permute-start(bf16[64,3072]{1,0:T(8,128)(2,1)S(1)} %collective-permute-done.10.refs_2_), channel_id=1, source_target_pairs={{0,1},{1,0},{2,3},{3,2},{4,5},{5,4},{6,7},{7,6},{8,9},{9,8},{10,11... | collective-permute-start | bytes 1179656 | tf_op jit(solution)/shard_map/ppermute | solution.py:271
  45.7 1.6 %collective-permute-start.15 = (bf16[32,3072]{1,0:T(8,128)(2,1)S(1)}, bf16[32,3072]{1,0:T(8,128)(2,1)S(1)}, u32[]{:S(2)}, u32[]{:S(2)}) collective-permute-start(bf16[32,3072]{1,0:T(8,128)(2,1)S(1)} %collective-permute-done.12.refs_3_), channel_id=1, source_target_pairs={{0,1},{1,0},{2,3},{3,2},{4,5},{5,4},{6,7},{7,6},{8,9},{9,8},{10,11... | collective-permute-start | bytes 589832 | tf_op jit(solution)/shard_map/ppermute | solution.py:271
  46.3 1.4 %collective-permute-start.16 = (bf16[32,3072]{1,0:T(8,128)(2,1)S(1)}, bf16[32,3072]{1,0:T(8,128)(2,1)S(1)}, u32[]{:S(2)}, u32[]{:S(2)}) collective-permute-start(bf16[32,3072]{1,0:T(8,128)(2,1)S(1)} %collective-permute-done.13.refs_4_), channel_id=1, source_target_pairs={{0,1},{1,0},{2,3},{3,2},{4,5},{5,4},{6,7},{7,6},{8,9},{9,8},{10,11... | collective-permute-start | bytes 589832 | tf_op jit(solution)/shard_map/ppermute | solution.py:271
  46.4 1.3 %copy-start.2 = (bf16[128,3072]{1,0:T(8,128)(2,1)}, bf16[128,3072]{1,0:T(8,128)(2,1)S(1)}, u32[]{:S(2)}) copy-start(bf16[128,3072]{1,0:T(8,128)(2,1)S(1)} %collective-permute-done.3.refs_1_) | copy-start | bytes 2359300
  68.5 9.5 %collective-permute-start.18 = (bf16[256,1536]{1,0:T(8,128)(2,1)S(1)}, bf16[256,1536]{1,0:T(8,128)(2,1)S(1)}, u32[]{:S(2)}, u32[]{:S(2)}) collective-permute-start(bf16[256,1536]{1,0:T(8,128)(2,1)S(1)} %get-tuple-element.94), channel_id=1, source_target_pairs={{0,1},{1,0},{2,3},{3,2},{4,5},{5,4},{6,7},{7,6},{8,9},{9,8},{10,11... | collective-permute-start | bytes 2359304 | tf_op jit(solution)/shard_map/ppermute | solution.py:271
  77.7 2.4 %collective-permute-start.17 = (bf16[256,1536]{1,0:T(8,128)(2,1)S(1)}, bf16[256,1536]{1,0:T(8,128)(2,1)S(1)}, u32[]{:S(2)}, u32[]{:S(2)}) collective-permute-start(bf16[256,1536]{1,0:T(8,128)(2,1)S(1)} %get-tuple-element.92), channel_id=1, source_target_pairs={{0,1},{1,0},{2,3},{3,2},{4,5},{5,4},{6,7},{7,6},{8,9},{9,8},{10,11... | collective-permute-start | bytes 2359304 | tf_op jit(solution)/shard_map/ppermute | solution.py:271
  78.0 7.3 %copy-start = (bf16[2,320,1024]{2,1,0:T(8,128)(2,1)S(1)}, bf16[2,320,1024]{2,1,0:T(8,128)(2,1)}, u32[]{:S(2)}) copy-start(bf16[2,320,1024]{2,1,0:T(8,128)(2,1)} %get-tuple-element.89.gate_grad) | copy-start | bytes 3932164
  80.3 13.8 %collective-permute-start.19 = (bf16[128,1536]{1,0:T(8,128)(2,1)S(1)}, bf16[128,1536]{1,0:T(8,128)(2,1)S(1)}, u32[]{:S(2)}, u32[]{:S(2)}) collective-permute-start(bf16[128,1536]{1,0:T(8,128)(2,1)S(1)} %slice.176), channel_id=1, source_target_pairs={{0,2},{1,3},{2,0},{3,1},{4,6},{5,7},{6,4},{7,5},{8,10},{9,11},{10,... | collective-permute-start | bytes 1179656 | tf_op jit(solution)/shard_map/ppermute | solution.py:271
  81.8 11.4 %collective-permute-start.20 = (bf16[64,1536]{1,0:T(8,128)(2,1)S(1)}, bf16[64,1536]{1,0:T(8,128)(2,1)S(1)}, u32[]{:S(2)}, u32[]{:S(2)}) collective-permute-start(bf16[64,1536]{1,0:T(8,128)(2,1)S(1)} %get-tuple-element.97), channel_id=1, source_target_pairs={{0,8},{4,12},{8,0},{12,4},{16,24},{20,28},{24,16},{28,20},{1,9},{5... | collective-permute-start | bytes 589832 | tf_op jit(solution)/shard_map/ppermute | solution.py:271
  83.4 10.7 %collective-permute-start.21 = (bf16[64,1536]{1,0:T(8,128)(2,1)S(1)}, bf16[64,1536]{1,0:T(8,128)(2,1)S(1)}, u32[]{:S(2)}, u32[]{:S(2)}) collective-permute-start(bf16[64,1536]{1,0:T(8,128)(2,1)S(1)} %get-tuple-element.98), channel_id=1, source_target_pairs={{0,4},{4,0},{8,12},{12,8},{16,20},{20,16},{24,28},{28,24},{1,5},{5... | collective-permute-start | bytes 589832 | tf_op jit(solution)/shard_map/ppermute | solution.py:271
  83.9 10.2 %collective-permute-start.22 = (bf16[64,1536]{1,0:T(8,128)(2,1)S(1)}, bf16[64,1536]{1,0:T(8,128)(2,1)S(1)}, u32[]{:S(2)}, u32[]{:S(2)}) collective-permute-start(bf16[64,1536]{1,0:T(8,128)(2,1)S(1)} %pad_maximum_fusion.5), channel_id=1, source_target_pairs={{0,12},{4,8},{8,4},{12,0},{16,28},{20,24},{24,20},{28,16},{1,13},{... | collective-permute-start | bytes 589832 | tf_op jit(solution)/shard_map/ppermute | solution.py:271
  94.3 9.3 %collective-permute-start.23 = (bf16[32,1536]{1,0:T(8,128)(2,1)S(1)}, bf16[32,1536]{1,0:T(8,128)(2,1)S(1)}, u32[]{:S(2)}, u32[]{:S(2)}) collective-permute-start(bf16[32,1536]{1,0:T(8,128)(2,1)S(1)} %get-tuple-element.108), channel_id=1, source_target_pairs={{0,8},{4,12},{8,0},{12,4},{16,24},{20,28},{24,16},{28,20},{1,9},{5... | collective-permute-start | bytes 294920 | tf_op jit(solution)/shard_map/ppermute | solution.py:271
  95.1 8.5 %collective-permute-start.24 = (bf16[32,1536]{1,0:T(8,128)(2,1)S(1)}, bf16[32,1536]{1,0:T(8,128)(2,1)S(1)}, u32[]{:S(2)}, u32[]{:S(2)}) collective-permute-start(bf16[32,1536]{1,0:T(8,128)(2,1)S(1)} %get-tuple-element.109), channel_id=1, source_target_pairs={{0,4},{4,0},{8,12},{12,8},{16,20},{20,16},{24,28},{28,24},{1,5},{5... | collective-permute-start | bytes 294920 | tf_op jit(solution)/shard_map/ppermute | solution.py:271
  96.1 7.5 %collective-permute-start.25 = (bf16[32,1536]{1,0:T(8,128)(2,1)S(1)}, bf16[32,1536]{1,0:T(8,128)(2,1)S(1)}, u32[]{:S(2)}, u32[]{:S(2)}) collective-permute-start(bf16[32,1536]{1,0:T(8,128)(2,1)S(1)} %get-tuple-element.110), channel_id=1, source_target_pairs={{0,12},{4,8},{8,4},{12,0},{16,28},{20,24},{24,20},{28,16},{1,13},{... | collective-permute-start | bytes 294920 | tf_op jit(solution)/shard_map/ppermute | solution.py:271
  97.8 5.8 %collective-permute-start.26 = (bf16[32,1536]{1,0:T(8,128)(2,1)S(1)}, bf16[32,1536]{1,0:T(8,128)(2,1)S(1)}, u32[]{:S(2)}, u32[]{:S(2)}) collective-permute-start(bf16[32,1536]{1,0:T(8,128)(2,1)S(1)} %add_convert_fusion.10), channel_id=1, source_target_pairs={{0,2},{1,3},{2,0},{3,1},{4,6},{5,7},{6,4},{7,5},{8,10},{9,11},{10,... | collective-permute-start | bytes 294920 | tf_op jit(solution)/shard_map/ppermute | solution.py:271
  103.8 9.6 %collective-permute-start.27 = (bf16[32,3072]{1,0:T(8,128)(2,1)S(1)}, bf16[32,3072]{1,0:T(8,128)(2,1)S(1)}, u32[]{:S(2)}, u32[]{:S(2)}) collective-permute-start(bf16[32,3072]{1,0:T(8,128)(2,1)S(1)} %pad_maximum_fusion.6), channel_id=1, source_target_pairs={{0,16},{4,20},{8,24},{12,28},{16,0},{20,4},{24,8},{28,12},{1,17},{... | collective-permute-start | bytes 589832 | tf_op jit(solution)/shard_map/ppermute | solution.py:271
  113.5 10.2 %collective-permute-start.30 = (bf16[32,3072]{1,0:T(8,128)(2,1)S(1)}, bf16[32,3072]{1,0:T(8,128)(2,1)S(1)}, u32[]{:S(2)}, u32[]{:S(2)}) collective-permute-start(bf16[32,3072]{1,0:T(8,128)(2,1)S(1)} %add_convert_fusion.1), channel_id=1, source_target_pairs={{0,12},{4,8},{8,4},{12,0},{16,28},{20,24},{24,20},{28,16},{1,13},{... | collective-permute-start | bytes 589832 | tf_op jit(solution)/shard_map/ppermute | solution.py:271
  114.4 9.7 %collective-permute-start.29 = (bf16[32,3072]{1,0:T(8,128)(2,1)S(1)}, bf16[32,3072]{1,0:T(8,128)(2,1)S(1)}, u32[]{:S(2)}, u32[]{:S(2)}) collective-permute-start(bf16[32,3072]{1,0:T(8,128)(2,1)S(1)} %add_convert_fusion.1), channel_id=1, source_target_pairs={{0,4},{4,0},{8,12},{12,8},{16,20},{20,16},{24,28},{28,24},{1,5},{5... | collective-permute-start | bytes 589832 | tf_op jit(solution)/shard_map/ppermute | solution.py:271
  115.4 8.6 %collective-permute-start.28 = (bf16[32,3072]{1,0:T(8,128)(2,1)S(1)}, bf16[32,3072]{1,0:T(8,128)(2,1)S(1)}, u32[]{:S(2)}, u32[]{:S(2)}) collective-permute-start(bf16[32,3072]{1,0:T(8,128)(2,1)S(1)} %add_convert_fusion.1), channel_id=1, source_target_pairs={{0,8},{4,12},{8,0},{12,4},{16,24},{20,28},{24,16},{28,20},{1,9},{5... | collective-permute-start | bytes 589832 | tf_op jit(solution)/shard_map/ppermute | solution.py:271
